TPU v7x, 32 devices: a whole 2x2x4 slice. The times are simulated.
32 devices in a mesh: seq: 2 (over x), shard: 16 (over z, y, core).
Axes of the slice: x: 2, y: 2, z: 4, core: 2. Of those that a mesh axis runs over, the one named last changes fastest.
Arguments:
- tokens: bfloat16 [16, 1024, 1024], P('shard', 'seq'), may hold values from -6 to 6
- doc_starts: int32 [16, 4], P('shard'), may hold values from 0 to 1023, as said below
- norm_gain: bfloat16 [1024], P('shard'), may hold values from 0.5 to 1.5
- query_weight: bfloat16 [1024, 1024], P('shard'), may hold values from -0.1875 to 0.1875
- key_weight: bfloat16 [1024, 1024], P('shard'), may hold values from -0.1875 to 0.1875
- value_weight: bfloat16 [1024, 2048], P('shard'), may hold values from -0.1875 to 0.1875
- gate_weight: bfloat16 [1024, 2048], P('shard'), may hold values from -0.1875 to 0.1875
- beta_decay_weight: bfloat16 [1024, 16], P('shard'), may hold values from -0.1875 to 0.1875
- conv_filters: float32 [4, 8, 512], P(None, 'seq'), may hold values from -2.5 to 2.5
- decay_params: float32 [8, 2], P('seq'), may hold values from -10 to 2.5
- out_norm_gain: bfloat16 [256], P('shard'), may hold values from 0.5 to 1.5
- out_weight: bfloat16 [2048, 1024], P('shard'), may hold values from -0.125 to 0.125
- ffn_norm_gain: bfloat16 [1024], P('shard'), may hold values from 0.5 to 1.5
- ffn_gate_weight: bfloat16 [1024, 2816], P('shard'), may hold values from -0.1875 to 0.1875
- ffn_up_weight: bfloat16 [1024, 2816], P('shard'), may hold values from -0.1875 to 0.1875
- down_weight: bfloat16 [2816, 1024], P('shard'), may hold values from -0.109375 to 0.109375
- out_cotangent: bfloat16 [16, 1024, 1024], P('shard', 'seq'), may hold values from -6 to 6
Outputs:
- block_out: bfloat16 [16, 1024, 1024], P('shard', 'seq')
- tokens_grad: float32 [16, 1024, 1024], P('shard', 'seq')
- norm_gain_grad: float32 [1024], P('shard')
- query_weight_grad: float32 [1024, 1024], P('shard')
- key_weight_grad: float32 [1024, 1024], P('shard')
- value_weight_grad: float32 [1024, 2048], P('shard')
- gate_weight_grad: float32 [1024, 2048], P('shard')
- beta_decay_weight_grad: float32 [1024, 16], P('shard')
- conv_filters_grad: float32 [4, 8, 512], P(None, 'seq')
- decay_params_grad: float32 [8, 2], P('seq')
- out_norm_gain_grad: float32 [256], P('shard')
- out_weight_grad: float32 [2048, 1024], P('shard')
- ffn_norm_gain_grad: float32 [1024], P('shard')
- ffn_gate_weight_grad: float32 [1024, 2816], P('shard')
- ffn_up_weight_grad: float32 [1024, 2816], P('shard')
- down_weight_grad: float32 [2816, 1024], P('shard')
Inputs may be any that keep to these rules, and one draw needn't show every extreme that they name: `doc_starts`: each row holds 4 document start positions in strictly increasing order, the first of which is 0.
All inputs are finite; a program needn't handle non-finite values.
Results may differ from a plain program's by a relative error of at most 0.022.
Values may be sent and summed in bfloat16 or wider, within the bound.
No kernel may reach another device: no remote copies, remote signals or barrier semaphores. Data moves between devices by JAX's collectives and lax.ppermute only.
A program may use at most 320 MiB of HBM per device.

v0:
```python
import functools

import jax
import jax.numpy as jnp
from jax import lax
from jax.experimental import pallas as pl
from jax.experimental.pallas import tpu as pltpu
from jax.sharding import PartitionSpec as P

HEADS = 8
KEY = 128
VALUE = 256
CONV = 4
GROUP = 64
HALO = 16
SUB = 4
epsilon = 1e-06
f32 = jnp.float32
bf16 = jnp.bfloat16


def dot(a, b, ca=1, cb=0):
    return lax.dot_general(a, b, (((ca,), (cb,)), ((), ())), preferred_element_type=f32)


def halves(values):
    high = values.astype(bf16)
    return high, (values - high.astype(f32)).astype(bf16)


def fine_dot(a, b, ca=1, cb=0):
    if not isinstance(a, tuple):
        return dot(a, b[0], ca, cb) + dot(a, b[1], ca, cb)
    if not isinstance(b, tuple):
        return dot(a[0], b, ca, cb) + dot(a[1], b, ca, cb)
    return dot(a[0], b[0], ca, cb) + (dot(a[0], b[1], ca, cb) + dot(a[1], b[0], ca, cb))


def iota(shape, dim):
    return lax.broadcasted_iota(jnp.int32, shape, dim)


def doc_count(starts_ref, times):
    count = jnp.zeros(times.shape, jnp.int32)
    for s in range(starts_ref.shape[1]):
        count = count + jnp.where(times >= starts_ref[0, s], 1, 0)
    return count


def scalar_doc(starts_ref, time):
    count = 0
    for s in range(starts_ref.shape[1]):
        count = count + (time >= starts_ref[0, s]).astype(jnp.int32)
    return count


def per_head(cols, heads, width):
    rows = cols.shape[0]
    lane = iota((rows, heads * width), 1)
    out = jnp.broadcast_to(cols[:, heads - 1 : heads], (rows, heads * width))
    for h in range(heads - 2, -1, -1):
        out = jnp.where(lane < (h + 1) * width, cols[:, h : h + 1], out)
    return out


def head_sums(panel, heads, width):
    lane = iota(panel.shape, 1)
    sums = []
    for h in range(heads):
        inside = (lane >= h * width) & (lane < (h + 1) * width)
        sums.append(jnp.sum(jnp.where(inside, panel, 0.0), axis=1, keepdims=True))
    return columns(sums)


def across(mask, width):
    return jnp.concatenate([mask] * (width // KEY), axis=1)


def columns(parts):
    rows = parts[0].shape[0]
    lane = iota((rows, len(parts)), 1)
    out = jnp.broadcast_to(parts[-1], (rows, len(parts)))
    for h in range(len(parts) - 2, -1, -1):
        out = jnp.where(lane == h, parts[h], out)
    return out


def block_diagonal(panel, heads):
    if heads == 1:
        return panel
    lane = iota(panel.shape, 1)
    zero = jnp.zeros_like(panel)
    parts = []
    for h in range(heads):
        inside = (lane >= h * GROUP) & (lane < (h + 1) * GROUP)
        parts.append(jnp.where(inside, panel, zero))
    return jnp.concatenate(parts, axis=0)


def diagonal_panel(full, heads):
    if heads == 1:
        return full
    lane = iota((GROUP, heads * GROUP), 1)
    out = full[(heads - 1) * GROUP :]
    for h in range(heads - 2, -1, -1):
        out = jnp.where(lane < (h + 1) * GROUP, full[h * GROUP : (h + 1) * GROUP], out)
    return out


def key_diagonal(keys):
    heads = len(keys)
    if heads == 1:
        return keys[0]
    zero = jnp.zeros_like(keys[0])
    rows = []
    for h in range(heads):
        rows.append(jnp.concatenate([keys[h] if o == h else zero for o in range(heads)], axis=1))
    return jnp.concatenate(rows, axis=0)


def scan_rows(values, reverse=False):
    rows = values.shape[0]
    index = iota(values.shape, 0)
    step = 1
    while step < rows:
        if reverse:
            moved = pltpu.roll(values, rows - step, 0)
            values = values + jnp.where(index < rows - step, moved, 0.0)
        else:
            moved = pltpu.roll(values, step, 0)
            values = values + jnp.where(index >= step, moved, 0.0)
        step *= 2
    return values


def sigmoid(v):
    return 1.0 / (1.0 + jnp.exp(-v))


def softplus(v):
    return jnp.maximum(v, 0.0) + jnp.log(1.0 + jnp.exp(-jnp.abs(v)))


def in_turn(generators):
    generators = list(generators)
    while generators:
        still = []
        for generator in generators:
            if next(generator, True) is None:
                still.append(generator)
        generators = still


class Block:
    def __init__(self, heads, base, raw_ref, value_ref, filters_ref, decay_ref, starts_ref):
        self.heads = heads
        self.base = base
        self.raw_ref = raw_ref
        self.value_ref = value_ref
        self.filters_ref = filters_ref
        self.decay_ref = decay_ref
        self.starts_ref = starts_ref

    def build(self):
        heads, base, starts_ref = self.heads, self.base, self.starts_ref
        raw_ref, decay_ref = self.raw_ref, self.decay_ref
        width = 2 * heads * KEY
        times = base + iota((GROUP, 1), 0)
        docs = doc_count(starts_ref, times)
        wide = (GROUP, KEY)
        self.masks, self.next_masks = [], []
        for o in range(1, CONV):
            same = (docs == doc_count(starts_ref, times - o)).astype(f32)
            self.masks.append(jnp.broadcast_to(same, wide))
            same = (docs == doc_count(starts_ref, times + o)).astype(f32)
            self.next_masks.append(jnp.broadcast_to(same, wide))
        self.query, self.keys, self.query_pre, self.key_pre = [], [], [], []
        self.query_conv, self.key_conv, self.query_scale, self.key_scale = [], [], [], []
        for h in range(heads):
            pre = self.convolve(h * KEY, KEY)
            conv = pre * sigmoid(pre)
            scale = lax.rsqrt(jnp.sum(conv * conv, axis=1, keepdims=True) + epsilon)
            self.query_pre.append(pre)
            self.query_conv.append(conv)
            self.query_scale.append(scale)
            self.query.append(conv * scale * KEY ** (-0.5))
        for h in range(heads):
            pre = self.convolve((heads + h) * KEY, KEY)
            conv = pre * sigmoid(pre)
            scale = lax.rsqrt(jnp.sum(conv * conv, axis=1, keepdims=True) + epsilon)
            self.key_pre.append(pre)
            self.key_conv.append(conv)
            self.key_scale.append(scale)
            self.keys.append(conv * scale)
        yield
        logits = raw_ref[pl.ds(base, GROUP), width : width + KEY].astype(f32)
        self.strength = sigmoid(logits[:, :heads])
        self.decay_logit = logits[:, heads : 2 * heads] + decay_ref[1:2, :heads]
        self.decay_rate = -jnp.exp(decay_ref[0:1, :heads])
        self.log_decay = self.decay_rate * softplus(self.decay_logit)
        yield
        sums = scan_rows(self.log_decay)
        yield
        self.sums = sums
        last = sums[GROUP - 1 : GROUP]
        before = scalar_doc(starts_ref, base - 1)
        final = scalar_doc(starts_ref, base + GROUP - 1)
        self.entering = jnp.where(docs == before, jnp.exp(sums), 0.0)
        same_last = docs == final
        self.leaving = jnp.where(same_last, jnp.exp(jnp.where(same_last, last - sums, 0.0)), 0.0)
        self.retain = self.entering[GROUP - 1 : GROUP]
        yield
        shape = (GROUP, heads * GROUP)
        row = iota(shape, 0)
        place = jnp.bitwise_and(iota(shape, 1), GROUP - 1)
        self.row, self.place = row, place
        across = jnp.bitwise_and(iota((1, heads * GROUP), 1), GROUP - 1)
        docs_across = doc_count(starts_ref, base + across)
        same = docs == docs_across
        self.inclusive = same & (row >= place)
        self.strict = same & (row > place)
        sums_down = per_head(sums, heads, GROUP)
        sums_across = jnp.sum(jnp.where(row == place, sums_down, 0.0), axis=0, keepdims=True)
        gap = jnp.where(self.inclusive, sums_down - sums_across, 0.0)
        self.fade = jnp.where(self.inclusive, jnp.exp(gap), 0.0)
        yield
        self.strength_down = per_head(self.strength, heads, GROUP)
        low_keys = [k.astype(bf16) for k in self.keys]
        low_query = [q.astype(bf16) for q in self.query]
        self.keys = [k.astype(f32) for k in low_keys]
        self.query = [q.astype(f32) for q in low_query]
        self.low_keys, self.low_query = low_keys, low_query
        self.key_diag = key_diagonal(low_keys)
        left = jnp.concatenate(
            [jnp.concatenate(low_keys, axis=1), jnp.concatenate(low_query, axis=1)], axis=0
        )
        self.query_key_rows = left
        grams = dot(left, self.key_diag, 1, 1)
        yield
        self.key_gram = grams[:GROUP]
        self.score_gram = grams[GROUP:]
        self.system = jnp.where(self.strict, self.strength_down * self.key_gram * self.fade, 0.0)
        self.scores = self.score_gram * self.fade

    def taps(self, start, width):
        source = self.raw_ref
        if start >= 2 * self.heads * KEY:
            source = self.value_ref
            start = start - 2 * self.heads * KEY
        current = source[pl.ds(self.base, GROUP), start : start + width].astype(f32)
        earlier = pl.multiple_of(jnp.maximum(self.base - HALO, 0), HALO)
        halo = source[pl.ds(earlier, HALO), start : start + width].astype(f32)
        extended = jnp.concatenate([halo, current], axis=0)
        return [current] + [
            pltpu.roll(extended, o, 0)[HALO:] * across(self.masks[o - 1], width)
            for o in range(1, CONV)
        ]

    def convolve(self, start, width):
        taps = self.taps(start, width)
        filters = self.filters_ref[:, start : start + width]
        total = taps[0] * filters[CONV - 1 : CONV]
        for o in range(1, CONV):
            total = total + taps[o] * filters[CONV - 1 - o : CONV - o]
        return total


def inverse(systems, heads, row, place):
    eye = (row == place).astype(f32)
    apart = jnp.bitwise_xor(row, place)

    def part(system, size):
        return jnp.where((apart >= size) & (apart < 2 * size), system, 0.0)

    results = [eye - part(system, 1) for system in systems]
    size = 2
    while size < GROUP:
        low = [result.astype(bf16) for result in results]
        inner = [
            dot(part(system, size).astype(bf16), block_diagonal(one, heads))
            for system, one in zip(systems, low)
        ]
        inner = [block_diagonal(one.astype(bf16), heads) for one in inner]
        results = [
            result - dot(one, right) for result, one, right in zip(results, low, inner)
        ]
        size *= 2
    return results


def forward_kernel(
    heads, starts_ref, raw_ref, value_ref, filters_ref, decay_ref, gate_ref, gain_ref,
    gated_ref, mixed_ref, inverse_ref, delta_ref, rest_ref, memory_ref, state,
):
    step = pl.program_id(0)

    @pl.when(step == 0)
    def _():
        state[...] = jnp.zeros_like(state)

    blocks = []
    for s in range(SUB):
        base = pl.multiple_of((step * SUB + s) * GROUP, GROUP)
        blocks.append(Block(heads, base, raw_ref, value_ref, filters_ref, decay_ref, starts_ref))
    in_turn(block.build() for block in blocks)
    solves = inverse([block.system for block in blocks], heads, blocks[0].row, blocks[0].place)
    for s, block in enumerate(blocks):
        block.values = []
        for h in range(heads):
            pre = block.convolve(2 * heads * KEY + h * VALUE, VALUE)
            block.values.append(pre * sigmoid(pre))
        block.solve = solves[s]
        inverse_ref[s * GROUP : (s + 1) * GROUP] = block.solve.astype(bf16)
    for s, block in enumerate(blocks):
        from_state, rest, right = [], [], []
        for h in range(heads):
            entering = block.entering[:, h : h + 1]
            memory = state[h * KEY : (h + 1) * KEY].astype(bf16)
            memory_ref[(s * heads + h) * KEY : (s * heads + h + 1) * KEY] = memory
            both = jnp.concatenate([block.low_keys[h], block.low_query[h]], axis=0)
            read = dot(both, memory)
            from_state.append(entering * read[GROUP:])
            missing = block.values[h] - entering * read[:GROUP]
            rest.append(missing.astype(bf16))
            right.append(block.strength[:, h : h + 1] * missing)
        rest_ref[s * heads * GROUP : (s + 1) * heads * GROUP] = jnp.concatenate(rest, axis=0)
        solve = tuple(block_diagonal(p, heads) for p in halves(block.solve))
        delta = fine_dot(solve, halves(jnp.concatenate(right, axis=0)))
        delta_ref[s * heads * GROUP : (s + 1) * heads * GROUP] = delta
        scores = tuple(block_diagonal(p, heads) for p in halves(block.scores))
        outputs = fine_dot(scores, halves(delta))
        for h in range(heads):
            rows = slice(h * GROUP, (h + 1) * GROUP)
            out = from_state[h] + outputs[rows]
            here = slice(s * GROUP, (s + 1) * GROUP)
            lanes = slice(h * VALUE, (h + 1) * VALUE)
            low = out.astype(bf16)
            mixed_ref[here, lanes] = low
            low = low.astype(f32)
            gate = gate_ref[here, lanes]
            scale = lax.rsqrt(jnp.mean(low * low, axis=1, keepdims=True) + epsilon)
            gated = low * scale * gain_ref[0:1] * (gate * sigmoid(gate))
            gated_ref[here, lanes] = gated.astype(bf16)
            leaving = halves(block.leaving[:, h : h + 1] * delta[rows])
            keep = block.retain[:, h : h + 1]
            own = slice(h * KEY, (h + 1) * KEY)
            state[own] = keep * state[own] + fine_dot(block.low_keys[h], leaving, 0, 0)


def silu_slope(pre):
    gate = sigmoid(pre)
    return gate * (1.0 + pre * (1.0 - gate))


def backward_kernel(
    heads, starts_ref, raw_ref, value_ref, filters_ref, decay_ref, gate_ref, gain_ref,
    gated_grad_ref, mixed_ref, inverse_ref, delta_ref, rest_ref, memory_ref,
    raw_grad_ref, filters_grad_ref, decay_grad_ref, gain_grad_ref,
    state, halo,
):
    step = pl.program_id(0)
    steps = pl.num_programs(0)
    width = 2 * heads * KEY

    @pl.when(step == 0)
    def _():
        state[...] = jnp.zeros_like(state)
        gain_grad_ref[...] = jnp.zeros_like(gain_grad_ref)
        halo[...] = jnp.zeros_like(halo)
        filters_grad_ref[...] = jnp.zeros_like(filters_grad_ref)
        decay_grad_ref[...] = jnp.zeros_like(decay_grad_ref)

    def pull(s):
        base = pl.multiple_of(((steps - 1 - step) * SUB + s) * GROUP, GROUP)
        block = Block(heads, base, raw_ref, value_ref, filters_ref, decay_ref, starts_ref)
        yield from block.build()
        yield
        here = slice(s * GROUP, (s + 1) * GROUP)
        stacked = slice(s * heads * GROUP, (s + 1) * heads * GROUP)
        solve = inverse_ref[here]
        delta = delta_ref[stacked]
        rest = rest_ref[stacked]
        mixed_grads = []
        for h in range(heads):
            lanes = slice(h * VALUE, (h + 1) * VALUE)
            grad = gated_grad_ref[here, lanes].astype(f32)
            mixed = mixed_ref[here, lanes].astype(f32)
            gate = gate_ref[here, lanes]
            scale = lax.rsqrt(jnp.mean(mixed * mixed, axis=1, keepdims=True) + epsilon)
            unit = mixed * scale
            open_gate = sigmoid(gate)
            swish = gate * open_gate
            along = grad * unit
            product = (along * swish).reshape(GROUP // 8, 8, VALUE)
            gain_grad_ref[...] = gain_grad_ref[...] + jnp.sum(product, axis=0)
            gate_grad = along * gain_ref[0:1] * (open_gate * (1.0 + gate * (1.0 - open_gate)))
            behind = width + KEY + (heads + h) * VALUE
            raw_grad_ref[here, behind : behind + VALUE] = gate_grad.astype(bf16)
            unit_grad = grad * swish * gain_ref[0:1]
            inner = jnp.mean(unit_grad * unit, axis=1, keepdims=True)
            mixed_grads.append((scale * (unit_grad - unit * inner)).astype(bf16))
        out_grad = jnp.concatenate(mixed_grads, axis=0)
        yield
        scores = tuple(block_diagonal(p, heads) for p in halves(block.scores))
        from_scores = fine_dot(scores, out_grad, 0, 0)
        delta = halves(delta)
        score_part = diagonal_panel(sum(dot(out_grad, d, 1, 1) for d in delta), heads)
        scores_grad = jnp.where(block.inclusive, score_part, 0.0)
        score_gram_grad = scores_grad * block.fade
        solve = block_diagonal(solve, heads)
        yield "chain"
        later = [state[h * KEY : (h + 1) * KEY] for h in range(heads)]
        later_low = [m.astype(bf16) for m in later]
        pulled = jnp.concatenate(
            [
                block.leaving[:, h : h + 1] * dot(block.low_keys[h], later_low[h])
                for h in range(heads)
            ],
            axis=0,
        )
        delta_grad = pulled + from_scores
        right_grad = dot(solve, delta_grad.astype(bf16), 0, 0)
        rest_grad, pairs = [], []
        for h in range(heads):
            rows = slice(h * GROUP, (h + 1) * GROUP)
            rest_grad.append(block.strength[:, h : h + 1] * right_grad[rows])
            pairs.append(jnp.concatenate([out_grad[rows], rest_grad[h].astype(bf16)], axis=0))
            entering = block.entering[:, h : h + 1]
            left = jnp.concatenate(
                [entering * block.query[h], -entering * block.keys[h]], axis=0
            ).astype(bf16)
            state[h * KEY : (h + 1) * KEY] = (
                block.retain[:, h : h + 1] * later[h] + dot(left, pairs[h], 0, 0)
            )
        yield "chain"
        entering_query_grad, entering_key_grad, leaving_key_grad, retain_grad = [], [], [], []
        strength_grad = []
        for h in range(heads):
            rows = slice(h * GROUP, (h + 1) * GROUP)
            strength_grad.append(
                jnp.sum(right_grad[rows] * rest[rows].astype(f32), axis=1, keepdims=True)
            )
            memory = memory_ref[(s * heads + h) * KEY : (s * heads + h + 1) * KEY]
            back = dot(pairs[h], memory, 1, 1)
            entering_query_grad.append(back[:GROUP])
            entering_key_grad.append(-back[GROUP:])
            leaving_key_grad.append(sum(dot(d[rows], later_low[h], 1, 1) for d in delta))
            product = later[h] * memory.astype(f32)
            retain_grad.append(
                jnp.sum(jnp.sum(product, axis=0, keepdims=True), axis=1, keepdims=True)
            )
        yield
        right_low = right_grad.astype(bf16)
        system_part = diagonal_panel(sum(dot(right_low, d, 1, 1) for d in delta), heads)
        system_grad = jnp.where(block.strict, -system_part, 0.0)
        faded = system_grad * block.fade
        key_gram_grad = block.strength_down * faded
        gap_grad = score_gram_grad * block.score_gram + key_gram_grad * block.key_gram
        yield
        strength_panel = head_sums(faded * block.key_gram, heads, GROUP)
        down = jnp.sum(gap_grad, axis=0, keepdims=True)
        gap_rows = head_sums(
            gap_grad - jnp.where(block.row == block.place, down, 0.0), heads, GROUP
        )
        yield
        both_low = jnp.concatenate([key_gram_grad, score_gram_grad], axis=0).astype(bf16)
        straight = dot(both_low, block.key_diag)
        turned = dot(both_low, block.query_key_rows, 0, 0)
        yield
        entering_grad, leaving_grad = [], []
        for h in range(heads):
            lanes = slice(h * KEY, (h + 1) * KEY)
            entering = block.entering[:, h : h + 1]
            fading = block.leaving[:, h : h + 1]
            query_grad = entering * entering_query_grad[h] + straight[GROUP:, lanes]
            key_grad = (
                turned[h * GROUP : (h + 1) * GROUP, lanes]
                + straight[:GROUP, lanes]
                + fading * leaving_key_grad[h]
                + entering * entering_key_grad[h]
            )
            entering_grad.append(
                jnp.sum(
                    entering_query_grad[h] * block.query[h] + entering_key_grad[h] * block.keys[h],
                    axis=1,
                    keepdims=True,
                )
            )
            leaving_grad.append(
                jnp.sum(leaving_key_grad[h] * block.keys[h], axis=1, keepdims=True)
            )
            for start, grad, conv, scale, pre, factor in (
                (h * KEY, query_grad, block.query_conv[h], block.query_scale[h],
                 block.query_pre[h], KEY ** (-0.5)),
                ((heads + h) * KEY, key_grad, block.key_conv[h], block.key_scale[h],
                 block.key_pre[h], 1.0),
            ):
                along = jnp.sum(grad * conv, axis=1, keepdims=True)
                conv_grad = (factor * scale) * (grad - conv * (scale * scale * along))
                convolve_back(
                    block, s, start, start, KEY, conv_grad * silu_slope(pre), starts_ref,
                    raw_grad_ref, filters_grad_ref, halo,
                )
            yield
            start = 2 * heads * KEY + h * VALUE
            pre = block.convolve(start, VALUE)
            convolve_back(
                block, s, start, start + KEY, VALUE, rest_grad[h] * silu_slope(pre), starts_ref,
                raw_grad_ref, filters_grad_ref, halo,
            )
        yield
        entering_grad = columns(entering_grad) * block.entering
        leaving_grad = columns(leaving_grad) * block.leaving
        strength_grad = columns(strength_grad) + strength_panel
        retain_grad = columns(retain_grad) * block.retain
        at_last = jnp.sum(leaving_grad, axis=0, keepdims=True) + retain_grad
        index = iota((GROUP, heads), 0)
        sums_grad = (
            entering_grad - leaving_grad + gap_rows + jnp.where(index == GROUP - 1, at_last, 0.0)
        )
        log_decay_grad = scan_rows(sums_grad, reverse=True)
        yield
        logit_grad = log_decay_grad * block.decay_rate * sigmoid(block.decay_logit)
        beta_grad = strength_grad * block.strength * (1.0 - block.strength)
        lane = iota((GROUP, KEY), 1)
        packed = jnp.zeros((GROUP, KEY), f32)
        for h in range(heads):
            packed = jnp.where(lane == h, beta_grad[:, h : h + 1], packed)
            packed = jnp.where(lane == heads + h, logit_grad[:, h : h + 1], packed)
        raw_grad_ref[here, width : width + KEY] = packed.astype(bf16)
        scale_sum = jnp.sum(log_decay_grad * block.log_decay, axis=0, keepdims=True)
        bias_sum = jnp.sum(logit_grad, axis=0, keepdims=True)
        decay_grad_ref[0:1] = decay_grad_ref[0:1] + scale_sum
        decay_grad_ref[1:2] = decay_grad_ref[1:2] + bias_sum

    pulls = [pull(s) for s in range(SUB - 1, -1, -1)]
    waiting = list(pulls)
    while waiting:
        waiting = [p for p in waiting if next(p) is None]
    for p in pulls:
        next(p)
    in_turn(pulls)


def convolve_back(
    block, s, start, place, width, pre_grad, starts_ref, grad_ref, filters_grad_ref, halo
):
    lanes = slice(start, start + width)
    taps = block.taps(start, width)
    for o in range(CONV):
        j = CONV - 1 - o
        product = (pre_grad * taps[o]).reshape(GROUP // 8, 8, width)
        filters_grad_ref[j * 8 : (j + 1) * 8, lanes] = filters_grad_ref[
            j * 8 : (j + 1) * 8, lanes
        ] + jnp.sum(product, axis=0)
    filters = block.filters_ref[:, lanes]
    extended = jnp.concatenate([pre_grad, halo[:, lanes]], axis=0)
    rows = GROUP + 8
    total = pre_grad * filters[CONV - 1 : CONV]
    for o in range(1, CONV):
        moved = pltpu.roll(extended, rows - o, 0)[:GROUP] * across(block.next_masks[o - 1], width)
        total = total + moved * filters[CONV - 1 - o : CONV - o]
    grad_ref[s * GROUP : (s + 1) * GROUP, place : place + width] = total.astype(bf16)
    halo[:, lanes] = pre_grad[:8]


SPACE = 56 * 2**20


def mixer_forward(raw, values, filters, decays, starts, gates, gain, heads):
    length, wide = raw.shape
    steps = length // (SUB * GROUP)
    rows = SUB * GROUP
    blocks = length // GROUP
    whole = lambda a: pl.BlockSpec(a.shape, lambda i: (0, 0))
    part = lambda r, c: pl.BlockSpec((r, c), lambda i: (i, 0))
    return pl.pallas_call(
        functools.partial(forward_kernel, heads),
        grid=(steps,),
        in_specs=[
            pl.BlockSpec(memory_space=pltpu.SMEM),
            whole(raw),
            whole(values),
            whole(filters),
            whole(decays),
            part(rows, heads * VALUE),
            whole(gain),
        ],
        out_specs=[
            part(rows, heads * VALUE),
            part(rows, heads * VALUE),
            part(rows, heads * GROUP),
            part(rows * heads, VALUE),
            part(rows * heads, VALUE),
            part(SUB * heads * KEY, VALUE),
        ],
        out_shape=[
            jax.ShapeDtypeStruct((length, heads * VALUE), bf16),
            jax.ShapeDtypeStruct((length, heads * VALUE), bf16),
            jax.ShapeDtypeStruct((length, heads * GROUP), bf16),
            jax.ShapeDtypeStruct((length * heads, VALUE), f32),
            jax.ShapeDtypeStruct((length * heads, VALUE), bf16),
            jax.ShapeDtypeStruct((blocks * heads * KEY, VALUE), bf16),
        ],
        scratch_shapes=[pltpu.VMEM((heads * KEY, VALUE), f32)],
        compiler_params=pltpu.CompilerParams(vmem_limit_bytes=SPACE),
        cost_estimate=pl.CostEstimate(
            flops=length * heads * 11_000_000, bytes_accessed=2**24, transcendentals=0
        ),
        name="mixer_forward",
    )(starts, raw, values, filters, decays, gates, gain)


def mixer_backward(raw, values, filters, decays, starts, gates, gain, gated_grad, kept, heads):
    length, wide = raw.shape
    steps = length // (SUB * GROUP)
    rows = SUB * GROUP
    whole = lambda a: pl.BlockSpec(a.shape, lambda i: (0, 0))
    same = lambda r, c: pl.BlockSpec((r, c), lambda i: (0, 0))
    part = lambda r, c: pl.BlockSpec((r, c), lambda i: (steps - 1 - i, 0))
    return pl.pallas_call(
        functools.partial(backward_kernel, heads),
        grid=(steps,),
        in_specs=[
            pl.BlockSpec(memory_space=pltpu.SMEM),
            whole(raw),
            whole(values),
            whole(filters),
            whole(decays),
            part(rows, heads * VALUE),
            whole(gain),
            part(rows, heads * VALUE),
            part(rows, heads * VALUE),
            part(rows, heads * GROUP),
            part(rows * heads, VALUE),
            part(rows * heads, VALUE),
            part(SUB * heads * KEY, VALUE),
        ],
        out_specs=[
            part(rows, wide + 2 * heads * VALUE),
            same(8 * CONV, filters.shape[1]),
            same(2, heads),
            same(8, VALUE),
        ],
        out_shape=[
            jax.ShapeDtypeStruct((length, wide + 2 * heads * VALUE), bf16),
            jax.ShapeDtypeStruct((8 * CONV, filters.shape[1]), f32),
            jax.ShapeDtypeStruct((2, heads), f32),
            jax.ShapeDtypeStruct((8, VALUE), f32),
        ],
        scratch_shapes=[
            pltpu.VMEM((heads * KEY, VALUE), f32),
            pltpu.VMEM((8, filters.shape[1]), f32),
        ],
        compiler_params=pltpu.CompilerParams(vmem_limit_bytes=SPACE),
        cost_estimate=pl.CostEstimate(
            flops=length * heads * 14_000_000, bytes_accessed=2**24, transcendentals=0
        ),
        name="mixer_backward",
    )(starts, raw, values, filters, decays, gates, gain, gated_grad, *kept)


def forward_dot(left_side, right_side):
    return jnp.dot(left_side, right_side, preferred_element_type=f32)


def times_transposed(left_side, right_side):
    return dot(left_side, right_side, 1, 1)


def transposed_times(left_side, right_side):
    return dot(left_side, right_side, 0, 0)


def rms_norm(values, gain):
    return values * lax.rsqrt(jnp.mean(values * values, axis=-1, keepdims=True) + epsilon) * gain


def swiglu(gate_rows, up_rows):
    return jax.nn.silu(gate_rows) * up_rows


def swap_seq(values):
    return lax.ppermute(values, "seq", [(0, 1), (1, 0)])


def in_order(own, other, axis):
    first = lax.axis_index("seq") == 0
    return jnp.where(
        first,
        jnp.concatenate([own, other], axis=axis),
        jnp.concatenate([other, own], axis=axis),
    )


def gather_seq(values, axis):
    if lax.axis_size("seq") == 2:
        return in_order(values, swap_seq(values), axis)
    return lax.all_gather(values, "seq", axis=axis, tiled=True)


def own_part(values, axis, index=None):
    size = values.shape[axis] // lax.axis_size("seq")
    index = lax.axis_index("seq") if index is None else index
    return lax.dynamic_slice_in_dim(values, index * size, size, axis=axis)


def sum_scatter_seq(values, axis):
    if lax.axis_size("seq") == 2:
        other = own_part(values, axis, 1 - lax.axis_index("seq")).astype(bf16)
        return own_part(values, axis) + swap_seq(other).astype(f32)
    return lax.psum_scatter(
        values.astype(bf16), "seq", scatter_dimension=axis, tiled=True
    ).astype(f32)


def own_first(values):
    if lax.axis_size("seq") == 2:
        return jnp.concatenate([values, swap_seq(values)], axis=0)
    return lax.all_gather(values, "seq", axis=0, tiled=True)


def sum_own_first(values):
    if lax.axis_size("seq") == 2:
        half = values.shape[0] // 2
        return values[:half] + swap_seq(values[half:].astype(bf16)).astype(f32)
    return sum_scatter_seq(values, 0)


def exchange_seq(values, split, join):
    if lax.axis_size("seq") == 2:
        other = own_part(values, split, 1 - lax.axis_index("seq"))
        return in_order(own_part(values, split), swap_seq(other), join)
    return lax.all_to_all(values, "seq", split_axis=split, concat_axis=join, tiled=True)


PLACES = 4


def in_grid():
    return lax.axis_size("shard") == 4 * PLACES and lax.axis_size("seq") == 2


def position():
    place = lax.axis_index("shard")
    return place // 4, (place // 2) % 2, place % 2


def flip(values, mask):
    size = lax.axis_size("shard")
    return lax.ppermute(values, "shard", [(i, i ^ mask) for i in range(size)])


def from_place(values, step):
    size = lax.axis_size("shard")
    return lax.ppermute(values, "shard", [(i, (i - 4 * step) % size) for i in range(size)])


def gather_shard(values):
    return lax.all_gather(values, "shard", axis=0, tiled=True)


def scatter_shard(values):
    return lax.psum_scatter(values, "shard", scatter_dimension=0, tiled=True)


def core_major(values):
    if not in_grid():
        return values
    rows, columns = values.shape
    places = values.reshape(rows, PLACES, 2, 2, columns // (4 * PLACES))
    return jnp.transpose(places, (0, 3, 2, 1, 4)).reshape(rows, columns)


def portion(values, index, count):
    size = values.shape[0] // count
    return lax.dynamic_slice_in_dim(values, index * size, size, axis=0)


def sum_pair(values, index, mask):
    sent = flip(portion(values, 1 - index, 2), mask)
    return (portion(values, index, 2).astype(f32) + sent.astype(f32)).astype(bf16)


def sum_along(values):
    z = position()[0]
    total = portion(values, z, PLACES).astype(f32)
    for r in range(1, PLACES):
        sent = from_place(portion(values, (z - r) % PLACES, PLACES), r)
        total = total + sent.astype(f32)
    return total.astype(bf16)


def first_sum(values):
    return sum_pair(values, position()[2], 1) if in_grid() else values


def second_sum(values):
    return sum_pair(values, position()[1], 2) if in_grid() else values


def third_sum(values):
    return sum_along(values) if in_grid() else scatter_shard(values)


def after(values, *earlier):
    return lax.optimization_barrier((values, earlier))[0]


def sum_small(values, axes):
    if not in_grid():
        return lax.psum(values, axes)
    for mask in (1, 2, 4, 8):
        values = values + flip(values, mask)
    return values


def on_device(
    tokens,
    doc_starts,
    norm_gain,
    query_weight,
    key_weight,
    value_weight,
    gate_weight,
    beta_decay_weight,
    conv_filters,
    decay_params,
    out_norm_gain,
    out_weight,
    ffn_norm_gain,
    ffn_gate_weight,
    ffn_up_weight,
    down_weight,
    out_cotangent,
):
    heads = HEADS // lax.axis_size("seq")
    shards = lax.axis_size("shard")
    rows = query_weight.shape[0]
    width = 2 * heads * KEY
    ff = ffn_gate_weight.shape[1]

    logit_weight = own_part(beta_decay_weight.reshape(rows, HEADS, 2), 1)
    gain_rows = out_norm_gain.shape[0]
    raw_piece = jnp.concatenate(
        [
            own_part(query_weight, 1),
            own_part(key_weight, 1),
            logit_weight[:, :, 0],
            logit_weight[:, :, 1],
            norm_gain[:, None],
            ffn_norm_gain[:, None],
            jnp.pad(out_norm_gain, (0, rows - gain_rows))[:, None],
            jnp.zeros((rows, KEY - 2 * heads - 3), bf16),
        ],
        axis=1,
    )
    units = ff // shards // lax.axis_size("seq")

    def own_units(weight):
        return own_part(weight.reshape(rows, shards, ff // shards), 2).reshape(rows, shards * units)

    raw_wide = raw_piece.shape[1]
    value_end = raw_wide + heads * VALUE
    mixer_full = gather_shard(
        jnp.concatenate([raw_piece, own_part(value_weight, 1), own_part(gate_weight, 1)], axis=1)
    )
    raw_full = mixer_full[:, :raw_wide]
    value_full = mixer_full[:, raw_wide:value_end]
    gate_full = mixer_full[:, value_end:]
    half = shards * units
    model = out_weight.shape[1]
    out_rows = out_weight.shape[0]
    tall_full = gather_shard(jnp.concatenate([out_weight, own_part(down_weight, 0)], axis=0))
    tall_full = tall_full.reshape(shards, out_rows + units, model)
    out_full = tall_full[:, :out_rows].reshape(shards * out_rows, model)
    down_full = tall_full[:, out_rows:].reshape(half, model)
    ffn_full = gather_shard(
        jnp.concatenate([own_units(ffn_gate_weight), own_units(ffn_up_weight)], axis=1)
    )
    first_gain = raw_full[:, width + 2 * heads].astype(f32)
    second_gain = raw_full[:, width + 2 * heads + 1].astype(f32)
    third_gain = (
        raw_full[:, width + 2 * heads + 2]
        .reshape(shards, rows)[:, :gain_rows]
        .reshape(1, shards * gain_rows)
        .astype(f32)
    )

    own_tokens = tokens[0]
    token_count = own_tokens.shape[0]
    inputs = own_tokens.astype(f32)
    cotangent = out_cotangent[0]
    if lax.axis_size("seq") == 2:
        other = swap_seq(jnp.concatenate([own_tokens, cotangent], axis=0))
        all_inputs = in_order(own_tokens, other[:token_count], 0).astype(f32)
        all_cotangent = jnp.concatenate([cotangent, other[token_count:]], axis=0)
    else:
        all_inputs = gather_seq(own_tokens, 0).astype(f32)
        all_cotangent = own_first(cotangent)
    length = all_inputs.shape[0]
    all_scaled = all_inputs * lax.rsqrt(
        jnp.mean(all_inputs * all_inputs, axis=-1, keepdims=True) + epsilon
    )
    normed = (all_scaled * first_gain).astype(bf16)
    raw = forward_dot(normed, raw_full).astype(bf16)
    values = forward_dot(normed, value_full).astype(bf16)
    gate_rows = forward_dot(normed, gate_full)
    filters = jnp.concatenate(
        [
            conv_filters[:, :, :KEY].reshape(CONV, heads * KEY),
            conv_filters[:, :, KEY : 2 * KEY].reshape(CONV, heads * KEY),
            conv_filters[:, :, 2 * KEY :].reshape(CONV, heads * VALUE),
        ],
        axis=1,
    )
    decays = decay_params.T
    gated, *kept = mixer_forward(
        raw, values, filters, decays, doc_starts, gate_rows, third_gain, heads
    )
    gated_low = exchange_seq(gated, 0, 1)
    gated_low, down_full = lax.optimization_barrier((gated_low, down_full))
    middle = inputs + forward_dot(gated_low, out_full)
    second_norm, second_pull = jax.vjp(rms_norm, middle, second_gain)
    hidden = own_first(second_norm.astype(bf16))
    both_ffn = forward_dot(hidden, ffn_full)
    activated, swiglu_pull = jax.vjp(swiglu, both_ffn[:, :half], both_ffn[:, half:])
    activated_low = activated.astype(bf16)
    act_grad = times_transposed(all_cotangent, down_full)
    both_grad = jnp.concatenate([g.astype(bf16) for g in swiglu_pull(act_grad)], axis=1)
    hidden_grad = sum_own_first(times_transposed(both_grad, ffn_full))
    out_parts = forward_dot(activated_low, down_full)
    down_grad = transposed_times(activated_low, all_cotangent).astype(bf16)
    ffn_grad = transposed_times(core_major(after(hidden, both_ffn)), both_grad).astype(bf16)
    ffn_grad = first_sum(ffn_grad)
    out_sent = out_parts[token_count:].astype(bf16)
    hidden_grad, ffn_grad, down_grad, out_parts, out_sent = lax.optimization_barrier(
        (hidden_grad, ffn_grad, down_grad, out_parts, out_sent)
    )
    middle_part, ffn_gain_grad = second_pull(hidden_grad)
    middle_grad = cotangent.astype(f32) + middle_part
    branch_low = middle_grad.astype(bf16)
    out_grad = transposed_times(gated_low, branch_low).astype(bf16)
    gated_grad = exchange_seq(times_transposed(branch_low, out_full).astype(bf16), 1, 0)
    ffn_grad = second_sum(ffn_grad)
    tall_grad = jnp.concatenate(
        [out_grad.reshape(shards, out_rows, model), down_grad.reshape(shards, units, model)], axis=1
    ).reshape(shards * (out_rows + units), model)
    gated_grad, ffn_grad, tall_grad = lax.optimization_barrier((gated_grad, ffn_grad, tall_grad))
    ffn_share = third_sum(ffn_grad)
    tall_share = scatter_shard(tall_grad)
    if lax.axis_size("seq") == 2:
        out_parts = out_parts[:token_count] + swap_seq(after(out_sent, gated_grad)).astype(f32)
    else:
        out_parts = sum_own_first(out_parts)
    block_out = (middle + out_parts).astype(bf16)
    mixer_grad, filters_grad, decays_grad, out_gain_grad = mixer_backward(
        raw,
        values,
        filters,
        decays,
        doc_starts,
        gate_rows,
        third_gain,
        gated_grad,
        kept,
        heads,
    )
    mixer_grad, ffn_share, block_out = lax.optimization_barrier((mixer_grad, ffn_share, block_out))
    mixer_weight_grad = transposed_times(normed, mixer_grad).astype(bf16)
    mixer_grad, mixer_weight_grad = lax.optimization_barrier((mixer_grad, mixer_weight_grad))
    mixer_share = scatter_shard(mixer_weight_grad)
    normed_grad = times_transposed(mixer_grad, mixer_full)
    norm_gain_grad = jnp.sum(normed_grad * all_scaled, axis=0)
    if lax.axis_size("seq") == 2:
        sent = own_part(normed_grad, 0, 1 - lax.axis_index("seq")).astype(bf16)
        own_normed_grad = own_part(normed_grad, 0) + swap_seq(sent).astype(f32)
    else:
        sent = normed_grad
        own_normed_grad = sum_scatter_seq(normed_grad, 0)
    _, first_pull = jax.vjp(lambda v: rms_norm(v, first_gain), inputs)
    tokens_grad = middle_grad + first_pull(own_normed_grad)[0]

    def all_units(share):
        share = gather_seq(share.reshape(rows, shards, units), 2)
        return share.reshape(rows, ff).astype(f32)

    ffn_gate_share = all_units(ffn_share[:, :half])
    ffn_up_share = all_units(ffn_share[:, half:])
    tall_share = gather_seq(after(tall_share, mixer_grad)[None], 0).astype(f32)
    out_share = jnp.sum(tall_share[:, :out_rows], axis=0)
    down_share = tall_share[:, out_rows:].reshape(-1, model)
    if lax.axis_size("seq") == 2:
        other_share = swap_seq(mixer_share)

        def side_by_side(start, stop):
            own, other = mixer_share[:, start:stop], other_share[:, start:stop]
            return in_order(own.astype(f32), other.astype(f32), 1)
    else:
        every = gather_seq(mixer_share[None], 0)

        def side_by_side(start, stop):
            part = jnp.swapaxes(every[:, :, start:stop], 0, 1)
            return part.reshape(rows, -1).astype(f32)

    query_share = side_by_side(0, heads * KEY)
    key_share = side_by_side(heads * KEY, width)
    value_share = side_by_side(raw_wide, value_end)
    gate_share = side_by_side(value_end, mixer_share.shape[1])
    logit_share = side_by_side(width, width + 2 * heads).reshape(rows, -1, 2, heads)
    logit_share = jnp.swapaxes(logit_share, 2, 3).reshape(rows, 2 * HEADS)

    all_width = filters.shape[1]
    filters_grad = jnp.sum(filters_grad.reshape(CONV, 8, all_width), axis=1)
    lengths = [shards * n for n in (norm_gain.shape[0], gain_rows, ffn_norm_gain.shape[0])]
    small = jnp.concatenate(
        [
            filters_grad.reshape(CONV * all_width),
            decays_grad.reshape(2 * heads),
            norm_gain_grad,
            jnp.sum(out_gain_grad, axis=0),
            ffn_gain_grad,
        ]
    )
    small = sum_small(after(small, sent), ("shard",))
    head_end = CONV * all_width + 2 * heads
    filters_grad = small[: CONV * all_width].reshape(CONV, all_width)
    decays_grad = small[CONV * all_width : head_end].reshape(2, heads)
    gains = small[head_end:]
    gains = gains + swap_seq(gains) if in_grid() else lax.psum(gains, "seq")
    split = (heads * KEY, 2 * heads * KEY)
    filters_out = jnp.concatenate(
        [
            filters_grad[:, : split[0]].reshape(CONV, heads, KEY),
            filters_grad[:, split[0] : split[1]].reshape(CONV, heads, KEY),
            filters_grad[:, split[1] :].reshape(CONV, heads, VALUE),
        ],
        axis=2,
    )
    gains = [
        gains[: lengths[0]],
        gains[lengths[0] : lengths[0] + lengths[1]],
        gains[lengths[0] + lengths[1] :],
    ]
    place = lax.axis_index("shard")
    gains = [
        lax.dynamic_slice_in_dim(g, place * (g.shape[0] // shards), g.shape[0] // shards)
        for g in gains
    ]
    return (
        block_out[None],
        tokens_grad[None],
        gains[0],
        query_share,
        key_share,
        value_share,
        gate_share,
        logit_share,
        filters_out,
        decays_grad.T,
        gains[1],
        out_share,
        gains[2],
        ffn_gate_share,
        ffn_up_share,
        down_share,
    )


def solution(mesh):
    in_specs = (
        P("shard", "seq", None),
        P("shard", None),
        P("shard"),
        P("shard", None),
        P("shard", None),
        P("shard", None),
        P("shard", None),
        P("shard", None),
        P(None, "seq", None),
        P("seq", None),
        P("shard"),
        P("shard", None),
        P("shard"),
        P("shard", None),
        P("shard", None),
        P("shard", None),
        P("shard", "seq", None),
    )
    out_specs = (
        P("shard", "seq", None),
        P("shard", "seq", None),
        P("shard"),
        P("shard", None),
        P("shard", None),
        P("shard", None),
        P("shard", None),
        P("shard", None),
        P(None, "seq", None),
        P("seq", None),
        P("shard"),
        P("shard", None),
        P("shard"),
        P("shard", None),
        P("shard", None),
        P("shard", None),
    )
    return jax.shard_map(
        on_device, mesh=mesh, in_specs=in_specs, out_specs=out_specs, check_vma=False
    )
```

profile of v0, /device:TPU:0, one launch (start us, length us, event | category | flops | bytes accessed | tf_op | source)
XLA Modules:
  0.0 528.5 jit_solution(9048654496092099374)
XLA Ops:
  13.6 1.8 pad_maximum_fusion.10
  17.0 2.9 collective-permute-start
  23.7 42.2 %collective-permute-done = bf16[1024,1024]{1,0:T(8,128)(2,1)} collective-permute-done((bf16[1024,1024]{1,0:T(8,128)(2,1)}, bf16[1024,1024]{1,0:T(8,128)(2,1)}, u32[]{:S(2)}, u32[]{:S(2)}) %collective-permute-start) | collective-permute-done | bytes 2097184 | tf_op jit(solution)/shard_map/ppermute | solution.py:684
  65.9 2.7 fusion.42
  69.4 10.4 %all-gather.4.cloned.1.call-done = bf16[1024,3200]{1,0:T(8,128)(2,1)} async-done(((bf16[64,3200]{1,0:T(8,128)(2,1)}), bf16[1024,3200]{1,0:T(8,128)(2,1)}) %all-gather.4.cloned.1.call-update) | async-done | bytes 6553616 | tf_op jit(solution)/shard_map/all_gather | solution.py:760
  83.3 6.1 %fusion.17.gate_ref = f32[1024,1024]{1,0:T(8,128)} fusion(bf16[1024,3200]{1,0:T(8,128)(2,1)} %all-gather.4.cloned.1.call-done, f32[1024]{0:T(1024)S(1)} %get-tuple-element.107, f32[1024]{0:T(1024)S(1)} %add_rsqrt_fusion, bf16[512,1024]{1,0:T(8,128)(2,1)S(1)} %bitcast.71, bf16[512,1024]{1,0:T(8,128)(2,1)S(1)} %get-tuple-element.118, pred[]{:T(512)S(6)} %eq.8), kind=kOutput, calls=%fused_computation.44 | convolution fusion | flops 2161115136 | bytes 8396801 | tf_op jit(solution)/shard_map/dot_general | solution.py:664
  89.4 5.7 %fusion.21.value_ref = bf16[1024,1024]{1,0:T(8,128)(2,1)} fusion(bf16[1024,3200]{1,0:T(8,128)(2,1)S(1)} %bitcast.96, f32[1024]{0:T(1024)S(1)} %get-tuple-element.107, f32[1024]{0:T(1024)S(1)} %add_rsqrt_fusion, bf16[512,1024]{1,0:T(8,128)(2,1)S(1)} %bitcast.72, bf16[512,1024]{1,0:T(8,128)(2,1)S(1)} %get-tuple-element.118, pred[]{:T(512)S(6)} %eq.8), kind=kOutput, calls=%fused_computation.59 | convolution fusion | flops 2162163712 | bytes 6299649 | tf_op jit(solution)/shard_map/dot_general | solution.py:664
  95.1 6.0 %convolution_convert_fusion.3.raw_ref = bf16[1024,1152]{1,0:T(8,128)(2,1)} fusion(bf16[1024,3200]{1,0:T(8,128)(2,1)S(1)} %bitcast.96, f32[1024]{0:T(1024)S(1)} %get-tuple-element.107, f32[1024]{0:T(1024)S(1)} %add_rsqrt_fusion, bf16[512,1024]{1,0:T(8,128)(2,1)S(1)} %bitcast.73, bf16[512,1024]{1,0:T(8,128)(2,1)S(1)} %get-tuple-element.118, pred[]{:T(512)S(6)} %eq.8), kind=kOutput, calls=%fused_computation.21 | convolution fusion | flops 2430730240 | bytes 6823937 | tf_op jit(solution)/shard_map/dot_general | solution.py:664
  101.0 35.4 %mixer_forward.1 = (bf16[1024,1024]{1,0:T(8,128)(2,1)}, bf16[1024,1024]{1,0:T(8,128)(2,1)}, bf16[1024,256]{1,0:T(8,128)(2,1)}, f32[4096,256]{1,0:T(8,128)}, bf16...) custom-call(s32[1,4]{1,0:T(1,128)} %starts_ref.3, bf16[1024,1152]{1,0:T(8,128)(2,1)} %convolution_convert_fusion.3.raw_ref, ...), custom_call_target="tpu_custom_call" | custom-call | flops 45056000000 | bytes 16777216 | tf_op jit(solution)/shard_map/mixer_forward/pallas_call | solution.py:577
  139.7 8.1 %all-gather.6.cloned.1.call-done = bf16[3456,1024]{1,0:T(8,128)(2,1)} async-done(((bf16[216,1024]{1,0:T(8,128)(2,1)}), bf16[3456,1024]{1,0:T(8,128)(2,1)}) %all-gather.6.cloned.1.call-update) | async-done | bytes 7077904 | tf_op jit(solution)/shard_map/all_gather | solution.py:760
  147.8 3.7 slice.204
  151.5 2.6 slice.205
  154.2 9.5 %collective-permute-done.1 = bf16[512,1024]{1,0:T(8,128)(2,1)} collective-permute-done((bf16[512,1024]{1,0:T(8,128)(2,1)S(1)}, bf16[512,1024]{1,0:T(8,128)(2,1)}, u32[]{:S(2)}, u32[]{:S(2)}) %collective-permute-start.1) | collective-permute-done | bytes 1048608 | tf_op jit(solution)/shard_map/ppermute | solution.py:684
  163.7 2.4 maximum_select_fusion
  166.1 2.5 multiply_reduce_fusion.2
  170.4 23.1 %collective-permute-done.2 = bf16[512,1024]{1,0:T(8,128)(2,1)} collective-permute-done((bf16[512,1024]{1,0:T(8,128)(2,1)S(1)}, bf16[512,1024]{1,0:T(8,128)(2,1)}, u32[]{:S(2)}, u32[]{:S(2)}) %collective-permute-start.2) | collective-permute-done | bytes 1048608 | tf_op jit(solution)/shard_map/ppermute | solution.py:684
  193.5 2.8 pad_maximum_fusion.7
  196.3 12.0 %all-gather.8.cloned.1.call-done = bf16[1024,2816]{1,0:T(8,128)(2,1)} async-done(((bf16[64,2816]{1,0:T(8,128)(2,1)}), bf16[1024,2816]{1,0:T(8,128)(2,1)}) %all-gather.8.cloned.1.call-update) | async-done | bytes 5767184 | tf_op jit(solution)/shard_map/all_gather | solution.py:760
  208.2 11.8 %fusion.37 = f32[1024,2816]{1,0:T(8,128)} fusion(bf16[1024,2816]{1,0:T(8,128)(2,1)} %all-gather.8.cloned.1.call-done, bf16[512,1024]{1,0:T(8,128)(2,1)} %collective-permute-done.2, bf16[512,1024]{1,0:T(8,128)(2,1)S(1)} %multiply_convert_fusion.2), kind=kOutput, calls=%fused_computation.122 | convolution fusion | flops 5909774336 | bytes 19398656 | tf_op jit(solution)/shard_map/dot_general | solution.py:664
  220.0 4.0 copy.71
  224.0 1.9 copy.72
  226.8 10.5 %fusion.2 = (bf16[1024,1408]{1,0:T(8,128)(2,1)S(1)}, bf16[1024,1408]{1,0:T(8,128)(2,1)S(1)}, bf16[1024,1408]{1,0:T(8,128)(2,1)}) fusion(f32[1024,2816]{1,0:T(8,128)} %fusion.37, bf16[1408,1024]{1,0:T(8,128)(2,1)S(1)} %bitcast.86, bf16[512,1024]{1,0:T(8,128)(2,1)S(1)} %copy-done.22, bf16[512,1024]{1,0:T(8,128)(2,1)S(1)} %bitcast.83), kind=kOutput, calls=%fused_computation.5 | convolution fusion | flops 2980052992 | bytes 25165824 | tf_op jit(solution)/shard_map/dot_general | solution.py:23
  239.8 6.8 %convolution_convert_fusion.1 = bf16[1024,2816]{1,0:T(8,128)(2,1)S(1)} fusion(bf16[1024,1024]{0,1:T(8,128)(2,1)S(1)} %bitcast.88, bf16[1024,1408]{1,0:T(8,128)(2,1)S(1)} %get-tuple-element.113, bf16[1024,1408]{1,0:T(8,128)(2,1)S(1)} %get-tuple-element.112), kind=kOutput, calls=%fused_computation.12 | convolution fusion | flops 5919997952 | bytes 13631488 | tf_op jit(solution)/shard_map/dot_general | solution.py:23
  247.1 9.9 %fusion.9 = f32[1024,1024]{1,0:T(8,128)S(1)} fusion(bf16[1024,2816]{1,0:T(8,128)(2,1)} %all-gather.8.cloned.1.call-done, bf16[1024,1408]{1,0:T(8,128)(2,1)} %copy-done.37, bf16[1024,1408]{1,0:T(8,128)(2,1)} %copy-done.36), kind=kOutput, calls=%fused_computation.23 | convolution fusion | flops 5917114368 | bytes 15728640 | tf_op jit(solution)/shard_map/dot_general | solution.py:23
  259.1 5.4 %fusion.50 = f32[1024,1024]{1,0:T(8,128)S(1)} fusion(bf16[1024,1408]{1,0:T(8,128)(2,1)} %get-tuple-element.114, bf16[1408,1024]{1,0:T(8,128)(2,1)S(1)} %bitcast.87), kind=kOutput, calls=%fused_computation.131 | convolution fusion | flops 2952790016 | bytes 9961472 | tf_op jit(solution)/shard_map/dot_general | solution.py:664
  265.7 4.7 convolution_convert_fusion.4
  270.5 12.0 %collective-permute-done.3 = bf16[512,1024]{1,0:T(8,128)(2,1)S(1)} collective-permute-done((bf16[512,1024]{1,0:T(8,128)(2,1)S(1)}, bf16[512,1024]{1,0:T(8,128)(2,1)S(1)}, u32[]{:S(2)}, u32[]{:S(2)}) %collective-permute-start.3) | collective-permute-done | bytes 1048608 | tf_op jit(solution)/shard_map/ppermute | solution.py:684
  288.0 2.4 convolution_convert_fusion.5
  292.1 4.3 convolution_convert_fusion.2
  296.5 7.0 %pad_maximum_fusion = bf16[16,216,1024]{2,1,0:T(8,128)(2,1)} fusion(bf16[16,88,1024]{2,1,0:T(8,128)(2,1)} %bitcast.85, bf16[16,128,1024]{2,1,0:T(8,128)(2,1)} %bitcast.79), kind=kLoop, calls=%fused_computation.2 | loop fusion | flops 14155776 | bytes 14155776 | tf_op jit(solution)/shard_map/concatenate | solution.py:946
  303.5 11.7 %collective-permute-done.5 = bf16[512,1024]{1,0:T(8,128)(2,1)} collective-permute-done((bf16[512,1024]{1,0:T(8,128)(2,1)S(1)}, bf16[512,1024]{1,0:T(8,128)(2,1)}, u32[]{:S(2)}, u32[]{:S(2)}) %collective-permute-start.5) | collective-permute-done | bytes 1048608 | tf_op jit(solution)/shard_map/ppermute | solution.py:684
  315.2 3.9 maximum_select_fusion.1.gated_grad_ref
  319.5 2.8 add_convert_fusion.1
  325.3 2.0 collective-permute-start.7
  327.4 1.9 collective-permute-start.8
  329.3 51.0 %mixer_backward.1 = (bf16[1024,3200]{1,0:T(8,128)(2,1)}, f32[32,2048]{1,0:T(8,128)}, f32[2,4]{1,0:T(2,128)}, f32[8,256]{1,0:T(8,128)}) custom-call(s32[1,4]{1,0:T(1,128)} %starts_ref.3, bf16[1024,1152]{1,0:T(8,128)(2,1)} %convolution_convert_fusion.3.raw_ref, bf16[1024,1024]{1,0:T(8,128)(2,1)} %fusion.21.value_ref, f32[4,2048]{1,0:T(4,128)} %copy-done.33, ...), custom_call_target="tpu_custom_call" | custom-call | flops 57344000000 | bytes 16777216 | tf_op jit(solution)/shard_map/mixer_backward/pallas_call | solution.py:621
  381.7 2.9 add_convert_fusion.2
  384.6 13.0 %convolution_convert_fusion = bf16[1024,3200]{1,0:T(8,128)(2,1)} fusion(bf16[1024,3200]{1,0:T(8,128)(2,1)} %get-tuple-element.65, f32[1024]{0:T(1024)S(1)} %copy-done.28, f32[1024]{0:T(1024)S(1)} %copy-done.32, bf16[512,1024]{1,0:T(8,128)(2,1)S(1)} %bitcast.74, bf16[512,1024]{1,0:T(8,128)(2,1)S(1)} %copy-done.11, pred[]{:T(512)S(6)} %eq.8), kind=kOutput, calls=%fused_computation.1 | convolution fusion | flops 6727794688 | bytes 15212545 | tf_op jit(solution)/shard_map/dot_general | solution.py:23
  399.0 12.8 %fusion.7 = (f32[1024]{0:T(1024)S(1)}, f32[1024,1024]{1,0:T(8,128)}) fusion(f32[1024]{0:T(1024)S(1)} %copy-done.32, bf16[512,1024]{1,0:T(8,128)(2,1)S(1)} %bitcast.75, bf16[512,1024]{1,0:T(8,128)(2,1)S(1)} %copy-done.12, pred[]{:T(512)S(6)} %eq.8, bf16[1024,3200]{1,0:T(8,128)(2,1)} %get-tuple-element.65, bf16[1024,3200]{1,0:T(8,128)(2,1)} %all-gather.4.cloned.1.call-done), kind=kOutput, calls=%fused_computation.18 | convolution fusion | flops 6724516864 | bytes 19406848 | tf_op jit(solution)/shard_map/dot_general | solution.py:23
  411.9 2.7 dynamic-slice_convert_fusion
  416.4 3.5 collective-permute-done.13
  419.9 2.4 collective-permute-start.14
  431.3 26.5 %collective-permute-done.16 = f32[2304]{0:T(1024)S(1)} collective-permute-done((f32[2304]{0:T(1024)S(1)}, f32[2304]{0:T(1024)S(1)}, u32[]{:S(2)}, u32[]{:S(2)}) %collective-permute-start.16) | collective-permute-done | bytes 9248 | tf_op jit(solution)/shard_map/ppermute | solution.py:684
  462.9 2.8 reshape.247
  465.7 2.6 fusion.15
  468.3 3.9 fusion.14
  472.7 29.2 %reduce-scatter.7.cloned.1.call-done = bf16[64,3200]{1,0:T(8,128)(2,1)} async-done(((bf16[1024,3200]{1,0:T(8,128)(2,1)}), bf16[64,3200]{1,0:T(8,128)(2,1)}) %reduce-scatter.7.cloned.1.call-update) | async-done | bytes 409616 | tf_op jit(solution)/shard_map/reduce_scatter | solution.py:764
  508.9 4.2 collective-permute-done.17
  (241 shorter events, 72.9 us)
Async XLA Ops:
  7.2 6.4 %copy-start = (bf16[176,1024]{1,0:T(8,128)(2,1)S(1)}, bf16[176,1024]{1,0:T(8,128)(2,1)}, u32[]{:S(2)}) copy-start(bf16[176,1024]{1,0:T(8,128)(2,1)} %param.32) | copy-start | bytes 1081348
  7.2 8.3 %copy-start.2 = (bf16[1,512,1024]{2,1,0:T(8,128)(2,1)S(1)}, bf16[1,512,1024]{2,1,0:T(8,128)(2,1)}, u32[]{:S(2)}) copy-start(bf16[1,512,1024]{2,1,0:T(8,128)(2,1)} %param.17) | copy-start | bytes 3145732
  7.2 8.3 %copy-start.13 = (bf16[1,512,1024]{2,1,0:T(8,128)(2,1)S(1)}, bf16[1,512,1024]{2,1,0:T(8,128)(2,1)}, u32[]{:S(2)}) copy-start(bf16[1,512,1024]{2,1,0:T(8,128)(2,1)} %param.33) | copy-start | bytes 3145732
  7.2 72.5 %all-gather.4.cloned.1.call-start = ((), (), s32[]{:S(2)}) async-start(), calls=%async_computation.2 | async-start | bytes 6963200 | tf_op jit(solution)/shard_map/all_gather | solution.py:760
  13.5 134.3 %all-gather.6.cloned.1.call-start = ((), (), s32[]{:S(2)}) async-start(), calls=%async_computation.3 | async-start | bytes 7520256 | tf_op jit(solution)/shard_map/all_gather | solution.py:760
  13.6 6.4 %copy-start.24 = (bf16[64,2816]{1,0:T(8,128)(2,1)S(1)}, bf16[64,2816]{1,0:T(8,128)(2,1)}, u32[]{:S(2)}) copy-start(bf16[64,2816]{1,0:T(8,128)(2,1)} %param.30) | copy-start | bytes 1081348
  15.4 5.5 %copy-start.25 = (bf16[64,2816]{1,0:T(8,128)(2,1)S(1)}, bf16[64,2816]{1,0:T(8,128)(2,1)}, u32[]{:S(2)}) copy-start(bf16[64,2816]{1,0:T(8,128)(2,1)} %param.31) | copy-start | bytes 1081348
  15.4 192.8 %all-gather.8.cloned.1.call-start = ((), (), s32[]{:S(2)}) async-start(), calls=%async_computation.4 | async-start | bytes 6127616 | tf_op jit(solution)/shard_map/all_gather | solution.py:760
  17.0 6.6 %copy-start.29 = (f32[4,4,512]{2,1,0:T(4,128)S(1)}, f32[4,4,512]{2,1,0:T(4,128)}, u32[]{:S(2)}) copy-start(f32[4,4,512]{2,1,0:T(4,128)} %param.25) | copy-start | bytes 98308
  17.0 48.9 %collective-permute-start = (bf16[1024,1024]{1,0:T(8,128)(2,1)}, bf16[1024,1024]{1,0:T(8,128)(2,1)}, u32[]{:S(2)}, u32[]{:S(2)}) collective-permute-start(bf16[1024,1024]{1,0:T(8,128)(2,1)} %pad_maximum_fusion.4), channel_id=1, source_target_pairs={{0,16},{16,0},{1,17},{17,1},{2,18},{18,2},{3,19},{19,3},{4,20},{20... | collective-permute-start | bytes 6291464 | tf_op jit(solution)/shard_map/ppermute | solution.py:684
  23.5 448.7 %reduce-scatter.5.cloned.1.call-start = ((), (), s32[]{:S(2)}) async-start(), calls=%async_computation.5 | async-start | bytes 7520256 | tf_op jit(solution)/shard_map/reduce_scatter | solution.py:764
  23.6 45.7 %copy-start.33 = (f32[4,2048]{1,0:T(4,128)}, f32[4,2048]{1,0:T(4,128)S(1)}, u32[]{:S(2)}) copy-start(f32[4,2048]{1,0:T(4,128)S(1)} %constant_dynamic-update-slice_fusion.filters_ref) | copy-start | bytes 98308
  68.6 26.5 %copy-start.10 = (bf16[512,1024]{1,0:T(8,128)(2,1)}, bf16[512,1024]{1,0:T(8,128)(2,1)S(1)}, u32[]{:S(2)}) copy-start(bf16[512,1024]{1,0:T(8,128)(2,1)S(1)} %get-tuple-element.118) | copy-start | bytes 3145732
  69.3 25.7 %copy-start.31 = (f32[1024]{0:T(1024)}, f32[1024]{0:T(1024)S(1)}, u32[]{:S(2)}) copy-start(f32[1024]{0:T(1024)S(1)} %add_rsqrt_fusion) | copy-start | bytes 12292
  81.7 7.7 %slice-start = ((s8[6553600]{0:T(1024)(128)(4,1)}), s8[4194304]{0:T(1024)(128)(4,1)S(1)}, s32[]{:S(2)}) async-start(s8[6553600]{0:T(1024)(128)(4,1)} %bitcast.95), calls=%async_computation.7 | async-start | bytes 8388608
  83.2 11.8 %copy-start.27 = (f32[1024]{0:T(1024)}, f32[1024]{0:T(1024)S(1)}, u32[]{:S(2)}) copy-start(f32[1024]{0:T(1024)S(1)} %get-tuple-element.107) | copy-start | bytes 12292
  83.3 6.1 %slice-start.1 = ((s8[6553600]{0:T(1024)(128)(4,1)}), s8[2359296]{0:T(1024)(128)(4,1)S(1)}, s32[]{:S(2)}) async-start(s8[6553600]{0:T(1024)(128)(4,1)} %bitcast.95), calls=%async_computation.8 | async-start | bytes 4718592
  138.2 25.5 %collective-permute-start.1 = (bf16[512,1024]{1,0:T(8,128)(2,1)S(1)}, bf16[512,1024]{1,0:T(8,128)(2,1)}, u32[]{:S(2)}, u32[]{:S(2)}) collective-permute-start(bf16[512,1024]{1,0:T(8,128)(2,1)S(1)} %get-tuple-element.120), channel_id=1, source_target_pairs={{0,16},{16,0},{1,17},{17,1},{2,18},{18,2},{3,19},{19,3},{4,20},{20... | collective-permute-start | bytes 3145736 | tf_op jit(solution)/shard_map/ppermute | solution.py:684
  154.2 14.4 %copy-start.8 = (bf16[16,128,1024]{2,1,0:T(8,128)(2,1)}, bf16[16,128,1024]{2,1,0:T(8,128)(2,1)S(1)}, u32[]{:S(2)}) copy-start(bf16[16,128,1024]{2,1,0:T(8,128)(2,1)S(1)} %slice.205) | copy-start | bytes 12582916
  168.8 24.7 %collective-permute-start.2 = (bf16[512,1024]{1,0:T(8,128)(2,1)S(1)}, bf16[512,1024]{1,0:T(8,128)(2,1)}, u32[]{:S(2)}, u32[]{:S(2)}) collective-permute-start(bf16[512,1024]{1,0:T(8,128)(2,1)S(1)} %multiply_convert_fusion.2), channel_id=1, source_target_pairs={{0,16},{16,0},{1,17},{17,1},{2,18},{18,2},{3,19},{19,3},{4,20},{20... | collective-permute-start | bytes 3145736 | tf_op jit(solution)/shard_map/ppermute | solution.py:684
  220.0 6.0 %copy-start.22 = (bf16[512,1024]{1,0:T(8,128)(2,1)S(1)}, bf16[512,1024]{1,0:T(8,128)(2,1)}, u32[]{:S(2)}) copy-start(bf16[512,1024]{1,0:T(8,128)(2,1)} %get-tuple-element.117) | copy-start | bytes 3145732
  246.7 36.1 %collective-permute-start.4 = (bf16[512,2816]{1,0:T(8,128)(2,1)S(1)}, bf16[512,2816]{1,0:T(8,128)(2,1)S(1)}, u32[]{:S(2)}, u32[]{:S(2)}) collective-permute-start(bf16[512,2816]{1,0:T(8,128)(2,1)S(1)} %constant_dynamic-slice_fusion.7), channel_id=1, source_target_pairs={{0,1},{1,0},{2,3},{3,2},{4,5},{5,4},{6,7},{7,6},{8,9},{9,8},{10,11... | collective-permute-start | bytes 8650760 | tf_op jit(solution)/shard_map/ppermute | solution.py:751
  257.2 25.3 %collective-permute-start.3 = (bf16[512,1024]{1,0:T(8,128)(2,1)S(1)}, bf16[512,1024]{1,0:T(8,128)(2,1)S(1)}, u32[]{:S(2)}, u32[]{:S(2)}) collective-permute-start(bf16[512,1024]{1,0:T(8,128)(2,1)S(1)} %slice.263), channel_id=1, source_target_pairs={{0,16},{16,0},{1,17},{17,1},{2,18},{18,2},{3,19},{19,3},{4,20},{20... | collective-permute-start | bytes 3145736 | tf_op jit(solution)/shard_map/ppermute | solution.py:684
  259.1 6.7 %copy-start.35 = (bf16[1024,1408]{1,0:T(8,128)(2,1)S(1)}, bf16[1024,1408]{1,0:T(8,128)(2,1)}, u32[]{:S(2)}) copy-start(bf16[1024,1408]{1,0:T(8,128)(2,1)} %get-tuple-element.114) | copy-start | bytes 8650756
  264.4 6.0 %copy-start.16 = (f32[1024,1024]{1,0:T(8,128)}, f32[1024,1024]{1,0:T(8,128)S(1)}, u32[]{:S(2)}) copy-start(f32[1024,1024]{1,0:T(8,128)S(1)} %fusion.50) | copy-start | bytes 12582916
  265.7 16.8 %copy-start.19 = (f32[1024,1024]{1,0:T(8,128)S(1)}, f32[1024,1024]{1,0:T(8,128)}, u32[]{:S(2)}) copy-start(f32[1024,1024]{1,0:T(8,128)} %copy-done.18) | copy-start | bytes 12582916
  285.0 7.1 %copy-start.6 = (f32[512,1024]{1,0:T(8,128)}, f32[512,1024]{1,0:T(8,128)S(1)}, u32[]{:S(2)}) copy-start(f32[512,1024]{1,0:T(8,128)S(1)} %fusion.12) | copy-start | bytes 6291460
  286.3 33.2 %collective-permute-start.6 = (bf16[256,2816]{1,0:T(8,128)(2,1)}, bf16[256,2816]{1,0:T(8,128)(2,1)}, u32[]{:S(2)}, u32[]{:S(2)}) collective-permute-start(bf16[256,2816]{1,0:T(8,128)(2,1)} %constant_dynamic-slice_fusion.4), channel_id=1, source_target_pairs={{0,2},{1,3},{2,0},{3,1},{4,6},{5,7},{6,4},{7,5},{8,10},{9,11},{10,... | collective-permute-start | bytes 4325384 | tf_op jit(solution)/shard_map/ppermute | solution.py:751
  290.6 24.6 %collective-permute-start.5 = (bf16[512,1024]{1,0:T(8,128)(2,1)S(1)}, bf16[512,1024]{1,0:T(8,128)(2,1)}, u32[]{:S(2)}, u32[]{:S(2)}) collective-permute-start(bf16[512,1024]{1,0:T(8,128)(2,1)S(1)} %get-tuple-element.116), channel_id=1, source_target_pairs={{0,16},{16,0},{1,17},{17,1},{2,18},{18,2},{3,19},{19,3},{4,20},{20... | collective-permute-start | bytes 3145736 | tf_op jit(solution)/shard_map/ppermute | solution.py:684
  303.5 16.0 %copy-start.5 = (bf16[512,2816]{1,0:T(8,128)(2,1)S(1)}, bf16[512,2816]{1,0:T(8,128)(2,1)}, u32[]{:S(2)}) copy-start(bf16[512,2816]{1,0:T(8,128)(2,1)} %copy-done.4) | copy-start | bytes 8650756
  322.3 179.6 %reduce-scatter.7.cloned.1.call-start = ((), (), s32[]{:S(2)}) async-start(), calls=%async_computation.6 | async-start | bytes 6963200 | tf_op jit(solution)/shard_map/reduce_scatter | solution.py:764
  322.5 59.2 %collective-permute-start.10 = (bf16[512,1024]{1,0:T(8,128)(2,1)}, bf16[512,1024]{1,0:T(8,128)(2,1)}, u32[]{:S(2)}, u32[]{:S(2)}) collective-permute-start(bf16[512,1024]{1,0:T(8,128)(2,1)} %slice.262), channel_id=1, source_target_pairs={{0,16},{16,0},{1,17},{17,1},{2,18},{18,2},{3,19},{19,3},{4,20},{20... | collective-permute-start | bytes 3145736 | tf_op jit(solution)/shard_map/ppermute | solution.py:684
  325.3 55.0 %collective-permute-start.7 = (bf16[64,2816]{1,0:T(8,128)(2,1)S(1)}, bf16[64,2816]{1,0:T(8,128)(2,1)S(1)}, u32[]{:S(2)}, u32[]{:S(2)}) collective-permute-start(bf16[64,2816]{1,0:T(8,128)(2,1)S(1)} %get-tuple-element.121), channel_id=1, source_target_pairs={{0,12},{1,13},{2,14},{3,15},{4,0},{5,1},{6,2},{7,3},{8,4},{9,5},{1... | collective-permute-start | bytes 1081352 | tf_op jit(solution)/shard_map/ppermute | solution.py:756
  327.3 53.1 %collective-permute-start.9 = (bf16[64,2816]{1,0:T(8,128)(2,1)S(1)}, bf16[64,2816]{1,0:T(8,128)(2,1)S(1)}, u32[]{:S(2)}, u32[]{:S(2)}) collective-permute-start(bf16[64,2816]{1,0:T(8,128)(2,1)S(1)} %get-tuple-element.122), channel_id=1, source_target_pairs={{0,4},{1,5},{2,6},{3,7},{4,8},{5,9},{6,10},{7,11},{8,12},{9,13},{1... | collective-permute-start | bytes 1081352 | tf_op jit(solution)/shard_map/ppermute | solution.py:756
  327.4 53.0 %collective-permute-start.8 = (bf16[64,2816]{1,0:T(8,128)(2,1)S(1)}, bf16[64,2816]{1,0:T(8,128)(2,1)}, u32[]{:S(2)}, u32[]{:S(2)}) collective-permute-start(bf16[64,2816]{1,0:T(8,128)(2,1)S(1)} %get-tuple-element.123), channel_id=1, source_target_pairs={{0,8},{1,9},{2,10},{3,11},{4,12},{5,13},{6,14},{7,15},{8,0},{9,1},... | collective-permute-start | bytes 1081352 | tf_op jit(solution)/shard_map/ppermute | solution.py:756
  329.3 52.4 %copy-start.17 = (f32[1024,1024]{1,0:T(8,128)S(1)}, f32[1024,1024]{1,0:T(8,128)}, u32[]{:S(2)}) copy-start(f32[1024,1024]{1,0:T(8,128)} %copy-done.16) | copy-start | bytes 12582916
  414.6 1.2 collective-permute-start.12
  415.8 4.1 collective-permute-start.13
  419.9 4.4 collective-permute-start.14
  422.3 43.4 %collective-permute-start.11 = (bf16[512,1024]{1,0:T(8,128)(2,1)}, bf16[512,1024]{1,0:T(8,128)(2,1)}, u32[]{:S(2)}, u32[]{:S(2)}) collective-permute-start(bf16[512,1024]{1,0:T(8,128)(2,1)} %dynamic-slice_convert_fusion), channel_id=1, source_target_pairs={{0,16},{16,0},{1,17},{17,1},{2,18},{18,2},{3,19},{19,3},{4,20},{20... | collective-permute-start | bytes 3145736 | tf_op jit(solution)/shard_map/ppermute | solution.py:684
  424.4 5.0 collective-permute-start.15
  426.1 35.4 %collective-permute-start.19 = (bf16[64,16,88]{2,1,0:T(8,128)(2,1)S(1)}, bf16[64,16,88]{2,1,0:T(8,128)(2,1)S(1)}, u32[]{:S(2)}, u32[]{:S(2)}) collective-permute-start(bf16[64,16,88]{2,1,0:T(8,128)(2,1)S(1)} %reshape.239), channel_id=1, source_target_pairs={{0,16},{16,0},{1,17},{17,1},{2,18},{18,2},{3,19},{19,3},{4,20},{20... | collective-permute-start | bytes 540680 | tf_op jit(solution)/shard_map/ppermute | solution.py:684
  426.6 33.0 %collective-permute-start.20 = (bf16[64,16,88]{2,1,0:T(8,128)(2,1)S(1)}, bf16[64,16,88]{2,1,0:T(8,128)(2,1)S(1)}, u32[]{:S(2)}, u32[]{:S(2)}) collective-permute-start(bf16[64,16,88]{2,1,0:T(8,128)(2,1)S(1)} %reshape.240), channel_id=1, source_target_pairs={{0,16},{16,0},{1,17},{17,1},{2,18},{18,2},{3,19},{19,3},{4,20},{20... | collective-permute-start | bytes 540680 | tf_op jit(solution)/shard_map/ppermute | solution.py:684
  429.4 28.3 %collective-permute-start.16 = (f32[2304]{0:T(1024)S(1)}, f32[2304]{0:T(1024)S(1)}, u32[]{:S(2)}, u32[]{:S(2)}) collective-permute-start(f32[2304]{0:T(1024)S(1)} %slice.212), channel_id=1, source_target_pairs={{0,16},{16,0},{1,17},{17,1},{2,18},{18,2},{3,19},{19,3},{4,20},{20... | collective-permute-start | bytes 27656 | tf_op jit(solution)/shard_map/ppermute | solution.py:684
  462.9 5.4 %copy-start.7 = (f32[512,1024]{1,0:T(8,128)S(1)}, f32[512,1024]{1,0:T(8,128)}, u32[]{:S(2)}) copy-start(f32[512,1024]{1,0:T(8,128)} %copy-done.6) | copy-start | bytes 6291460
  472.2 34.6 %copy-start.23 = (bf16[216,1024]{1,0:T(8,128)(2,1)S(1)}, bf16[216,1024]{1,0:T(8,128)(2,1)}, u32[]{:S(2)}) copy-start(bf16[216,1024]{1,0:T(8,128)(2,1)} %reduce-scatter.5.cloned.1.call-done) | copy-start | bytes 1327108
  472.2 34.6 %collective-permute-start.18 = (bf16[1,216,1024]{2,1,0:T(8,128)(2,1)}, bf16[1,216,1024]{2,1,0:T(8,128)(2,1)S(1)}, u32[]{:S(2)}, u32[]{:S(2)}) collective-permute-start(bf16[1,216,1024]{2,1,0:T(8,128)(2,1)} %bitcast.91), channel_id=1, source_target_pairs={{0,16},{16,0},{1,17},{17,1},{2,18},{18,2},{3,19},{19,3},{4,20},{20... | collective-permute-start | bytes 1327112 | tf_op jit(solution)/shard_map/ppermute | solution.py:684
  502.0 11.1 %collective-permute-start.17 = (bf16[64,3200]{1,0:T(8,128)(2,1)}, bf16[64,3200]{1,0:T(8,128)(2,1)}, u32[]{:S(2)}, u32[]{:S(2)}) collective-permute-start(bf16[64,3200]{1,0:T(8,128)(2,1)} %reduce-scatter.7.cloned.1.call-done), channel_id=1, source_target_pairs={{0,16},{16,0},{1,17},{17,1},{2,18},{18,2},{3,19},{19,3},{4,20},{20... | collective-permute-start | bytes 1228808 | tf_op jit(solution)/shard_map/ppermute | solution.py:684
  (18 other events, 39.2 us)
Sparse Core Ops, SparseCore 0:
  13.6 66.0 all-gather.3
  82.6 65.1 all-gather.5
  150.7 57.5 all-gather.7
  322.4 88.6 reduce-scatter.4
  415.5 86.4 reduce-scatter.6
where the time goes:
time: 535 us; the launch traced here: 529 us
  waiting for transfers between devices  197 us (37%)
  matrix products  102 us (19%)
  Pallas kernels  86.4 us (16%)
  local copies, waits for them, and re-layouts  60.9 us (11%)
  other arithmetic  42.9 us (8%)
  starting transfers between devices  24.4 us (5%)
  between operations  15.2 us (3%)
    ppermute x12, waiting for transfers between devices, swap_seq(): return lax.ppermute(values, 'seq', [(0, 1), (1, 0)])  129 us
    dot_general x8, matrix products, dot(): lax.dot_general(a, b, (((ca,), (cb,)), ((), ())), preferred_element_type=...  64.4 us
    pallas_call x1, Pallas kernels, mixer_backward(): pl.pallas_call(functools.partial(backward_kernel, heads), grid=(steps,),...  51 us
    dot_general x6, matrix products, forward_dot(): return jnp.dot(left_side, right_side, preferred_element_type=f32)  37.4 us
    pallas_call x1, Pallas kernels, mixer_forward(): pl.pallas_call(functools.partial(forward_kernel, heads), grid=(steps,), i...  35.4 us
    all_gather x3, waiting for transfers between devices, gather_shard(): return lax.all_gather(values, 'shard', axis=0, tiled=True)  30.4 us
    reduce_scatter x2, waiting for transfers between devices, scatter_shard(): return lax.psum_scatter(values, 'shard', scatter_dimension=0, tiled=True)  29.2 us
    ppermute x12, starting transfers between devices, swap_seq(): return lax.ppermute(values, 'seq', [(0, 1), (1, 0)])  15.6 us
  transfers between devices with their start and end apart: 26, of which 16 were waited for; matrix products, arithmetic and copies ran while one was open for 27% of the time, Pallas kernels for 16%

commit v1 on v0

--- a/solution.py
+++ b/solution.py
@@ -353,14 +353,15 @@
 
 
 def backward_kernel(
-    heads, starts_ref, raw_ref, value_ref, filters_ref, decay_ref, gate_ref, gain_ref,
-    gated_grad_ref, mixed_ref, inverse_ref, delta_ref, rest_ref, memory_ref,
+    heads, starts_ref, seq_ref, raw_ref, value_ref, filters_ref, decay_ref, gate_ref, gain_ref,
+    own_grad_ref, other_grad_ref, mixed_ref, inverse_ref, delta_ref, rest_ref, memory_ref,
     raw_grad_ref, filters_grad_ref, decay_grad_ref, gain_grad_ref,
     state, halo,
 ):
     step = pl.program_id(0)
     steps = pl.num_programs(0)
     width = 2 * heads * KEY
+    own_rows = (2 * (steps - 1 - step) >= steps) == (seq_ref[0] != 0)
 
     @pl.when(step == 0)
     def _():
@@ -383,7 +384,11 @@
         mixed_grads = []
         for h in range(heads):
             lanes = slice(h * VALUE, (h + 1) * VALUE)
-            grad = gated_grad_ref[here, lanes].astype(f32)
+            grad = jnp.where(
+                own_rows,
+                own_grad_ref[here, lanes].astype(f32),
+                other_grad_ref[here, lanes].astype(f32),
+            )
             mixed = mixed_ref[here, lanes].astype(f32)
             gate = gate_ref[here, lanes]
             scale = lax.rsqrt(jnp.mean(mixed * mixed, axis=1, keepdims=True) + epsilon)
@@ -611,17 +616,20 @@
     )(starts, raw, values, filters, decays, gates, gain)
 
 
-def mixer_backward(raw, values, filters, decays, starts, gates, gain, gated_grad, kept, heads):
+def mixer_backward(raw, values, filters, decays, starts, gates, gain, gated_grads, kept, heads):
     length, wide = raw.shape
     steps = length // (SUB * GROUP)
     rows = SUB * GROUP
     whole = lambda a: pl.BlockSpec(a.shape, lambda i: (0, 0))
     same = lambda r, c: pl.BlockSpec((r, c), lambda i: (0, 0))
     part = lambda r, c: pl.BlockSpec((r, c), lambda i: (steps - 1 - i, 0))
+    count = gated_grads[0].shape[0] // rows
+    part_grad = pl.BlockSpec((rows, heads * VALUE), lambda i: (lax.rem(steps - 1 - i, count), 0))
     return pl.pallas_call(
         functools.partial(backward_kernel, heads),
         grid=(steps,),
         in_specs=[
+            pl.BlockSpec(memory_space=pltpu.SMEM),
             pl.BlockSpec(memory_space=pltpu.SMEM),
             whole(raw),
             whole(values),
@@ -629,7 +637,8 @@
             whole(decays),
             part(rows, heads * VALUE),
             whole(gain),
-            part(rows, heads * VALUE),
+            part_grad,
+            part_grad,
             part(rows, heads * VALUE),
             part(rows, heads * GROUP),
             part(rows * heads, VALUE),
@@ -657,7 +666,7 @@
             flops=length * heads * 14_000_000, bytes_accessed=2**24, transcendentals=0
         ),
         name="mixer_backward",
-    )(starts, raw, values, filters, decays, gates, gain, gated_grad, *kept)
+    )(starts, seq_index(), raw, values, filters, decays, gates, gain, *gated_grads, *kept)
 
 
 def forward_dot(left_side, right_side):
@@ -801,6 +810,39 @@
 
 def third_sum(values):
     return sum_along(values) if in_grid() else scatter_shard(values)
+
+
+def spread_kernel(cuts, seq_ref, own_ref, other_ref, *out_refs):
+    def write(first, second):
+        for (start, stop), out_ref in zip(cuts, out_refs):
+            out_ref[:, : stop - start] = first[:, start:stop].astype(f32)
+            out_ref[:, stop - start :] = second[:, start:stop].astype(f32)
+
+    @pl.when(seq_ref[0] == 0)
+    def _():
+        write(own_ref, other_ref)
+
+    @pl.when(seq_ref[0] != 0)
+    def _():
+        write(other_ref, own_ref)
+
+
+def spread(own, other, cuts):
+    rows = own.shape[0]
+    memory = pl.BlockSpec(memory_space=pltpu.VMEM)
+    return pl.pallas_call(
+        functools.partial(spread_kernel, cuts),
+        in_specs=[pl.BlockSpec(memory_space=pltpu.SMEM), memory, memory],
+        out_specs=[memory] * len(cuts),
+        out_shape=[jax.ShapeDtypeStruct((rows, 2 * (b - a)), f32) for a, b in cuts],
+        compiler_params=pltpu.CompilerParams(vmem_limit_bytes=SPACE // 4),
+        cost_estimate=pl.CostEstimate(flops=2**20, bytes_accessed=2**22, transcendentals=0),
+        name="spread",
+    )(seq_index(), own, other)
+
+
+def seq_index():
+    return jnp.stack([lax.axis_index("seq")]).astype(jnp.int32)
 
 
 def after(values, *earlier):
@@ -941,16 +983,23 @@
     middle_grad = cotangent.astype(f32) + middle_part
     branch_low = middle_grad.astype(bf16)
     out_grad = transposed_times(gated_low, branch_low).astype(bf16)
-    gated_grad = exchange_seq(times_transposed(branch_low, out_full).astype(bf16), 1, 0)
+    gated_grad = times_transposed(branch_low, out_full).astype(bf16)
+    if lax.axis_size("seq") == 2:
+        other_grad = swap_seq(own_part(gated_grad, 1, 1 - lax.axis_index("seq")))
+        own_grad = own_part(gated_grad, 1)
+    else:
+        own_grad = other_grad = exchange_seq(gated_grad, 1, 0)
     ffn_grad = second_sum(ffn_grad)
     tall_grad = jnp.concatenate(
         [out_grad.reshape(shards, out_rows, model), down_grad.reshape(shards, units, model)], axis=1
     ).reshape(shards * (out_rows + units), model)
-    gated_grad, ffn_grad, tall_grad = lax.optimization_barrier((gated_grad, ffn_grad, tall_grad))
+    own_grad, other_grad, ffn_grad, tall_grad = lax.optimization_barrier(
+        (own_grad, other_grad, ffn_grad, tall_grad)
+    )
     ffn_share = third_sum(ffn_grad)
     tall_share = scatter_shard(tall_grad)
     if lax.axis_size("seq") == 2:
-        out_parts = out_parts[:token_count] + swap_seq(after(out_sent, gated_grad)).astype(f32)
+        out_parts = out_parts[:token_count] + swap_seq(after(out_sent, other_grad)).astype(f32)
     else:
         out_parts = sum_own_first(out_parts)
     block_out = (middle + out_parts).astype(bf16)
@@ -962,7 +1011,7 @@
         doc_starts,
         gate_rows,
         third_gain,
-        gated_grad,
+        (own_grad, other_grad),
         kept,
         heads,
     )
@@ -1003,10 +1052,17 @@
             part = jnp.swapaxes(every[:, :, start:stop], 0, 1)
             return part.reshape(rows, -1).astype(f32)
 
-    query_share = side_by_side(0, heads * KEY)
-    key_share = side_by_side(heads * KEY, width)
-    value_share = side_by_side(raw_wide, value_end)
-    gate_share = side_by_side(value_end, mixer_share.shape[1])
+    cuts = (
+        (0, heads * KEY),
+        (heads * KEY, width),
+        (raw_wide, value_end),
+        (value_end, mixer_share.shape[1]),
+    )
+    if lax.axis_size("seq") == 2:
+        shares = spread(mixer_share, other_share, cuts)
+    else:
+        shares = [side_by_side(start, stop) for start, stop in cuts]
+    query_share, key_share, value_share, gate_share = shares
     logit_share = side_by_side(width, width + 2 * heads).reshape(rows, -1, 2, heads)
     logit_share = jnp.swapaxes(logit_share, 2, 3).reshape(rows, 2 * HEADS)
 

time: 535 us -> 528 us (0.987)
  local copies, waits for them, and re-layouts: 60.9 us -> 51.5 us
    ppermute x6, waiting for transfers between devices: 7.9 us -> 22.4 us  [flip(): return lax.ppermute(values, 'shard', [(i, i ^ mask) for i in range(size)])]
    ppermute x12, waiting for transfers between devices: 129 us -> 119 us  [swap_seq(): return lax.ppermute(values, 'seq', [(0, 1), (1, 0)])]
    unnamed x102 -> x86, local copies, waits for them, and re-layouts: 11.9 us -> 6.34 us
  transfers between devices with their start and end apart: 26 -> 26, of which waited for: 16 -> 15; matrix products, arithmetic and copies ran while one was open for 27% -> 27% of each run, Pallas kernels for 16% -> 17%
where the time goes in v1:
time: 528 us; the launch traced here: 522 us
  waiting for transfers between devices  200 us (38%)
  matrix products  102 us (19%)
  Pallas kernels  88.3 us (17%)
  local copies, waits for them, and re-layouts  51.5 us (10%)
  other arithmetic  40.6 us (8%)
  starting transfers between devices  24.1 us (5%)
  between operations  15 us (3%)
    ppermute x12, waiting for transfers between devices, swap_seq(): return lax.ppermute(values, 'seq', [(0, 1), (1, 0)])  119 us
    dot_general x8, matrix products, dot(): lax.dot_general(a, b, (((ca,), (cb,)), ((), ())), preferred_element_type=...  64.5 us
    pallas_call x1, Pallas kernels, mixer_backward(): pl.pallas_call(functools.partial(backward_kernel, heads), grid=(steps,),...  51.6 us
    dot_general x6, matrix products, forward_dot(): return jnp.dot(left_side, right_side, preferred_element_type=f32)  37.5 us
    pallas_call x1, Pallas kernels, mixer_forward(): pl.pallas_call(functools.partial(forward_kernel, heads), grid=(steps,), i...  35.4 us
    all_gather x3, waiting for transfers between devices, gather_shard(): return lax.all_gather(values, 'shard', axis=0, tiled=True)  30.5 us
    reduce_scatter x2, waiting for transfers between devices, scatter_shard(): return lax.psum_scatter(values, 'shard', scatter_dimension=0, tiled=True)  28.5 us
    ppermute x6, waiting for transfers between devices, flip(): return lax.ppermute(values, 'shard', [(i, i ^ mask) for i in range(size)])  22.4 us
  transfers between devices with their start and end apart: 26, of which 15 were waited for; matrix products, arithmetic and copies ran while one was open for 27% of the time, Pallas kernels for 17%

profile of v1, /device:TPU:0, one launch (start us, length us, event | category | flops | bytes accessed | tf_op | source)
XLA Modules:
  0.0 521.8 jit_solution(9865070097452778642)
XLA Ops:
  13.6 1.8 pad_maximum_fusion.10
  17.0 2.9 collective-permute-start
  23.7 42.2 %collective-permute-done = bf16[1024,1024]{1,0:T(8,128)(2,1)} collective-permute-done((bf16[1024,1024]{1,0:T(8,128)(2,1)}, bf16[1024,1024]{1,0:T(8,128)(2,1)}, u32[]{:S(2)}, u32[]{:S(2)}) %collective-permute-start) | collective-permute-done | bytes 2097184 | tf_op jit(solution)/shard_map/ppermute | solution.py:693
  65.9 2.7 fusion.42
  69.4 10.4 %all-gather.4.cloned.1.call-done = bf16[1024,3200]{1,0:T(8,128)(2,1)} async-done(((bf16[64,3200]{1,0:T(8,128)(2,1)}), bf16[1024,3200]{1,0:T(8,128)(2,1)}) %all-gather.4.cloned.1.call-update) | async-done | bytes 6553616 | tf_op jit(solution)/shard_map/all_gather | solution.py:769
  83.3 6.1 %fusion.17.gate_ref = f32[1024,1024]{1,0:T(8,128)} fusion(bf16[1024,3200]{1,0:T(8,128)(2,1)} %all-gather.4.cloned.1.call-done, f32[1024]{0:T(1024)S(1)} %get-tuple-element.85, f32[1024]{0:T(1024)S(1)} %add_rsqrt_fusion, bf16[512,1024]{1,0:T(8,128)(2,1)S(1)} %bitcast.69, bf16[512,1024]{1,0:T(8,128)(2,1)S(1)} %get-tuple-element.96, pred[]{:T(512)S(6)} %eq.14), kind=kOutput, calls=%fused_computation.44 | convolution fusion | flops 2161115136 | bytes 8396801 | tf_op jit(solution)/shard_map/dot_general | solution.py:673
  89.4 5.7 %fusion.21.value_ref = bf16[1024,1024]{1,0:T(8,128)(2,1)} fusion(bf16[1024,3200]{1,0:T(8,128)(2,1)S(1)} %bitcast.94, f32[1024]{0:T(1024)S(1)} %get-tuple-element.85, f32[1024]{0:T(1024)S(1)} %add_rsqrt_fusion, bf16[512,1024]{1,0:T(8,128)(2,1)S(1)} %bitcast.70, bf16[512,1024]{1,0:T(8,128)(2,1)S(1)} %get-tuple-element.96, pred[]{:T(512)S(6)} %eq.14), kind=kOutput, calls=%fused_computation.58 | convolution fusion | flops 2162163712 | bytes 6299649 | tf_op jit(solution)/shard_map/dot_general | solution.py:673
  95.1 6.0 %convolution_convert_fusion.3.raw_ref = bf16[1024,1152]{1,0:T(8,128)(2,1)} fusion(bf16[1024,3200]{1,0:T(8,128)(2,1)S(1)} %bitcast.94, f32[1024]{0:T(1024)S(1)} %get-tuple-element.85, f32[1024]{0:T(1024)S(1)} %add_rsqrt_fusion, bf16[512,1024]{1,0:T(8,128)(2,1)S(1)} %bitcast.71, bf16[512,1024]{1,0:T(8,128)(2,1)S(1)} %get-tuple-element.96, pred[]{:T(512)S(6)} %eq.14), kind=kOutput, calls=%fused_computation.21 | convolution fusion | flops 2430730240 | bytes 6823937 | tf_op jit(solution)/shard_map/dot_general | solution.py:673
  101.0 35.4 %mixer_forward.1 = (bf16[1024,1024]{1,0:T(8,128)(2,1)}, bf16[1024,1024]{1,0:T(8,128)(2,1)}, bf16[1024,256]{1,0:T(8,128)(2,1)}, f32[4096,256]{1,0:T(8,128)}, bf16...) custom-call(s32[1,4]{1,0:T(1,128)} %starts_ref.3, bf16[1024,1152]{1,0:T(8,128)(2,1)} %convolution_convert_fusion.3.raw_ref, ...), custom_call_target="tpu_custom_call" | custom-call | flops 45056000000 | bytes 16777216 | tf_op jit(solution)/shard_map/mixer_forward/pallas_call | solution.py:582
  136.5 1.7 constant_dynamic-slice_fusion.12
  139.7 8.1 %all-gather.6.cloned.1.call-done = bf16[3456,1024]{1,0:T(8,128)(2,1)} async-done(((bf16[216,1024]{1,0:T(8,128)(2,1)}), bf16[3456,1024]{1,0:T(8,128)(2,1)}) %all-gather.6.cloned.1.call-update) | async-done | bytes 7077904 | tf_op jit(solution)/shard_map/all_gather | solution.py:769
  147.8 3.7 slice.172
  151.5 2.6 slice.173
  154.1 9.6 %collective-permute-done.1 = bf16[512,1024]{1,0:T(8,128)(2,1)} collective-permute-done((bf16[512,1024]{1,0:T(8,128)(2,1)S(1)}, bf16[512,1024]{1,0:T(8,128)(2,1)}, u32[]{:S(2)}, u32[]{:S(2)}) %collective-permute-start.1) | collective-permute-done | bytes 1048608 | tf_op jit(solution)/shard_map/ppermute | solution.py:693
  163.7 2.4 maximum_select_fusion
  166.1 2.5 multiply_reduce_fusion.2
  170.4 23.2 %collective-permute-done.2 = bf16[512,1024]{1,0:T(8,128)(2,1)} collective-permute-done((bf16[512,1024]{1,0:T(8,128)(2,1)S(1)}, bf16[512,1024]{1,0:T(8,128)(2,1)}, u32[]{:S(2)}, u32[]{:S(2)}) %collective-permute-start.2) | collective-permute-done | bytes 1048608 | tf_op jit(solution)/shard_map/ppermute | solution.py:693
  193.5 2.7 pad_maximum_fusion.7
  196.2 12.0 %all-gather.8.cloned.1.call-done = bf16[1024,2816]{1,0:T(8,128)(2,1)} async-done(((bf16[64,2816]{1,0:T(8,128)(2,1)}), bf16[1024,2816]{1,0:T(8,128)(2,1)}) %all-gather.8.cloned.1.call-update) | async-done | bytes 5767184 | tf_op jit(solution)/shard_map/all_gather | solution.py:769
  208.3 11.9 %fusion.37 = f32[1024,2816]{1,0:T(8,128)} fusion(bf16[1024,2816]{1,0:T(8,128)(2,1)} %all-gather.8.cloned.1.call-done, bf16[512,1024]{1,0:T(8,128)(2,1)} %collective-permute-done.2, bf16[512,1024]{1,0:T(8,128)(2,1)S(1)} %multiply_convert_fusion.2), kind=kOutput, calls=%fused_computation.119 | convolution fusion | flops 5909774336 | bytes 19398656 | tf_op jit(solution)/shard_map/dot_general | solution.py:673
  220.1 4.1 copy.59
  224.2 1.9 copy.60
  226.9 10.5 %fusion.2 = (bf16[1024,1408]{1,0:T(8,128)(2,1)S(1)}, bf16[1024,1408]{1,0:T(8,128)(2,1)S(1)}, bf16[1024,1408]{1,0:T(8,128)(2,1)}) fusion(f32[1024,2816]{1,0:T(8,128)} %fusion.37, bf16[1408,1024]{1,0:T(8,128)(2,1)S(1)} %bitcast.84, bf16[512,1024]{1,0:T(8,128)(2,1)S(1)} %copy-done.22, bf16[512,1024]{1,0:T(8,128)(2,1)S(1)} %bitcast.81), kind=kOutput, calls=%fused_computation.5 | convolution fusion | flops 2980052992 | bytes 25165824 | tf_op jit(solution)/shard_map/dot_general | solution.py:23
  239.8 6.8 %convolution_convert_fusion.1 = bf16[1024,2816]{1,0:T(8,128)(2,1)S(1)} fusion(bf16[1024,1024]{0,1:T(8,128)(2,1)S(1)} %bitcast.86, bf16[1024,1408]{1,0:T(8,128)(2,1)S(1)} %get-tuple-element.91, bf16[1024,1408]{1,0:T(8,128)(2,1)S(1)} %get-tuple-element.90), kind=kOutput, calls=%fused_computation.12 | convolution fusion | flops 5919997952 | bytes 13631488 | tf_op jit(solution)/shard_map/dot_general | solution.py:23
  247.1 9.9 %fusion.9 = f32[1024,1024]{1,0:T(8,128)S(1)} fusion(bf16[1024,2816]{1,0:T(8,128)(2,1)} %all-gather.8.cloned.1.call-done, bf16[1024,1408]{1,0:T(8,128)(2,1)} %copy-done.36, bf16[1024,1408]{1,0:T(8,128)(2,1)} %copy-done.35), kind=kOutput, calls=%fused_computation.23 | convolution fusion | flops 5917114368 | bytes 15728640 | tf_op jit(solution)/shard_map/dot_general | solution.py:23
  259.0 5.4 %fusion.46 = f32[1024,1024]{1,0:T(8,128)S(1)} fusion(bf16[1024,1408]{1,0:T(8,128)(2,1)} %get-tuple-element.92, bf16[1408,1024]{1,0:T(8,128)(2,1)S(1)} %bitcast.85), kind=kOutput, calls=%fused_computation.124 | convolution fusion | flops 2952790016 | bytes 9961472 | tf_op jit(solution)/shard_map/dot_general | solution.py:673
  265.7 4.7 convolution_convert_fusion.4
  270.4 12.1 %collective-permute-done.3 = bf16[512,1024]{1,0:T(8,128)(2,1)S(1)} collective-permute-done((bf16[512,1024]{1,0:T(8,128)(2,1)S(1)}, bf16[512,1024]{1,0:T(8,128)(2,1)S(1)}, u32[]{:S(2)}, u32[]{:S(2)}) %collective-permute-start.3) | collective-permute-done | bytes 1048608 | tf_op jit(solution)/shard_map/ppermute | solution.py:693
  288.1 2.4 convolution_convert_fusion.5
  293.2 4.5 convolution_convert_fusion.2
  297.6 7.0 %pad_maximum_fusion = bf16[16,216,1024]{2,1,0:T(8,128)(2,1)} fusion(bf16[16,88,1024]{2,1,0:T(8,128)(2,1)} %bitcast.83, bf16[16,128,1024]{2,1,0:T(8,128)(2,1)} %bitcast.77), kind=kLoop, calls=%fused_computation.2 | loop fusion | flops 14155776 | bytes 14155776 | tf_op jit(solution)/shard_map/concatenate | solution.py:993
  304.7 14.8 %collective-permute-done.6 = bf16[256,2816]{1,0:T(8,128)(2,1)S(1)} collective-permute-done((bf16[256,2816]{1,0:T(8,128)(2,1)}, bf16[256,2816]{1,0:T(8,128)(2,1)S(1)}, u32[]{:S(2)}, u32[]{:S(2)}) %collective-permute-start.6) | collective-permute-done | bytes 1441824 | tf_op jit(solution)/shard_map/ppermute | solution.py:760
  319.5 2.8 add_convert_fusion.1
  325.3 2.0 collective-permute-start.7
  327.4 1.9 collective-permute-start.8
  329.3 51.6 %mixer_backward.1 = (bf16[1024,3200]{1,0:T(8,128)(2,1)}, f32[32,2048]{1,0:T(8,128)}, f32[2,4]{1,0:T(2,128)}, f32[8,256]{1,0:T(8,128)}) custom-call(s32[1,4]{1,0:T(1,128)} %starts_ref.3, s32[1]{0:T(128)} %bitcast.seq_ref, bf16[1024,1152]{1,0:T(8,128)(2,1)} %convolution_convert_fusion.3.raw_ref, bf16[1024,1024]{1,0:T(8,128)(2,1)} %fusion.21.value_ref, ...), custom_call_target="tpu_custom_call" | custom-call | flops 57344000000 | bytes 16777216 | tf_op jit(solution)/shard_map/mixer_backward/pallas_call | solution.py:628
  382.4 2.9 add_convert_fusion.2
  385.3 13.0 %convolution_convert_fusion = bf16[1024,3200]{1,0:T(8,128)(2,1)} fusion(bf16[1024,3200]{1,0:T(8,128)(2,1)} %get-tuple-element.71, f32[1024]{0:T(1024)S(1)} %copy-done.27, f32[1024]{0:T(1024)S(1)} %copy-done.31, bf16[512,1024]{1,0:T(8,128)(2,1)S(1)} %bitcast.72, bf16[512,1024]{1,0:T(8,128)(2,1)S(1)} %copy-done.11, pred[]{:T(512)S(6)} %eq.14), kind=kOutput, calls=%fused_computation.1 | convolution fusion | flops 6727794688 | bytes 15212545 | tf_op jit(solution)/shard_map/dot_general | solution.py:23
  399.7 12.8 %fusion.7 = (f32[1024]{0:T(1024)S(1)}, f32[1024,1024]{1,0:T(8,128)}) fusion(f32[1024]{0:T(1024)S(1)} %copy-done.31, bf16[512,1024]{1,0:T(8,128)(2,1)S(1)} %bitcast.73, bf16[512,1024]{1,0:T(8,128)(2,1)S(1)} %copy-done.12, pred[]{:T(512)S(6)} %eq.14, bf16[1024,3200]{1,0:T(8,128)(2,1)} %get-tuple-element.71, bf16[1024,3200]{1,0:T(8,128)(2,1)} %all-gather.4.cloned.1.call-done), kind=kOutput, calls=%fused_computation.18 | convolution fusion | flops 6724516864 | bytes 19406848 | tf_op jit(solution)/shard_map/dot_general | solution.py:23
  412.6 2.7 dynamic-slice_convert_fusion
  417.1 3.6 collective-permute-done.13
  420.7 2.4 collective-permute-start.14
  432.0 26.5 %collective-permute-done.16 = f32[2304]{0:T(1024)S(1)} collective-permute-done((f32[2304]{0:T(1024)S(1)}, f32[2304]{0:T(1024)S(1)}, u32[]{:S(2)}, u32[]{:S(2)}) %collective-permute-start.16) | collective-permute-done | bytes 9248 | tf_op jit(solution)/shard_map/ppermute | solution.py:693
  463.6 2.8 reshape.247
  466.4 2.8 fusion.15
  469.6 3.9 fusion.14
  473.4 28.5 %reduce-scatter.3.cloned.1.call-done.own_ref = bf16[64,3200]{1,0:T(8,128)(2,1)} async-done(((bf16[1024,3200]{1,0:T(8,128)(2,1)}), bf16[64,3200]{1,0:T(8,128)(2,1)}) %reduce-scatter.3.cloned.1.call-update) | async-done | bytes 409616 | tf_op jit(solution)/shard_map/reduce_scatter | solution.py:773
  507.7 5.2 %collective-permute-done.17.other_ref = bf16[64,3200]{1,0:T(8,128)(2,1)S(1)} collective-permute-done((bf16[64,3200]{1,0:T(8,128)(2,1)}, bf16[64,3200]{1,0:T(8,128)(2,1)S(1)}, u32[]{:S(2)}, u32[]{:S(2)}) %collective-permute-start.17) | collective-permute-done | bytes 409632 | tf_op jit(solution)/shard_map/ppermute | solution.py:693
  (209 shorter events, 63.7 us)
Async XLA Ops:
  7.2 6.4 %copy-start = (bf16[176,1024]{1,0:T(8,128)(2,1)S(1)}, bf16[176,1024]{1,0:T(8,128)(2,1)}, u32[]{:S(2)}) copy-start(bf16[176,1024]{1,0:T(8,128)(2,1)} %param.32) | copy-start | bytes 1081348
  7.2 8.3 %copy-start.3 = (bf16[1,512,1024]{2,1,0:T(8,128)(2,1)S(1)}, bf16[1,512,1024]{2,1,0:T(8,128)(2,1)}, u32[]{:S(2)}) copy-start(bf16[1,512,1024]{2,1,0:T(8,128)(2,1)} %param.17) | copy-start | bytes 3145732
  7.2 8.3 %copy-start.13 = (bf16[1,512,1024]{2,1,0:T(8,128)(2,1)S(1)}, bf16[1,512,1024]{2,1,0:T(8,128)(2,1)}, u32[]{:S(2)}) copy-start(bf16[1,512,1024]{2,1,0:T(8,128)(2,1)} %param.33) | copy-start | bytes 3145732
  7.2 72.5 %all-gather.4.cloned.1.call-start = ((), (), s32[]{:S(2)}) async-start(), calls=%async_computation.2 | async-start | bytes 6963200 | tf_op jit(solution)/shard_map/all_gather | solution.py:769
  13.5 134.3 %all-gather.6.cloned.1.call-start = ((), (), s32[]{:S(2)}) async-start(), calls=%async_computation.3 | async-start | bytes 7520256 | tf_op jit(solution)/shard_map/all_gather | solution.py:769
  13.6 6.4 %copy-start.23 = (bf16[64,2816]{1,0:T(8,128)(2,1)S(1)}, bf16[64,2816]{1,0:T(8,128)(2,1)}, u32[]{:S(2)}) copy-start(bf16[64,2816]{1,0:T(8,128)(2,1)} %param.30) | copy-start | bytes 1081348
  15.4 5.5 %copy-start.24 = (bf16[64,2816]{1,0:T(8,128)(2,1)S(1)}, bf16[64,2816]{1,0:T(8,128)(2,1)}, u32[]{:S(2)}) copy-start(bf16[64,2816]{1,0:T(8,128)(2,1)} %param.31) | copy-start | bytes 1081348
  15.4 192.8 %all-gather.8.cloned.1.call-start = ((), (), s32[]{:S(2)}) async-start(), calls=%async_computation.4 | async-start | bytes 6127616 | tf_op jit(solution)/shard_map/all_gather | solution.py:769
  17.0 6.6 %copy-start.28 = (f32[4,4,512]{2,1,0:T(4,128)S(1)}, f32[4,4,512]{2,1,0:T(4,128)}, u32[]{:S(2)}) copy-start(f32[4,4,512]{2,1,0:T(4,128)} %param.25) | copy-start | bytes 98308
  17.0 48.9 %collective-permute-start = (bf16[1024,1024]{1,0:T(8,128)(2,1)}, bf16[1024,1024]{1,0:T(8,128)(2,1)}, u32[]{:S(2)}, u32[]{:S(2)}) collective-permute-start(bf16[1024,1024]{1,0:T(8,128)(2,1)} %pad_maximum_fusion.4), channel_id=1, source_target_pairs={{0,16},{16,0},{1,17},{17,1},{2,18},{18,2},{3,19},{19,3},{4,20},{20... | collective-permute-start | bytes 6291464 | tf_op jit(solution)/shard_map/ppermute | solution.py:693
  23.5 445.7 %reduce-scatter.5.cloned.1.call-start = ((), (), s32[]{:S(2)}) async-start(), calls=%async_computation.6 | async-start | bytes 7520256 | tf_op jit(solution)/shard_map/reduce_scatter | solution.py:773
  23.6 45.7 %copy-start.32 = (f32[4,2048]{1,0:T(4,128)}, f32[4,2048]{1,0:T(4,128)S(1)}, u32[]{:S(2)}) copy-start(f32[4,2048]{1,0:T(4,128)S(1)} %constant_dynamic-update-slice_fusion.filters_ref) | copy-start | bytes 98308
  68.6 26.5 %copy-start.10 = (bf16[512,1024]{1,0:T(8,128)(2,1)}, bf16[512,1024]{1,0:T(8,128)(2,1)S(1)}, u32[]{:S(2)}) copy-start(bf16[512,1024]{1,0:T(8,128)(2,1)S(1)} %get-tuple-element.96) | copy-start | bytes 3145732
  69.3 25.7 %copy-start.30 = (f32[1024]{0:T(1024)}, f32[1024]{0:T(1024)S(1)}, u32[]{:S(2)}) copy-start(f32[1024]{0:T(1024)S(1)} %add_rsqrt_fusion) | copy-start | bytes 12292
  81.7 7.7 %slice-start = ((s8[6553600]{0:T(1024)(128)(4,1)}), s8[4194304]{0:T(1024)(128)(4,1)S(1)}, s32[]{:S(2)}) async-start(s8[6553600]{0:T(1024)(128)(4,1)} %bitcast.93), calls=%async_computation.7 | async-start | bytes 8388608
  83.2 11.8 %copy-start.26 = (f32[1024]{0:T(1024)}, f32[1024]{0:T(1024)S(1)}, u32[]{:S(2)}) copy-start(f32[1024]{0:T(1024)S(1)} %get-tuple-element.85) | copy-start | bytes 12292
  83.3 6.1 %slice-start.1 = ((s8[6553600]{0:T(1024)(128)(4,1)}), s8[2359296]{0:T(1024)(128)(4,1)S(1)}, s32[]{:S(2)}) async-start(s8[6553600]{0:T(1024)(128)(4,1)} %bitcast.93), calls=%async_computation.8 | async-start | bytes 4718592
  138.2 25.5 %collective-permute-start.1 = (bf16[512,1024]{1,0:T(8,128)(2,1)S(1)}, bf16[512,1024]{1,0:T(8,128)(2,1)}, u32[]{:S(2)}, u32[]{:S(2)}) collective-permute-start(bf16[512,1024]{1,0:T(8,128)(2,1)S(1)} %get-tuple-element.98), channel_id=1, source_target_pairs={{0,16},{16,0},{1,17},{17,1},{2,18},{18,2},{3,19},{19,3},{4,20},{20... | collective-permute-start | bytes 3145736 | tf_op jit(solution)/shard_map/ppermute | solution.py:693
  154.1 14.4 %copy-start.8 = (bf16[16,128,1024]{2,1,0:T(8,128)(2,1)}, bf16[16,128,1024]{2,1,0:T(8,128)(2,1)S(1)}, u32[]{:S(2)}) copy-start(bf16[16,128,1024]{2,1,0:T(8,128)(2,1)S(1)} %slice.173) | copy-start | bytes 12582916
  168.8 24.7 %collective-permute-start.2 = (bf16[512,1024]{1,0:T(8,128)(2,1)S(1)}, bf16[512,1024]{1,0:T(8,128)(2,1)}, u32[]{:S(2)}, u32[]{:S(2)}) collective-permute-start(bf16[512,1024]{1,0:T(8,128)(2,1)S(1)} %multiply_convert_fusion.2), channel_id=1, source_target_pairs={{0,16},{16,0},{1,17},{17,1},{2,18},{18,2},{3,19},{19,3},{4,20},{20... | collective-permute-start | bytes 3145736 | tf_op jit(solution)/shard_map/ppermute | solution.py:693
  220.1 6.0 %copy-start.22 = (bf16[512,1024]{1,0:T(8,128)(2,1)S(1)}, bf16[512,1024]{1,0:T(8,128)(2,1)}, u32[]{:S(2)}) copy-start(bf16[512,1024]{1,0:T(8,128)(2,1)} %get-tuple-element.95) | copy-start | bytes 3145732
  246.8 36.1 %collective-permute-start.4 = (bf16[512,2816]{1,0:T(8,128)(2,1)S(1)}, bf16[512,2816]{1,0:T(8,128)(2,1)S(1)}, u32[]{:S(2)}, u32[]{:S(2)}) collective-permute-start(bf16[512,2816]{1,0:T(8,128)(2,1)S(1)} %constant_dynamic-slice_fusion.7), channel_id=1, source_target_pairs={{0,1},{1,0},{2,3},{3,2},{4,5},{5,4},{6,7},{7,6},{8,9},{9,8},{10,11... | collective-permute-start | bytes 8650760 | tf_op jit(solution)/shard_map/ppermute | solution.py:760
  257.2 25.4 %collective-permute-start.3 = (bf16[512,1024]{1,0:T(8,128)(2,1)S(1)}, bf16[512,1024]{1,0:T(8,128)(2,1)S(1)}, u32[]{:S(2)}, u32[]{:S(2)}) collective-permute-start(bf16[512,1024]{1,0:T(8,128)(2,1)S(1)} %slice.225), channel_id=1, source_target_pairs={{0,16},{16,0},{1,17},{17,1},{2,18},{18,2},{3,19},{19,3},{4,20},{20... | collective-permute-start | bytes 3145736 | tf_op jit(solution)/shard_map/ppermute | solution.py:693
  259.0 6.7 %copy-start.34 = (bf16[1024,1408]{1,0:T(8,128)(2,1)S(1)}, bf16[1024,1408]{1,0:T(8,128)(2,1)}, u32[]{:S(2)}) copy-start(bf16[1024,1408]{1,0:T(8,128)(2,1)} %get-tuple-element.92) | copy-start | bytes 8650756
  264.4 6.1 %copy-start.16 = (f32[1024,1024]{1,0:T(8,128)}, f32[1024,1024]{1,0:T(8,128)S(1)}, u32[]{:S(2)}) copy-start(f32[1024,1024]{1,0:T(8,128)S(1)} %fusion.46) | copy-start | bytes 12582916
  265.7 16.9 %copy-start.19 = (f32[1024,1024]{1,0:T(8,128)S(1)}, f32[1024,1024]{1,0:T(8,128)}, u32[]{:S(2)}) copy-start(f32[1024,1024]{1,0:T(8,128)} %copy-done.18) | copy-start | bytes 12582916
  285.1 8.0 %copy-start.6 = (f32[512,1024]{1,0:T(8,128)}, f32[512,1024]{1,0:T(8,128)S(1)}, u32[]{:S(2)}) copy-start(f32[512,1024]{1,0:T(8,128)S(1)} %fusion.12) | copy-start | bytes 6291460
  286.4 33.1 %collective-permute-start.6 = (bf16[256,2816]{1,0:T(8,128)(2,1)}, bf16[256,2816]{1,0:T(8,128)(2,1)S(1)}, u32[]{:S(2)}, u32[]{:S(2)}) collective-permute-start(bf16[256,2816]{1,0:T(8,128)(2,1)} %constant_dynamic-slice_fusion.4), channel_id=1, source_target_pairs={{0,2},{1,3},{2,0},{3,1},{4,6},{5,7},{6,4},{7,5},{8,10},{9,11},{10,... | collective-permute-start | bytes 4325384 | tf_op jit(solution)/shard_map/ppermute | solution.py:760
  291.7 30.6 %collective-permute-start.5 = (bf16[512,1024]{1,0:T(8,128)(2,1)S(1)}, bf16[512,1024]{1,0:T(8,128)(2,1)}, u32[]{:S(2)}, u32[]{:S(2)}) collective-permute-start(bf16[512,1024]{1,0:T(8,128)(2,1)S(1)} %get-tuple-element.93), channel_id=1, source_target_pairs={{0,16},{16,0},{1,17},{17,1},{2,18},{18,2},{3,19},{19,3},{4,20},{20... | collective-permute-start | bytes 3145736 | tf_op jit(solution)/shard_map/ppermute | solution.py:693
  322.3 179.6 %reduce-scatter.3.cloned.1.call-start = ((), (), s32[]{:S(2)}) async-start(), calls=%async_computation.5 | async-start | bytes 6963200 | tf_op jit(solution)/shard_map/reduce_scatter | solution.py:773
  322.5 59.9 %collective-permute-start.10 = (bf16[512,1024]{1,0:T(8,128)(2,1)}, bf16[512,1024]{1,0:T(8,128)(2,1)}, u32[]{:S(2)}, u32[]{:S(2)}) collective-permute-start(bf16[512,1024]{1,0:T(8,128)(2,1)} %slice.224), channel_id=1, source_target_pairs={{0,16},{16,0},{1,17},{17,1},{2,18},{18,2},{3,19},{19,3},{4,20},{20... | collective-permute-start | bytes 3145736 | tf_op jit(solution)/shard_map/ppermute | solution.py:693
  325.3 55.7 %collective-permute-start.7 = (bf16[64,2816]{1,0:T(8,128)(2,1)S(1)}, bf16[64,2816]{1,0:T(8,128)(2,1)S(1)}, u32[]{:S(2)}, u32[]{:S(2)}) collective-permute-start(bf16[64,2816]{1,0:T(8,128)(2,1)S(1)} %get-tuple-element.99), channel_id=1, source_target_pairs={{0,12},{1,13},{2,14},{3,15},{4,0},{5,1},{6,2},{7,3},{8,4},{9,5},{1... | collective-permute-start | bytes 1081352 | tf_op jit(solution)/shard_map/ppermute | solution.py:765
  327.3 53.7 %collective-permute-start.9 = (bf16[64,2816]{1,0:T(8,128)(2,1)S(1)}, bf16[64,2816]{1,0:T(8,128)(2,1)S(1)}, u32[]{:S(2)}, u32[]{:S(2)}) collective-permute-start(bf16[64,2816]{1,0:T(8,128)(2,1)S(1)} %get-tuple-element.100), channel_id=1, source_target_pairs={{0,4},{1,5},{2,6},{3,7},{4,8},{5,9},{6,10},{7,11},{8,12},{9,13},{1... | collective-permute-start | bytes 1081352 | tf_op jit(solution)/shard_map/ppermute | solution.py:765
  327.4 53.6 %collective-permute-start.8 = (bf16[64,2816]{1,0:T(8,128)(2,1)S(1)}, bf16[64,2816]{1,0:T(8,128)(2,1)}, u32[]{:S(2)}, u32[]{:S(2)}) collective-permute-start(bf16[64,2816]{1,0:T(8,128)(2,1)S(1)} %get-tuple-element.101), channel_id=1, source_target_pairs={{0,8},{1,9},{2,10},{3,11},{4,12},{5,13},{6,14},{7,15},{8,0},{9,1},... | collective-permute-start | bytes 1081352 | tf_op jit(solution)/shard_map/ppermute | solution.py:765
  329.3 53.0 %copy-start.17 = (f32[1024,1024]{1,0:T(8,128)S(1)}, f32[1024,1024]{1,0:T(8,128)}, u32[]{:S(2)}) copy-start(f32[1024,1024]{1,0:T(8,128)} %copy-done.16) | copy-start | bytes 12582916
  415.3 1.2 collective-permute-start.12
  416.6 4.1 collective-permute-start.13
  420.7 4.4 collective-permute-start.14
  423.1 43.3 %collective-permute-start.11 = (bf16[512,1024]{1,0:T(8,128)(2,1)}, bf16[512,1024]{1,0:T(8,128)(2,1)}, u32[]{:S(2)}, u32[]{:S(2)}) collective-permute-start(bf16[512,1024]{1,0:T(8,128)(2,1)} %dynamic-slice_convert_fusion), channel_id=1, source_target_pairs={{0,16},{16,0},{1,17},{17,1},{2,18},{18,2},{3,19},{19,3},{4,20},{20... | collective-permute-start | bytes 3145736 | tf_op jit(solution)/shard_map/ppermute | solution.py:693
  425.1 5.0 collective-permute-start.15
  426.9 35.4 %collective-permute-start.19 = (bf16[64,16,88]{2,1,0:T(8,128)(2,1)S(1)}, bf16[64,16,88]{2,1,0:T(8,128)(2,1)S(1)}, u32[]{:S(2)}, u32[]{:S(2)}) collective-permute-start(bf16[64,16,88]{2,1,0:T(8,128)(2,1)S(1)} %reshape.239), channel_id=1, source_target_pairs={{0,16},{16,0},{1,17},{17,1},{2,18},{18,2},{3,19},{19,3},{4,20},{20... | collective-permute-start | bytes 540680 | tf_op jit(solution)/shard_map/ppermute | solution.py:693
  427.3 33.1 %collective-permute-start.20 = (bf16[64,16,88]{2,1,0:T(8,128)(2,1)S(1)}, bf16[64,16,88]{2,1,0:T(8,128)(2,1)S(1)}, u32[]{:S(2)}, u32[]{:S(2)}) collective-permute-start(bf16[64,16,88]{2,1,0:T(8,128)(2,1)S(1)} %reshape.240), channel_id=1, source_target_pairs={{0,16},{16,0},{1,17},{17,1},{2,18},{18,2},{3,19},{19,3},{4,20},{20... | collective-permute-start | bytes 540680 | tf_op jit(solution)/shard_map/ppermute | solution.py:693
  430.2 28.3 %collective-permute-start.16 = (f32[2304]{0:T(1024)S(1)}, f32[2304]{0:T(1024)S(1)}, u32[]{:S(2)}, u32[]{:S(2)}) collective-permute-start(f32[2304]{0:T(1024)S(1)} %slice.180), channel_id=1, source_target_pairs={{0,16},{16,0},{1,17},{17,1},{2,18},{18,2},{3,19},{19,3},{4,20},{20... | collective-permute-start | bytes 27656 | tf_op jit(solution)/shard_map/ppermute | solution.py:693
  463.6 5.9 %copy-start.7 = (f32[512,1024]{1,0:T(8,128)S(1)}, f32[512,1024]{1,0:T(8,128)}, u32[]{:S(2)}) copy-start(f32[512,1024]{1,0:T(8,128)} %copy-done.6) | copy-start | bytes 6291460
  469.2 35.0 %collective-permute-start.18 = (bf16[1,216,1024]{2,1,0:T(8,128)(2,1)}, bf16[1,216,1024]{2,1,0:T(8,128)(2,1)}, u32[]{:S(2)}, u32[]{:S(2)}) collective-permute-start(bf16[1,216,1024]{2,1,0:T(8,128)(2,1)} %bitcast.89), channel_id=1, source_target_pairs={{0,16},{16,0},{1,17},{17,1},{2,18},{18,2},{3,19},{19,3},{4,20},{20... | collective-permute-start | bytes 1327112 | tf_op jit(solution)/shard_map/ppermute | solution.py:693
  501.9 11.0 %collective-permute-start.17 = (bf16[64,3200]{1,0:T(8,128)(2,1)}, bf16[64,3200]{1,0:T(8,128)(2,1)S(1)}, u32[]{:S(2)}, u32[]{:S(2)}) collective-permute-start(bf16[64,3200]{1,0:T(8,128)(2,1)} %reduce-scatter.3.cloned.1.call-done.own_ref), channel_id=1, source_target_pairs={{0,16},{16,0},{1,17},{17,1},{2,18},{18,2},{3,19},{19,3},{4,20},{20... | collective-permute-start | bytes 1228808 | tf_op jit(solution)/shard_map/ppermute | solution.py:693
  504.2 10.7 %copy-start.1 = (bf16[176,1024]{1,0:T(8,128)(2,1)S(1)}, bf16[176,1024]{1,0:T(8,128)(2,1)}, u32[]{:S(2)}) copy-start(bf16[176,1024]{1,0:T(8,128)(2,1)} %param.32) | copy-start | bytes 1081348
  504.2 9.4 %copy-start.2 = (bf16[64,3200]{1,0:T(8,128)(2,1)S(1)}, bf16[64,3200]{1,0:T(8,128)(2,1)}, u32[]{:S(2)}) copy-start(bf16[64,3200]{1,0:T(8,128)(2,1)} %reduce-scatter.3.cloned.1.call-done.own_ref) | copy-start | bytes 1228804
  (17 other events, 37.2 us)
Sparse Core Ops, SparseCore 0:
  13.6 66.0 all-gather.3
  82.6 65.1 all-gather.5
  150.7 57.5 all-gather.7
  322.5 88.6 reduce-scatter.4
  415.4 86.4 reduce-scatter.2

commit v2 on v1

--- a/solution.py
+++ b/solution.py
@@ -965,6 +965,7 @@
     middle = inputs + forward_dot(gated_low, out_full)
     second_norm, second_pull = jax.vjp(rms_norm, middle, second_gain)
     hidden = own_first(second_norm.astype(bf16))
+    turned, ffn_full = lax.optimization_barrier((core_major(hidden), ffn_full))
     both_ffn = forward_dot(hidden, ffn_full)
     activated, swiglu_pull = jax.vjp(swiglu, both_ffn[:, :half], both_ffn[:, half:])
     activated_low = activated.astype(bf16)
@@ -973,7 +974,7 @@
     hidden_grad = sum_own_first(times_transposed(both_grad, ffn_full))
     out_parts = forward_dot(activated_low, down_full)
     down_grad = transposed_times(activated_low, all_cotangent).astype(bf16)
-    ffn_grad = transposed_times(core_major(after(hidden, both_ffn)), both_grad).astype(bf16)
+    ffn_grad = transposed_times(turned, both_grad).astype(bf16)
     ffn_grad = first_sum(ffn_grad)
     out_sent = out_parts[token_count:].astype(bf16)
     hidden_grad, ffn_grad, down_grad, out_parts, out_sent = lax.optimization_barrier(

time: 528 us -> 520 us (0.985)
  waiting for transfers between devices: 200 us -> 192 us
    all_gather x3, waiting for transfers between devices: 30.5 us -> 23.2 us  [gather_shard(): return lax.all_gather(values, 'shard', axis=0, tiled=True)]
  transfers between devices with their start and end apart: 26 -> 26, of which waited for: 15 -> 15; matrix products, arithmetic and copies ran while one was open for 27% -> 29% of each run, Pallas kernels for 17% -> 17%
where the time goes in v2:
time: 520 us; the launch traced here: 514 us
  waiting for transfers between devices  192 us (37%)
  matrix products  102 us (20%)
  Pallas kernels  88.3 us (17%)
  local copies, waits for them, and re-layouts  52.6 us (10%)
  other arithmetic  40.4 us (8%)
  starting transfers between devices  23.7 us (5%)
  between operations  15 us (3%)
    ppermute x12, waiting for transfers between devices, swap_seq(): return lax.ppermute(values, 'seq', [(0, 1), (1, 0)])  115 us
    dot_general x8, matrix products, dot(): lax.dot_general(a, b, (((ca,), (cb,)), ((), ())), preferred_element_type=...  64.7 us
    pallas_call x1, Pallas kernels, mixer_backward(): pl.pallas_call(functools.partial(backward_kernel, heads), grid=(steps,),...  51.6 us
    dot_general x6, matrix products, forward_dot(): return jnp.dot(left_side, right_side, preferred_element_type=f32)  37.6 us
    pallas_call x1, Pallas kernels, mixer_forward(): pl.pallas_call(functools.partial(forward_kernel, heads), grid=(steps,), i...  35.4 us
    reduce_scatter x2, waiting for transfers between devices, scatter_shard(): return lax.psum_scatter(values, 'shard', scatter_dimension=0, tiled=True)  29.7 us
    ppermute x6, waiting for transfers between devices, flip(): return lax.ppermute(values, 'shard', [(i, i ^ mask) for i in range(size)])  23.8 us
    all_gather x3, waiting for transfers between devices, gather_shard(): return lax.all_gather(values, 'shard', axis=0, tiled=True)  23.2 us
  transfers between devices with their start and end apart: 26, of which 15 were waited for; matrix products, arithmetic and copies ran while one was open for 29% of the time, Pallas kernels for 17%

profile of v2, /device:TPU:0, one launch (start us, length us, event | category | flops | bytes accessed | tf_op | source)
XLA Modules:
  0.0 514.3 jit_solution(662747125247128710)
XLA Ops:
  13.5 1.8 pad_maximum_fusion.10
  16.9 2.9 collective-permute-start
  23.6 42.2 %collective-permute-done = bf16[1024,1024]{1,0:T(8,128)(2,1)} collective-permute-done((bf16[1024,1024]{1,0:T(8,128)(2,1)}, bf16[1024,1024]{1,0:T(8,128)(2,1)}, u32[]{:S(2)}, u32[]{:S(2)}) %collective-permute-start) | collective-permute-done | bytes 2097184 | tf_op jit(solution)/shard_map/ppermute | solution.py:693
  65.8 2.7 fusion.42
  69.3 10.4 %all-gather.4.cloned.1.call-done = bf16[1024,3200]{1,0:T(8,128)(2,1)} async-done(((bf16[64,3200]{1,0:T(8,128)(2,1)}), bf16[1024,3200]{1,0:T(8,128)(2,1)}) %all-gather.4.cloned.1.call-update) | async-done | bytes 6553616 | tf_op jit(solution)/shard_map/all_gather | solution.py:769
  83.2 6.1 %fusion.17.gate_ref = f32[1024,1024]{1,0:T(8,128)} fusion(bf16[1024,3200]{1,0:T(8,128)(2,1)} %all-gather.4.cloned.1.call-done, f32[1024]{0:T(1024)S(1)} %get-tuple-element.87, f32[1024]{0:T(1024)S(1)} %add_rsqrt_fusion, bf16[512,1024]{1,0:T(8,128)(2,1)S(1)} %bitcast.69, bf16[512,1024]{1,0:T(8,128)(2,1)S(1)} %get-tuple-element.98, pred[]{:T(512)S(6)} %eq.14), kind=kOutput, calls=%fused_computation.44 | convolution fusion | flops 2161115136 | bytes 8396801 | tf_op jit(solution)/shard_map/dot_general | solution.py:673
  89.3 5.7 %fusion.21.value_ref = bf16[1024,1024]{1,0:T(8,128)(2,1)} fusion(bf16[1024,3200]{1,0:T(8,128)(2,1)S(1)} %bitcast.94, f32[1024]{0:T(1024)S(1)} %get-tuple-element.87, f32[1024]{0:T(1024)S(1)} %add_rsqrt_fusion, bf16[512,1024]{1,0:T(8,128)(2,1)S(1)} %bitcast.70, bf16[512,1024]{1,0:T(8,128)(2,1)S(1)} %get-tuple-element.98, pred[]{:T(512)S(6)} %eq.14), kind=kOutput, calls=%fused_computation.58 | convolution fusion | flops 2162163712 | bytes 6299649 | tf_op jit(solution)/shard_map/dot_general | solution.py:673
  95.0 6.0 %convolution_convert_fusion.3.raw_ref = bf16[1024,1152]{1,0:T(8,128)(2,1)} fusion(bf16[1024,3200]{1,0:T(8,128)(2,1)S(1)} %bitcast.94, f32[1024]{0:T(1024)S(1)} %get-tuple-element.87, f32[1024]{0:T(1024)S(1)} %add_rsqrt_fusion, bf16[512,1024]{1,0:T(8,128)(2,1)S(1)} %bitcast.71, bf16[512,1024]{1,0:T(8,128)(2,1)S(1)} %get-tuple-element.98, pred[]{:T(512)S(6)} %eq.14), kind=kOutput, calls=%fused_computation.21 | convolution fusion | flops 2430730240 | bytes 6823937 | tf_op jit(solution)/shard_map/dot_general | solution.py:673
  101.0 35.4 %mixer_forward.1 = (bf16[1024,1024]{1,0:T(8,128)(2,1)}, bf16[1024,1024]{1,0:T(8,128)(2,1)}, bf16[1024,256]{1,0:T(8,128)(2,1)}, f32[4096,256]{1,0:T(8,128)}, bf16...) custom-call(s32[1,4]{1,0:T(1,128)} %starts_ref.3, bf16[1024,1152]{1,0:T(8,128)(2,1)} %convolution_convert_fusion.3.raw_ref, ...), custom_call_target="tpu_custom_call" | custom-call | flops 45056000000 | bytes 16777216 | tf_op jit(solution)/shard_map/mixer_forward/pallas_call | solution.py:582
  136.4 1.7 constant_dynamic-slice_fusion.12
  139.7 8.1 %all-gather.6.cloned.1.call-done = bf16[3456,1024]{1,0:T(8,128)(2,1)} async-done(((bf16[216,1024]{1,0:T(8,128)(2,1)}), bf16[3456,1024]{1,0:T(8,128)(2,1)}) %all-gather.6.cloned.1.call-update) | async-done | bytes 7077904 | tf_op jit(solution)/shard_map/all_gather | solution.py:769
  147.8 2.6 slice.173
  150.4 5.2 %slice.172 = bf16[16,88,1024]{2,1,0:T(8,128)(2,1)} slice(bf16[16,216,1024]{2,1,0:T(8,128)(2,1)} %bitcast.76), slice={[0:16], [128:216], [0:1024]} | slice | bytes 5767168 | tf_op jit(solution)/shard_map/slice | solution.py:919
  155.6 8.0 %collective-permute-done.1 = bf16[512,1024]{1,0:T(8,128)(2,1)} collective-permute-done((bf16[512,1024]{1,0:T(8,128)(2,1)S(1)}, bf16[512,1024]{1,0:T(8,128)(2,1)}, u32[]{:S(2)}, u32[]{:S(2)}) %collective-permute-start.1) | collective-permute-done | bytes 1048608 | tf_op jit(solution)/shard_map/ppermute | solution.py:693
  163.6 2.3 maximum_select_fusion
  166.0 2.5 multiply_reduce_fusion.2
  170.3 23.1 %collective-permute-done.2 = bf16[512,1024]{1,0:T(8,128)(2,1)} collective-permute-done((bf16[512,1024]{1,0:T(8,128)(2,1)S(1)}, bf16[512,1024]{1,0:T(8,128)(2,1)}, u32[]{:S(2)}, u32[]{:S(2)}) %collective-permute-start.2) | collective-permute-done | bytes 1048608 | tf_op jit(solution)/shard_map/ppermute | solution.py:693
  193.4 2.8 pad_maximum_fusion.7
  196.2 4.1 copy.59
  200.2 3.2 copy.60
  203.4 4.7 all-gather.8.cloned.1.call-done
  208.2 12.0 %fusion.37 = f32[1024,2816]{1,0:T(8,128)} fusion(bf16[1024,2816]{1,0:T(8,128)(2,1)} %all-gather.8.cloned.1.call-done, bf16[512,1024]{1,0:T(8,128)(2,1)} %collective-permute-done.2, bf16[512,1024]{1,0:T(8,128)(2,1)S(1)} %multiply_convert_fusion.2), kind=kOutput, calls=%fused_computation.119 | convolution fusion | flops 5909774336 | bytes 19398656 | tf_op jit(solution)/shard_map/dot_general | solution.py:673
  220.2 10.6 %fusion.2 = (bf16[1024,1408]{1,0:T(8,128)(2,1)S(1)}, bf16[1024,1408]{1,0:T(8,128)(2,1)S(1)}, bf16[1024,1408]{1,0:T(8,128)(2,1)}) fusion(f32[1024,2816]{1,0:T(8,128)} %fusion.37, bf16[1408,1024]{1,0:T(8,128)(2,1)S(1)} %bitcast.84, bf16[512,1024]{1,0:T(8,128)(2,1)S(1)} %copy-done.23, bf16[512,1024]{1,0:T(8,128)(2,1)S(1)} %bitcast.81), kind=kOutput, calls=%fused_computation.5 | convolution fusion | flops 2980052992 | bytes 25165824 | tf_op jit(solution)/shard_map/dot_general | solution.py:23
  232.4 6.8 %convolution_convert_fusion.1 = bf16[1024,2816]{1,0:T(8,128)(2,1)S(1)} fusion(bf16[1024,1024]{0,1:T(8,128)(2,1)S(1)} %bitcast.86, bf16[1024,1408]{1,0:T(8,128)(2,1)S(1)} %get-tuple-element.93, bf16[1024,1408]{1,0:T(8,128)(2,1)S(1)} %get-tuple-element.92), kind=kOutput, calls=%fused_computation.12 | convolution fusion | flops 5919997952 | bytes 13631488 | tf_op jit(solution)/shard_map/dot_general | solution.py:23
  239.7 9.9 %fusion.9 = f32[1024,1024]{1,0:T(8,128)S(1)} fusion(bf16[1024,2816]{1,0:T(8,128)(2,1)} %all-gather.8.cloned.1.call-done, bf16[1024,1408]{1,0:T(8,128)(2,1)} %copy-done.38, bf16[1024,1408]{1,0:T(8,128)(2,1)} %copy-done.37), kind=kOutput, calls=%fused_computation.23 | convolution fusion | flops 5917114368 | bytes 15728640 | tf_op jit(solution)/shard_map/dot_general | solution.py:23
  251.5 5.4 %fusion.46 = f32[1024,1024]{1,0:T(8,128)S(1)} fusion(bf16[1024,1408]{1,0:T(8,128)(2,1)} %get-tuple-element.94, bf16[1408,1024]{1,0:T(8,128)(2,1)S(1)} %bitcast.85), kind=kOutput, calls=%fused_computation.124 | convolution fusion | flops 2952790016 | bytes 9961472 | tf_op jit(solution)/shard_map/dot_general | solution.py:673
  258.3 4.8 convolution_convert_fusion.4
  263.0 12.1 %collective-permute-done.3 = bf16[512,1024]{1,0:T(8,128)(2,1)S(1)} collective-permute-done((bf16[512,1024]{1,0:T(8,128)(2,1)S(1)}, bf16[512,1024]{1,0:T(8,128)(2,1)S(1)}, u32[]{:S(2)}, u32[]{:S(2)}) %collective-permute-start.3) | collective-permute-done | bytes 1048608 | tf_op jit(solution)/shard_map/ppermute | solution.py:693
  280.6 2.4 convolution_convert_fusion.5
  285.6 4.5 convolution_convert_fusion.2
  290.1 7.0 %pad_maximum_fusion = bf16[16,216,1024]{2,1,0:T(8,128)(2,1)} fusion(bf16[16,88,1024]{2,1,0:T(8,128)(2,1)} %bitcast.83, bf16[16,128,1024]{2,1,0:T(8,128)(2,1)} %bitcast.77), kind=kLoop, calls=%fused_computation.2 | loop fusion | flops 14155776 | bytes 14155776 | tf_op jit(solution)/shard_map/concatenate | solution.py:994
  297.1 14.9 %collective-permute-done.6 = bf16[256,2816]{1,0:T(8,128)(2,1)S(1)} collective-permute-done((bf16[256,2816]{1,0:T(8,128)(2,1)}, bf16[256,2816]{1,0:T(8,128)(2,1)S(1)}, u32[]{:S(2)}, u32[]{:S(2)}) %collective-permute-start.6) | collective-permute-done | bytes 1441824 | tf_op jit(solution)/shard_map/ppermute | solution.py:760
  312.0 2.8 add_convert_fusion.1
  318.8 2.4 collective-permute-start.7
  322.7 51.6 %mixer_backward.1 = (bf16[1024,3200]{1,0:T(8,128)(2,1)}, f32[32,2048]{1,0:T(8,128)}, f32[2,4]{1,0:T(2,128)}, f32[8,256]{1,0:T(8,128)}) custom-call(s32[1,4]{1,0:T(1,128)} %starts_ref.3, s32[1]{0:T(128)} %bitcast.seq_ref, bf16[1024,1152]{1,0:T(8,128)(2,1)} %convolution_convert_fusion.3.raw_ref, bf16[1024,1024]{1,0:T(8,128)(2,1)} %fusion.21.value_ref, ...), custom_call_target="tpu_custom_call" | custom-call | flops 57344000000 | bytes 16777216 | tf_op jit(solution)/shard_map/mixer_backward/pallas_call | solution.py:628
  375.6 2.9 add_convert_fusion.2
  378.6 13.0 %convolution_convert_fusion = bf16[1024,3200]{1,0:T(8,128)(2,1)} fusion(bf16[1024,3200]{1,0:T(8,128)(2,1)} %get-tuple-element.73, f32[1024]{0:T(1024)S(1)} %copy-done.29, f32[1024]{0:T(1024)S(1)} %copy-done.33, bf16[512,1024]{1,0:T(8,128)(2,1)S(1)} %bitcast.72, bf16[512,1024]{1,0:T(8,128)(2,1)S(1)} %copy-done.11, pred[]{:T(512)S(6)} %eq.14), kind=kOutput, calls=%fused_computation.1 | convolution fusion | flops 6727794688 | bytes 15212545 | tf_op jit(solution)/shard_map/dot_general | solution.py:23
  392.9 12.9 %fusion.7 = (f32[1024]{0:T(1024)S(1)}, f32[1024,1024]{1,0:T(8,128)}) fusion(f32[1024]{0:T(1024)S(1)} %copy-done.33, bf16[512,1024]{1,0:T(8,128)(2,1)S(1)} %bitcast.73, bf16[512,1024]{1,0:T(8,128)(2,1)S(1)} %copy-done.12, pred[]{:T(512)S(6)} %eq.14, bf16[1024,3200]{1,0:T(8,128)(2,1)} %get-tuple-element.73, bf16[1024,3200]{1,0:T(8,128)(2,1)} %all-gather.4.cloned.1.call-done), kind=kOutput, calls=%fused_computation.18 | convolution fusion | flops 6724516864 | bytes 19406848 | tf_op jit(solution)/shard_map/dot_general | solution.py:23
  405.9 2.7 dynamic-slice_convert_fusion
  410.5 3.5 collective-permute-done.13
  414.6 3.4 collective-permute-done.14
  425.1 24.7 %collective-permute-done.16 = f32[2304]{0:T(1024)S(1)} collective-permute-done((f32[2304]{0:T(1024)S(1)}, f32[2304]{0:T(1024)S(1)}, u32[]{:S(2)}, u32[]{:S(2)}) %collective-permute-start.16) | collective-permute-done | bytes 9248 | tf_op jit(solution)/shard_map/ppermute | solution.py:693
  454.9 2.8 reshape.248
  457.7 2.6 fusion.15
  460.9 3.9 fusion.14
  464.8 29.7 %reduce-scatter.3.cloned.1.call-done.own_ref = bf16[64,3200]{1,0:T(8,128)(2,1)} async-done(((bf16[1024,3200]{1,0:T(8,128)(2,1)}), bf16[64,3200]{1,0:T(8,128)(2,1)}) %reduce-scatter.3.cloned.1.call-update) | async-done | bytes 409616 | tf_op jit(solution)/shard_map/reduce_scatter | solution.py:773
  496.8 1.6 fusion.25
  500.2 5.2 %collective-permute-done.17.other_ref = bf16[64,3200]{1,0:T(8,128)(2,1)S(1)} collective-permute-done((bf16[64,3200]{1,0:T(8,128)(2,1)}, bf16[64,3200]{1,0:T(8,128)(2,1)S(1)}, u32[]{:S(2)}, u32[]{:S(2)}) %collective-permute-start.17) | collective-permute-done | bytes 409632 | tf_op jit(solution)/shard_map/ppermute | solution.py:693
  (213 shorter events, 62.0 us)
Async XLA Ops:
  7.2 8.2 %copy-start.3 = (bf16[1,512,1024]{2,1,0:T(8,128)(2,1)S(1)}, bf16[1,512,1024]{2,1,0:T(8,128)(2,1)}, u32[]{:S(2)}) copy-start(bf16[1,512,1024]{2,1,0:T(8,128)(2,1)} %param.17) | copy-start | bytes 3145732
  7.2 8.2 %copy-start.13 = (bf16[1,512,1024]{2,1,0:T(8,128)(2,1)S(1)}, bf16[1,512,1024]{2,1,0:T(8,128)(2,1)}, u32[]{:S(2)}) copy-start(bf16[1,512,1024]{2,1,0:T(8,128)(2,1)} %param.33) | copy-start | bytes 3145732
  7.2 72.5 %all-gather.4.cloned.1.call-start = ((), (), s32[]{:S(2)}) async-start(), calls=%async_computation.2 | async-start | bytes 6963200 | tf_op jit(solution)/shard_map/all_gather | solution.py:769
  13.4 134.3 %all-gather.6.cloned.1.call-start = ((), (), s32[]{:S(2)}) async-start(), calls=%async_computation.3 | async-start | bytes 7520256 | tf_op jit(solution)/shard_map/all_gather | solution.py:769
  13.5 6.4 %copy-start.25 = (bf16[64,2816]{1,0:T(8,128)(2,1)S(1)}, bf16[64,2816]{1,0:T(8,128)(2,1)}, u32[]{:S(2)}) copy-start(bf16[64,2816]{1,0:T(8,128)(2,1)} %param.31) | copy-start | bytes 1081348
  15.4 192.8 %all-gather.8.cloned.1.call-start = ((), (), s32[]{:S(2)}) async-start(), calls=%async_computation.4 | async-start | bytes 6127616 | tf_op jit(solution)/shard_map/all_gather | solution.py:769
  16.9 6.6 %copy-start.30 = (f32[4,4,512]{2,1,0:T(4,128)S(1)}, f32[4,4,512]{2,1,0:T(4,128)}, u32[]{:S(2)}) copy-start(f32[4,4,512]{2,1,0:T(4,128)} %param.25) | copy-start | bytes 98308
  16.9 48.9 %collective-permute-start = (bf16[1024,1024]{1,0:T(8,128)(2,1)}, bf16[1024,1024]{1,0:T(8,128)(2,1)}, u32[]{:S(2)}, u32[]{:S(2)}) collective-permute-start(bf16[1024,1024]{1,0:T(8,128)(2,1)} %pad_maximum_fusion.4), channel_id=1, source_target_pairs={{0,16},{16,0},{1,17},{17,1},{2,18},{18,2},{3,19},{19,3},{4,20},{20... | collective-permute-start | bytes 6291464 | tf_op jit(solution)/shard_map/ppermute | solution.py:693
  23.4 436.9 %reduce-scatter.5.cloned.1.call-start = ((), (), s32[]{:S(2)}) async-start(), calls=%async_computation.6 | async-start | bytes 7520256 | tf_op jit(solution)/shard_map/reduce_scatter | solution.py:773
  23.6 45.7 %copy-start.34 = (f32[4,2048]{1,0:T(4,128)}, f32[4,2048]{1,0:T(4,128)S(1)}, u32[]{:S(2)}) copy-start(f32[4,2048]{1,0:T(4,128)S(1)} %constant_dynamic-update-slice_fusion.filters_ref) | copy-start | bytes 98308
  68.5 26.5 %copy-start.10 = (bf16[512,1024]{1,0:T(8,128)(2,1)}, bf16[512,1024]{1,0:T(8,128)(2,1)S(1)}, u32[]{:S(2)}) copy-start(bf16[512,1024]{1,0:T(8,128)(2,1)S(1)} %get-tuple-element.98) | copy-start | bytes 3145732
  69.3 25.7 %copy-start.32 = (f32[1024]{0:T(1024)}, f32[1024]{0:T(1024)S(1)}, u32[]{:S(2)}) copy-start(f32[1024]{0:T(1024)S(1)} %add_rsqrt_fusion) | copy-start | bytes 12292
  81.6 7.7 %slice-start = ((s8[6553600]{0:T(1024)(128)(4,1)}), s8[4194304]{0:T(1024)(128)(4,1)S(1)}, s32[]{:S(2)}) async-start(s8[6553600]{0:T(1024)(128)(4,1)} %bitcast.93), calls=%async_computation.7 | async-start | bytes 8388608
  83.2 11.8 %copy-start.28 = (f32[1024]{0:T(1024)}, f32[1024]{0:T(1024)S(1)}, u32[]{:S(2)}) copy-start(f32[1024]{0:T(1024)S(1)} %get-tuple-element.87) | copy-start | bytes 12292
  138.2 25.5 %collective-permute-start.1 = (bf16[512,1024]{1,0:T(8,128)(2,1)S(1)}, bf16[512,1024]{1,0:T(8,128)(2,1)}, u32[]{:S(2)}, u32[]{:S(2)}) collective-permute-start(bf16[512,1024]{1,0:T(8,128)(2,1)S(1)} %get-tuple-element.100), channel_id=1, source_target_pairs={{0,16},{16,0},{1,17},{17,1},{2,18},{18,2},{3,19},{19,3},{4,20},{20... | collective-permute-start | bytes 3145736 | tf_op jit(solution)/shard_map/ppermute | solution.py:693
  150.4 15.6 %copy-start.8 = (bf16[16,128,1024]{2,1,0:T(8,128)(2,1)}, bf16[16,128,1024]{2,1,0:T(8,128)(2,1)S(1)}, u32[]{:S(2)}) copy-start(bf16[16,128,1024]{2,1,0:T(8,128)(2,1)S(1)} %slice.173) | copy-start | bytes 12582916
  168.8 24.7 %collective-permute-start.2 = (bf16[512,1024]{1,0:T(8,128)(2,1)S(1)}, bf16[512,1024]{1,0:T(8,128)(2,1)}, u32[]{:S(2)}, u32[]{:S(2)}) collective-permute-start(bf16[512,1024]{1,0:T(8,128)(2,1)S(1)} %multiply_convert_fusion.2), channel_id=1, source_target_pairs={{0,16},{16,0},{1,17},{17,1},{2,18},{18,2},{3,19},{19,3},{4,20},{20... | collective-permute-start | bytes 3145736 | tf_op jit(solution)/shard_map/ppermute | solution.py:693
  208.2 12.0 %copy-start.14 = (bf16[1,512,1024]{2,1,0:T(8,128)(2,1)S(1)}, bf16[1,512,1024]{2,1,0:T(8,128)(2,1)}, u32[]{:S(2)}) copy-start(bf16[1,512,1024]{2,1,0:T(8,128)(2,1)} %param.33) | copy-start | bytes 3145732
  208.2 12.0 %copy-start.15 = (bf16[16,88,1024]{2,1,0:T(8,128)(2,1)S(1)}, bf16[16,88,1024]{2,1,0:T(8,128)(2,1)}, u32[]{:S(2)}) copy-start(bf16[16,88,1024]{2,1,0:T(8,128)(2,1)} %slice.172) | copy-start | bytes 8650756
  208.2 12.0 %copy-start.23 = (bf16[512,1024]{1,0:T(8,128)(2,1)S(1)}, bf16[512,1024]{1,0:T(8,128)(2,1)}, u32[]{:S(2)}) copy-start(bf16[512,1024]{1,0:T(8,128)(2,1)} %get-tuple-element.97) | copy-start | bytes 3145732
  220.2 12.2 %copy-start.22 = (bf16[1024,2,2,4,64]{0,4,3,2,1:T(8,128)(2,1)S(1)}, bf16[1024,2,2,4,64]{0,4,3,2,1:T(8,128)(2,1)}, u32[]{:S(2)}) copy-start(bf16[1024,2,2,4,64]{0,4,3,2,1:T(8,128)(2,1)} %copy.60) | copy-start | bytes 6291460
  230.8 8.3 %copy-start.38 = (bf16[1024,1408]{1,0:T(8,128)(2,1)}, bf16[1024,1408]{1,0:T(8,128)(2,1)S(1)}, u32[]{:S(2)}) copy-start(bf16[1024,1408]{1,0:T(8,128)(2,1)S(1)} %get-tuple-element.93) | copy-start | bytes 8650756
  239.3 36.1 %collective-permute-start.4 = (bf16[512,2816]{1,0:T(8,128)(2,1)S(1)}, bf16[512,2816]{1,0:T(8,128)(2,1)S(1)}, u32[]{:S(2)}, u32[]{:S(2)}) collective-permute-start(bf16[512,2816]{1,0:T(8,128)(2,1)S(1)} %constant_dynamic-slice_fusion.7), channel_id=1, source_target_pairs={{0,1},{1,0},{2,3},{3,2},{4,5},{5,4},{6,7},{7,6},{8,9},{9,8},{10,11... | collective-permute-start | bytes 8650760 | tf_op jit(solution)/shard_map/ppermute | solution.py:760
  249.7 25.4 %collective-permute-start.3 = (bf16[512,1024]{1,0:T(8,128)(2,1)S(1)}, bf16[512,1024]{1,0:T(8,128)(2,1)S(1)}, u32[]{:S(2)}, u32[]{:S(2)}) collective-permute-start(bf16[512,1024]{1,0:T(8,128)(2,1)S(1)} %slice.225), channel_id=1, source_target_pairs={{0,16},{16,0},{1,17},{17,1},{2,18},{18,2},{3,19},{19,3},{4,20},{20... | collective-permute-start | bytes 3145736 | tf_op jit(solution)/shard_map/ppermute | solution.py:693
  251.5 6.8 %copy-start.24 = (bf16[512,1024]{1,0:T(8,128)(2,1)S(1)}, bf16[512,1024]{1,0:T(8,128)(2,1)}, u32[]{:S(2)}) copy-start(bf16[512,1024]{1,0:T(8,128)(2,1)} %get-tuple-element.97) | copy-start | bytes 3145732
  251.5 6.8 %copy-start.36 = (bf16[1024,1408]{1,0:T(8,128)(2,1)S(1)}, bf16[1024,1408]{1,0:T(8,128)(2,1)}, u32[]{:S(2)}) copy-start(bf16[1024,1408]{1,0:T(8,128)(2,1)} %get-tuple-element.94) | copy-start | bytes 8650756
  258.3 16.8 %copy-start.19 = (f32[1024,1024]{1,0:T(8,128)S(1)}, f32[1024,1024]{1,0:T(8,128)}, u32[]{:S(2)}) copy-start(f32[1024,1024]{1,0:T(8,128)} %copy-done.18) | copy-start | bytes 12582916
  277.6 8.0 %copy-start.6 = (f32[512,1024]{1,0:T(8,128)}, f32[512,1024]{1,0:T(8,128)S(1)}, u32[]{:S(2)}) copy-start(f32[512,1024]{1,0:T(8,128)S(1)} %fusion.12) | copy-start | bytes 6291460
  278.9 33.1 %collective-permute-start.6 = (bf16[256,2816]{1,0:T(8,128)(2,1)}, bf16[256,2816]{1,0:T(8,128)(2,1)S(1)}, u32[]{:S(2)}, u32[]{:S(2)}) collective-permute-start(bf16[256,2816]{1,0:T(8,128)(2,1)} %constant_dynamic-slice_fusion.4), channel_id=1, source_target_pairs={{0,2},{1,3},{2,0},{3,1},{4,6},{5,7},{6,4},{7,5},{8,10},{9,11},{10,... | collective-permute-start | bytes 4325384 | tf_op jit(solution)/shard_map/ppermute | solution.py:760
  284.1 30.7 %collective-permute-start.5 = (bf16[512,1024]{1,0:T(8,128)(2,1)S(1)}, bf16[512,1024]{1,0:T(8,128)(2,1)}, u32[]{:S(2)}, u32[]{:S(2)}) collective-permute-start(bf16[512,1024]{1,0:T(8,128)(2,1)S(1)} %get-tuple-element.95), channel_id=1, source_target_pairs={{0,16},{16,0},{1,17},{17,1},{2,18},{18,2},{3,19},{19,3},{4,20},{20... | collective-permute-start | bytes 3145736 | tf_op jit(solution)/shard_map/ppermute | solution.py:693
  314.9 179.6 %reduce-scatter.3.cloned.1.call-start = ((), (), s32[]{:S(2)}) async-start(), calls=%async_computation.5 | async-start | bytes 6963200 | tf_op jit(solution)/shard_map/reduce_scatter | solution.py:773
  316.3 58.0 %collective-permute-start.9 = (bf16[64,2816]{1,0:T(8,128)(2,1)S(1)}, bf16[64,2816]{1,0:T(8,128)(2,1)S(1)}, u32[]{:S(2)}, u32[]{:S(2)}) collective-permute-start(bf16[64,2816]{1,0:T(8,128)(2,1)S(1)} %get-tuple-element.102), channel_id=1, source_target_pairs={{0,4},{1,5},{2,6},{3,7},{4,8},{5,9},{6,10},{7,11},{8,12},{9,13},{1... | collective-permute-start | bytes 1081352 | tf_op jit(solution)/shard_map/ppermute | solution.py:765
  317.9 56.4 %collective-permute-start.8 = (bf16[64,2816]{1,0:T(8,128)(2,1)S(1)}, bf16[64,2816]{1,0:T(8,128)(2,1)S(1)}, u32[]{:S(2)}, u32[]{:S(2)}) collective-permute-start(bf16[64,2816]{1,0:T(8,128)(2,1)S(1)} %get-tuple-element.103), channel_id=1, source_target_pairs={{0,8},{1,9},{2,10},{3,11},{4,12},{5,13},{6,14},{7,15},{8,0},{9,1},... | collective-permute-start | bytes 1081352 | tf_op jit(solution)/shard_map/ppermute | solution.py:765
  318.8 55.5 %collective-permute-start.7 = (bf16[64,2816]{1,0:T(8,128)(2,1)S(1)}, bf16[64,2816]{1,0:T(8,128)(2,1)}, u32[]{:S(2)}, u32[]{:S(2)}) collective-permute-start(bf16[64,2816]{1,0:T(8,128)(2,1)S(1)} %get-tuple-element.101), channel_id=1, source_target_pairs={{0,12},{1,13},{2,14},{3,15},{4,0},{5,1},{6,2},{7,3},{8,4},{9,5},{1... | collective-permute-start | bytes 1081352 | tf_op jit(solution)/shard_map/ppermute | solution.py:765
  321.2 54.4 %collective-permute-start.10 = (bf16[512,1024]{1,0:T(8,128)(2,1)}, bf16[512,1024]{1,0:T(8,128)(2,1)}, u32[]{:S(2)}, u32[]{:S(2)}) collective-permute-start(bf16[512,1024]{1,0:T(8,128)(2,1)} %slice.224), channel_id=1, source_target_pairs={{0,16},{16,0},{1,17},{17,1},{2,18},{18,2},{3,19},{19,3},{4,20},{20... | collective-permute-start | bytes 3145736 | tf_op jit(solution)/shard_map/ppermute | solution.py:693
  322.6 53.0 %copy-start.17 = (f32[1024,1024]{1,0:T(8,128)S(1)}, f32[1024,1024]{1,0:T(8,128)}, u32[]{:S(2)}) copy-start(f32[1024,1024]{1,0:T(8,128)} %copy-done.16) | copy-start | bytes 12582916
  408.6 1.2 collective-permute-start.12
  409.8 4.1 collective-permute-start.13
  413.9 4.1 collective-permute-start.14
  414.0 43.7 %collective-permute-start.11 = (bf16[512,1024]{1,0:T(8,128)(2,1)}, bf16[512,1024]{1,0:T(8,128)(2,1)}, u32[]{:S(2)}, u32[]{:S(2)}) collective-permute-start(bf16[512,1024]{1,0:T(8,128)(2,1)} %dynamic-slice_convert_fusion), channel_id=1, source_target_pairs={{0,16},{16,0},{1,17},{17,1},{2,18},{18,2},{3,19},{19,3},{4,20},{20... | collective-permute-start | bytes 3145736 | tf_op jit(solution)/shard_map/ppermute | solution.py:693
  418.1 5.0 collective-permute-start.15
  419.7 32.0 %collective-permute-start.19 = (bf16[64,16,88]{2,1,0:T(8,128)(2,1)S(1)}, bf16[64,16,88]{2,1,0:T(8,128)(2,1)S(1)}, u32[]{:S(2)}, u32[]{:S(2)}) collective-permute-start(bf16[64,16,88]{2,1,0:T(8,128)(2,1)S(1)} %reshape.239), channel_id=1, source_target_pairs={{0,16},{16,0},{1,17},{17,1},{2,18},{18,2},{3,19},{19,3},{4,20},{20... | collective-permute-start | bytes 540680 | tf_op jit(solution)/shard_map/ppermute | solution.py:693
  420.8 32.7 %collective-permute-start.20 = (bf16[64,16,88]{2,1,0:T(8,128)(2,1)S(1)}, bf16[64,16,88]{2,1,0:T(8,128)(2,1)S(1)}, u32[]{:S(2)}, u32[]{:S(2)}) collective-permute-start(bf16[64,16,88]{2,1,0:T(8,128)(2,1)S(1)} %reshape.240), channel_id=1, source_target_pairs={{0,16},{16,0},{1,17},{17,1},{2,18},{18,2},{3,19},{19,3},{4,20},{20... | collective-permute-start | bytes 540680 | tf_op jit(solution)/shard_map/ppermute | solution.py:693
  423.2 26.7 %collective-permute-start.16 = (f32[2304]{0:T(1024)S(1)}, f32[2304]{0:T(1024)S(1)}, u32[]{:S(2)}, u32[]{:S(2)}) collective-permute-start(f32[2304]{0:T(1024)S(1)} %slice.180), channel_id=1, source_target_pairs={{0,16},{16,0},{1,17},{17,1},{2,18},{18,2},{3,19},{19,3},{4,20},{20... | collective-permute-start | bytes 27656 | tf_op jit(solution)/shard_map/ppermute | solution.py:693
  460.3 36.5 %collective-permute-start.18 = (bf16[1,216,1024]{2,1,0:T(8,128)(2,1)}, bf16[1,216,1024]{2,1,0:T(8,128)(2,1)}, u32[]{:S(2)}, u32[]{:S(2)}) collective-permute-start(bf16[1,216,1024]{2,1,0:T(8,128)(2,1)} %bitcast.89), channel_id=1, source_target_pairs={{0,16},{16,0},{1,17},{17,1},{2,18},{18,2},{3,19},{19,3},{4,20},{20... | collective-permute-start | bytes 1327112 | tf_op jit(solution)/shard_map/ppermute | solution.py:693
  494.5 10.9 %collective-permute-start.17 = (bf16[64,3200]{1,0:T(8,128)(2,1)}, bf16[64,3200]{1,0:T(8,128)(2,1)S(1)}, u32[]{:S(2)}, u32[]{:S(2)}) collective-permute-start(bf16[64,3200]{1,0:T(8,128)(2,1)} %reduce-scatter.3.cloned.1.call-done.own_ref), channel_id=1, source_target_pairs={{0,16},{16,0},{1,17},{17,1},{2,18},{18,2},{3,19},{19,3},{4,20},{20... | collective-permute-start | bytes 1228808 | tf_op jit(solution)/shard_map/ppermute | solution.py:693
  496.7 10.7 %copy-start.1 = (bf16[176,1024]{1,0:T(8,128)(2,1)S(1)}, bf16[176,1024]{1,0:T(8,128)(2,1)}, u32[]{:S(2)}) copy-start(bf16[176,1024]{1,0:T(8,128)(2,1)} %param.32) | copy-start | bytes 1081348
  496.8 9.4 %copy-start.2 = (bf16[64,3200]{1,0:T(8,128)(2,1)S(1)}, bf16[64,3200]{1,0:T(8,128)(2,1)}, u32[]{:S(2)}) copy-start(bf16[64,3200]{1,0:T(8,128)(2,1)} %reduce-scatter.3.cloned.1.call-done.own_ref) | copy-start | bytes 1228804
  (19 other events, 60.6 us)
Sparse Core Ops, SparseCore 0:
  13.6 66.0 all-gather.3
  82.5 65.1 all-gather.5
  150.6 57.4 all-gather.7
  315.0 88.6 reduce-scatter.4
  408.0 86.4 reduce-scatter.2

commit v3 on v2

--- a/solution.py
+++ b/solution.py
@@ -977,8 +977,9 @@
     ffn_grad = transposed_times(turned, both_grad).astype(bf16)
     ffn_grad = first_sum(ffn_grad)
     out_sent = out_parts[token_count:].astype(bf16)
-    hidden_grad, ffn_grad, down_grad, out_parts, out_sent = lax.optimization_barrier(
-        (hidden_grad, ffn_grad, down_grad, out_parts, out_sent)
+    tall_grad = jnp.pad(down_grad.reshape(shards, units, model), ((0, 0), (out_rows, 0), (0, 0)))
+    hidden_grad, ffn_grad, tall_grad, out_parts, out_sent = lax.optimization_barrier(
+        (hidden_grad, ffn_grad, tall_grad, out_parts, out_sent)
     )
     middle_part, ffn_gain_grad = second_pull(hidden_grad)
     middle_grad = cotangent.astype(f32) + middle_part
@@ -991,8 +992,8 @@
     else:
         own_grad = other_grad = exchange_seq(gated_grad, 1, 0)
     ffn_grad = second_sum(ffn_grad)
-    tall_grad = jnp.concatenate(
-        [out_grad.reshape(shards, out_rows, model), down_grad.reshape(shards, units, model)], axis=1
+    tall_grad = lax.dynamic_update_slice(
+        tall_grad, out_grad.reshape(shards, out_rows, model), (0, 0, 0)
     ).reshape(shards * (out_rows + units), model)
     own_grad, other_grad, ffn_grad, tall_grad = lax.optimization_barrier(
         (own_grad, other_grad, ffn_grad, tall_grad)

time: 520 us -> 524 us (level)
  local copies, waits for them, and re-layouts: 52.6 us -> 60.3 us
  other arithmetic: 40.4 us -> 33.9 us
    concatenate x1 -> x0, other arithmetic: 7 us -> none  [on_device(): jnp.concatenate([out_grad.reshape(shards, out_rows, model), down_grad.res...]
    ppermute x12, waiting for transfers between devices: 115 us -> 109 us  [swap_seq(): return lax.ppermute(values, 'seq', [(0, 1), (1, 0)])]
    ppermute x6, waiting for transfers between devices: 23.8 us -> 29.8 us  [flip(): return lax.ppermute(values, 'shard', [(i, i ^ mask) for i in range(size)])]
    pad x0 -> x1, local copies, waits for them, and re-layouts: none -> 5.52 us  [on_device(): jnp.pad(down_grad.reshape(shards, units, model), ((0, 0), (out_rows, 0),...]
where the time goes in v3:
time: 524 us; the launch traced here: 518 us
  waiting for transfers between devices  191 us (36%)
  matrix products  105 us (20%)
  Pallas kernels  88.5 us (17%)
  local copies, waits for them, and re-layouts  60.3 us (12%)
  other arithmetic  33.9 us (6%)
  starting transfers between devices  23.6 us (5%)
  between operations  15 us (3%)
    ppermute x12, waiting for transfers between devices, swap_seq(): return lax.ppermute(values, 'seq', [(0, 1), (1, 0)])  109 us
    dot_general x8, matrix products, dot(): lax.dot_general(a, b, (((ca,), (cb,)), ((), ())), preferred_element_type=...  67.6 us
    pallas_call x1, Pallas kernels, mixer_backward(): pl.pallas_call(functools.partial(backward_kernel, heads), grid=(steps,),...  51.6 us
    dot_general x6, matrix products, forward_dot(): return jnp.dot(left_side, right_side, preferred_element_type=f32)  37.7 us
    pallas_call x1, Pallas kernels, mixer_forward(): pl.pallas_call(functools.partial(forward_kernel, heads), grid=(steps,), i...  35.7 us
    ppermute x6, waiting for transfers between devices, flip(): return lax.ppermute(values, 'shard', [(i, i ^ mask) for i in range(size)])  29.8 us
    reduce_scatter x2, waiting for transfers between devices, scatter_shard(): return lax.psum_scatter(values, 'shard', scatter_dimension=0, tiled=True)  29.8 us
    all_gather x3, waiting for transfers between devices, gather_shard(): return lax.all_gather(values, 'shard', axis=0, tiled=True)  22.6 us
  transfers between devices with their start and end apart: 26, of which 15 were waited for; matrix products, arithmetic and copies ran while one was open for 29% of the time, Pallas kernels for 17%

profile of v3, /device:TPU:0, one launch (start us, length us, event | category | flops | bytes accessed | tf_op | source)
XLA Modules:
  0.0 517.5 jit_solution(5434183708084181698)
XLA Ops:
  13.5 1.8 pad_maximum_fusion.9
  16.9 2.9 collective-permute-start
  23.6 42.2 %collective-permute-done = bf16[1024,1024]{1,0:T(8,128)(2,1)} collective-permute-done((bf16[1024,1024]{1,0:T(8,128)(2,1)}, bf16[1024,1024]{1,0:T(8,128)(2,1)}, u32[]{:S(2)}, u32[]{:S(2)}) %collective-permute-start) | collective-permute-done | bytes 2097184 | tf_op jit(solution)/shard_map/ppermute | solution.py:693
  65.8 2.7 fusion.42
  69.3 10.4 %all-gather.4.cloned.1.call-done = bf16[1024,3200]{1,0:T(8,128)(2,1)} async-done(((bf16[64,3200]{1,0:T(8,128)(2,1)}), bf16[1024,3200]{1,0:T(8,128)(2,1)}) %all-gather.4.cloned.1.call-update) | async-done | bytes 6553616 | tf_op jit(solution)/shard_map/all_gather | solution.py:769
  83.2 6.1 %fusion.17.gate_ref = f32[1024,1024]{1,0:T(8,128)} fusion(bf16[1024,3200]{1,0:T(8,128)(2,1)} %all-gather.4.cloned.1.call-done, f32[1024]{0:T(1024)S(1)} %get-tuple-element.87, f32[1024]{0:T(1024)S(1)} %add_rsqrt_fusion, bf16[512,1024]{1,0:T(8,128)(2,1)S(1)} %bitcast.68, bf16[512,1024]{1,0:T(8,128)(2,1)S(1)} %get-tuple-element.98, pred[]{:T(512)S(6)} %eq.14), kind=kOutput, calls=%fused_computation.43 | convolution fusion | flops 2161115136 | bytes 8396801 | tf_op jit(solution)/shard_map/dot_general | solution.py:673
  89.3 5.7 %fusion.21.value_ref = bf16[1024,1024]{1,0:T(8,128)(2,1)} fusion(bf16[1024,3200]{1,0:T(8,128)(2,1)S(1)} %bitcast.93, f32[1024]{0:T(1024)S(1)} %get-tuple-element.87, f32[1024]{0:T(1024)S(1)} %add_rsqrt_fusion, bf16[512,1024]{1,0:T(8,128)(2,1)S(1)} %bitcast.69, bf16[512,1024]{1,0:T(8,128)(2,1)S(1)} %get-tuple-element.98, pred[]{:T(512)S(6)} %eq.14), kind=kOutput, calls=%fused_computation.57 | convolution fusion | flops 2162163712 | bytes 6299649 | tf_op jit(solution)/shard_map/dot_general | solution.py:673
  95.1 6.0 %convolution_convert_fusion.3.raw_ref = bf16[1024,1152]{1,0:T(8,128)(2,1)} fusion(bf16[1024,3200]{1,0:T(8,128)(2,1)S(1)} %bitcast.93, f32[1024]{0:T(1024)S(1)} %get-tuple-element.87, f32[1024]{0:T(1024)S(1)} %add_rsqrt_fusion, bf16[512,1024]{1,0:T(8,128)(2,1)S(1)} %bitcast.70, bf16[512,1024]{1,0:T(8,128)(2,1)S(1)} %get-tuple-element.98, pred[]{:T(512)S(6)} %eq.14), kind=kOutput, calls=%fused_computation.20 | convolution fusion | flops 2430730240 | bytes 6823937 | tf_op jit(solution)/shard_map/dot_general | solution.py:673
  101.1 35.7 %mixer_forward.1 = (bf16[1024,1024]{1,0:T(8,128)(2,1)}, bf16[1024,1024]{1,0:T(8,128)(2,1)}, bf16[1024,256]{1,0:T(8,128)(2,1)}, f32[4096,256]{1,0:T(8,128)}, bf16...) custom-call(s32[1,4]{1,0:T(1,128)} %starts_ref.3, bf16[1024,1152]{1,0:T(8,128)(2,1)} %convolution_convert_fusion.3.raw_ref, ...), custom_call_target="tpu_custom_call" | custom-call | flops 45056000000 | bytes 16777216 | tf_op jit(solution)/shard_map/mixer_forward/pallas_call | solution.py:582
  140.0 7.7 %all-gather.6.cloned.1.call-done = bf16[3456,1024]{1,0:T(8,128)(2,1)} async-done(((bf16[216,1024]{1,0:T(8,128)(2,1)}), bf16[3456,1024]{1,0:T(8,128)(2,1)}) %all-gather.6.cloned.1.call-update) | async-done | bytes 7077904 | tf_op jit(solution)/shard_map/all_gather | solution.py:769
  147.8 2.6 slice.173
  150.4 5.2 %slice.172 = bf16[16,88,1024]{2,1,0:T(8,128)(2,1)} slice(bf16[16,216,1024]{2,1,0:T(8,128)(2,1)} %bitcast.75), slice={[0:16], [128:216], [0:1024]} | slice | bytes 5767168 | tf_op jit(solution)/shard_map/slice | solution.py:919
  155.6 8.4 %collective-permute-done.1 = bf16[512,1024]{1,0:T(8,128)(2,1)} collective-permute-done((bf16[512,1024]{1,0:T(8,128)(2,1)S(1)}, bf16[512,1024]{1,0:T(8,128)(2,1)}, u32[]{:S(2)}, u32[]{:S(2)}) %collective-permute-start.1) | collective-permute-done | bytes 1048608 | tf_op jit(solution)/shard_map/ppermute | solution.py:693
  164.0 2.4 maximum_select_fusion
  166.4 2.5 multiply_reduce_fusion.2
  170.7 23.1 %collective-permute-done.2 = bf16[512,1024]{1,0:T(8,128)(2,1)} collective-permute-done((bf16[512,1024]{1,0:T(8,128)(2,1)S(1)}, bf16[512,1024]{1,0:T(8,128)(2,1)}, u32[]{:S(2)}, u32[]{:S(2)}) %collective-permute-start.2) | collective-permute-done | bytes 1048608 | tf_op jit(solution)/shard_map/ppermute | solution.py:693
  193.8 2.7 pad_maximum_fusion.6
  196.6 4.0 copy.59
  200.6 3.2 copy.60
  203.7 4.4 all-gather.8.cloned.1.call-done
  208.2 12.0 %fusion.37 = f32[1024,2816]{1,0:T(8,128)} fusion(bf16[1024,2816]{1,0:T(8,128)(2,1)} %all-gather.8.cloned.1.call-done, bf16[512,1024]{1,0:T(8,128)(2,1)} %collective-permute-done.2, bf16[512,1024]{1,0:T(8,128)(2,1)S(1)} %multiply_convert_fusion.2), kind=kOutput, calls=%fused_computation.119 | convolution fusion | flops 5909774336 | bytes 19398656 | tf_op jit(solution)/shard_map/dot_general | solution.py:673
  220.2 11.5 %fusion.2 = (bf16[1024,1408]{1,0:T(8,128)(2,1)}, bf16[1024,1408]{1,0:T(8,128)(2,1)}, bf16[1024,1408]{1,0:T(8,128)(2,1)}) fusion(f32[1024,2816]{1,0:T(8,128)} %fusion.37, bf16[1408,1024]{1,0:T(8,128)(2,1)S(1)} %bitcast.82, bf16[512,1024]{1,0:T(8,128)(2,1)S(1)} %copy-done.22, bf16[512,1024]{1,0:T(8,128)(2,1)S(1)} %bitcast.80), kind=kOutput, calls=%fused_computation.4 | convolution fusion | flops 2980052992 | bytes 25165824 | tf_op jit(solution)/shard_map/dot_general | solution.py:23
  231.7 9.1 %convolution_convert_fusion.1 = bf16[1024,2816]{1,0:T(8,128)(2,1)S(1)} fusion(bf16[1024,1024]{0,1:T(8,128)(2,1)S(1)} %bitcast.85, bf16[1024,1408]{1,0:T(8,128)(2,1)} %get-tuple-element.93, bf16[1024,1408]{1,0:T(8,128)(2,1)} %get-tuple-element.92), kind=kOutput, calls=%fused_computation.11 | convolution fusion | flops 5919997952 | bytes 13631488 | tf_op jit(solution)/shard_map/dot_general | solution.py:23
  240.8 1.8 constant_dynamic-slice_fusion.7
  242.9 9.9 %fusion.9 = f32[1024,1024]{1,0:T(8,128)S(1)} fusion(bf16[1024,2816]{1,0:T(8,128)(2,1)} %all-gather.8.cloned.1.call-done, bf16[1024,1408]{1,0:T(8,128)(2,1)} %get-tuple-element.93, bf16[1024,1408]{1,0:T(8,128)(2,1)} %get-tuple-element.92), kind=kOutput, calls=%fused_computation.22 | convolution fusion | flops 5917114368 | bytes 15728640 | tf_op jit(solution)/shard_map/dot_general | solution.py:23
  254.5 6.6 %convolution_convert_fusion.4 = bf16[1408,1024]{1,0:T(8,128)(2,1)} fusion(bf16[1024,1408]{1,0:T(8,128)(2,1)} %get-tuple-element.94, bf16[512,1024]{1,0:T(8,128)(2,1)S(1)} %copy-done.22, bf16[512,1024]{1,0:T(8,128)(2,1)S(1)} %bitcast.81), kind=kOutput, calls=%fused_computation.21 | convolution fusion | flops 2958426112 | bytes 7864320 | tf_op jit(solution)/shard_map/dot_general | solution.py:23
  261.0 5.5 %pad.9 = bf16[16,216,1024]{2,1,0:T(8,128)(2,1)} pad(bf16[16,88,1024]{2,1,0:T(8,128)(2,1)} %bitcast.84, bf16[]{:T(256)} %constant.94.clone.1), padding=0_0x128_0x0_0 | pad | bytes 9961474 | tf_op jit(solution)/shard_map/jit(_pad)/pad | solution.py:980
  266.6 5.4 %fusion.46 = f32[1024,1024]{1,0:T(8,128)S(1)} fusion(bf16[1024,1408]{1,0:T(8,128)(2,1)} %get-tuple-element.94, bf16[1408,1024]{1,0:T(8,128)(2,1)S(1)} %bitcast.83), kind=kOutput, calls=%fused_computation.124 | convolution fusion | flops 2952790016 | bytes 9961472 | tf_op jit(solution)/shard_map/dot_general | solution.py:673
  273.2 5.1 collective-permute-done.3
  278.7 2.5 add_convert_fusion
  284.8 2.4 convolution_convert_fusion.5
  289.8 2.4 convolution_convert_fusion.2
  292.2 2.4 constant_dynamic-update-slice_fusion.1
  294.7 20.9 %collective-permute-done.6 = bf16[256,2816]{1,0:T(8,128)(2,1)S(1)} collective-permute-done((bf16[256,2816]{1,0:T(8,128)(2,1)S(1)}, bf16[256,2816]{1,0:T(8,128)(2,1)S(1)}, u32[]{:S(2)}, u32[]{:S(2)}) %collective-permute-start.6) | collective-permute-done | bytes 1441824 | tf_op jit(solution)/shard_map/ppermute | solution.py:760
  321.9 2.4 collective-permute-start.7
  325.8 51.6 %mixer_backward.1 = (bf16[1024,3200]{1,0:T(8,128)(2,1)}, f32[32,2048]{1,0:T(8,128)}, f32[2,4]{1,0:T(2,128)}, f32[8,256]{1,0:T(8,128)}) custom-call(s32[1,4]{1,0:T(1,128)} %starts_ref.3, s32[1]{0:T(128)} %bitcast.seq_ref, bf16[1024,1152]{1,0:T(8,128)(2,1)} %convolution_convert_fusion.3.raw_ref, bf16[1024,1024]{1,0:T(8,128)(2,1)} %fusion.21.value_ref, ...), custom_call_target="tpu_custom_call" | custom-call | flops 57344000000 | bytes 16777216 | tf_op jit(solution)/shard_map/mixer_backward/pallas_call | solution.py:628
  378.8 2.9 add_convert_fusion.2
  381.8 12.9 %convolution_convert_fusion = bf16[1024,3200]{1,0:T(8,128)(2,1)} fusion(bf16[1024,3200]{1,0:T(8,128)(2,1)} %get-tuple-element.73, f32[1024]{0:T(1024)S(1)} %copy-done.27, f32[1024]{0:T(1024)S(1)} %copy-done.31, bf16[512,1024]{1,0:T(8,128)(2,1)S(1)} %bitcast.71, bf16[512,1024]{1,0:T(8,128)(2,1)S(1)} %copy-done.10, pred[]{:T(512)S(6)} %eq.14), kind=kOutput, calls=%fused_computation.1 | convolution fusion | flops 6727794688 | bytes 15212545 | tf_op jit(solution)/shard_map/dot_general | solution.py:23
  396.0 12.8 %fusion.7 = (f32[1024]{0:T(1024)S(1)}, f32[1024,1024]{1,0:T(8,128)}) fusion(f32[1024]{0:T(1024)S(1)} %copy-done.31, bf16[512,1024]{1,0:T(8,128)(2,1)S(1)} %bitcast.72, bf16[512,1024]{1,0:T(8,128)(2,1)S(1)} %copy-done.11, pred[]{:T(512)S(6)} %eq.14, bf16[1024,3200]{1,0:T(8,128)(2,1)} %get-tuple-element.73, bf16[1024,3200]{1,0:T(8,128)(2,1)} %all-gather.4.cloned.1.call-done), kind=kOutput, calls=%fused_computation.17 | convolution fusion | flops 6724516864 | bytes 19406848 | tf_op jit(solution)/shard_map/dot_general | solution.py:23
  409.0 2.7 dynamic-slice_convert_fusion
  413.5 3.5 collective-permute-done.13
  417.7 3.4 collective-permute-done.14
  428.1 24.7 %collective-permute-done.16 = f32[2304]{0:T(1024)S(1)} collective-permute-done((f32[2304]{0:T(1024)S(1)}, f32[2304]{0:T(1024)S(1)}, u32[]{:S(2)}, u32[]{:S(2)}) %collective-permute-start.16) | collective-permute-done | bytes 9248 | tf_op jit(solution)/shard_map/ppermute | solution.py:693
  458.0 2.8 reshape.248
  460.8 2.6 fusion.15
  464.0 3.9 fusion.14
  467.9 29.8 %reduce-scatter.3.cloned.1.call-done.own_ref = bf16[64,3200]{1,0:T(8,128)(2,1)} async-done(((bf16[1024,3200]{1,0:T(8,128)(2,1)}), bf16[64,3200]{1,0:T(8,128)(2,1)}) %reduce-scatter.3.cloned.1.call-update) | async-done | bytes 409616 | tf_op jit(solution)/shard_map/reduce_scatter | solution.py:773
  503.4 5.2 %collective-permute-done.17.other_ref = bf16[64,3200]{1,0:T(8,128)(2,1)S(1)} collective-permute-done((bf16[64,3200]{1,0:T(8,128)(2,1)}, bf16[64,3200]{1,0:T(8,128)(2,1)S(1)}, u32[]{:S(2)}, u32[]{:S(2)}) %collective-permute-start.17) | collective-permute-done | bytes 409632 | tf_op jit(solution)/shard_map/ppermute | solution.py:693
  (206 shorter events, 64.0 us)
Async XLA Ops:
  7.2 6.3 %copy-start = (bf16[176,1024]{1,0:T(8,128)(2,1)S(1)}, bf16[176,1024]{1,0:T(8,128)(2,1)}, u32[]{:S(2)}) copy-start(bf16[176,1024]{1,0:T(8,128)(2,1)} %param.32) | copy-start | bytes 1081348
  7.2 8.2 %copy-start.3 = (bf16[1,512,1024]{2,1,0:T(8,128)(2,1)S(1)}, bf16[1,512,1024]{2,1,0:T(8,128)(2,1)}, u32[]{:S(2)}) copy-start(bf16[1,512,1024]{2,1,0:T(8,128)(2,1)} %param.17) | copy-start | bytes 3145732
  7.2 8.2 %copy-start.12 = (bf16[1,512,1024]{2,1,0:T(8,128)(2,1)S(1)}, bf16[1,512,1024]{2,1,0:T(8,128)(2,1)}, u32[]{:S(2)}) copy-start(bf16[1,512,1024]{2,1,0:T(8,128)(2,1)} %param.33) | copy-start | bytes 3145732
  7.2 72.5 %all-gather.4.cloned.1.call-start = ((), (), s32[]{:S(2)}) async-start(), calls=%async_computation.2 | async-start | bytes 6963200 | tf_op jit(solution)/shard_map/all_gather | solution.py:769
  13.4 134.3 %all-gather.6.cloned.1.call-start = ((), (), s32[]{:S(2)}) async-start(), calls=%async_computation.3 | async-start | bytes 7520256 | tf_op jit(solution)/shard_map/all_gather | solution.py:769
  13.5 6.4 %copy-start.23 = (bf16[64,2816]{1,0:T(8,128)(2,1)S(1)}, bf16[64,2816]{1,0:T(8,128)(2,1)}, u32[]{:S(2)}) copy-start(bf16[64,2816]{1,0:T(8,128)(2,1)} %param.31) | copy-start | bytes 1081348
  15.4 192.8 %all-gather.8.cloned.1.call-start = ((), (), s32[]{:S(2)}) async-start(), calls=%async_computation.4 | async-start | bytes 6127616 | tf_op jit(solution)/shard_map/all_gather | solution.py:769
  16.9 6.6 %copy-start.28 = (f32[4,4,512]{2,1,0:T(4,128)S(1)}, f32[4,4,512]{2,1,0:T(4,128)}, u32[]{:S(2)}) copy-start(f32[4,4,512]{2,1,0:T(4,128)} %param.25) | copy-start | bytes 98308
  16.9 48.9 %collective-permute-start = (bf16[1024,1024]{1,0:T(8,128)(2,1)}, bf16[1024,1024]{1,0:T(8,128)(2,1)}, u32[]{:S(2)}, u32[]{:S(2)}) collective-permute-start(bf16[1024,1024]{1,0:T(8,128)(2,1)} %pad_maximum_fusion.3), channel_id=1, source_target_pairs={{0,16},{16,0},{1,17},{17,1},{2,18},{18,2},{3,19},{19,3},{4,20},{20... | collective-permute-start | bytes 6291464 | tf_op jit(solution)/shard_map/ppermute | solution.py:693
  23.4 440.0 %reduce-scatter.5.cloned.1.call-start = ((), (), s32[]{:S(2)}) async-start(), calls=%async_computation.6 | async-start | bytes 7520256 | tf_op jit(solution)/shard_map/reduce_scatter | solution.py:773
  23.6 45.7 %copy-start.32 = (f32[4,2048]{1,0:T(4,128)}, f32[4,2048]{1,0:T(4,128)S(1)}, u32[]{:S(2)}) copy-start(f32[4,2048]{1,0:T(4,128)S(1)} %constant_dynamic-update-slice_fusion.filters_ref) | copy-start | bytes 98308
  68.5 26.5 %copy-start.9 = (bf16[512,1024]{1,0:T(8,128)(2,1)}, bf16[512,1024]{1,0:T(8,128)(2,1)S(1)}, u32[]{:S(2)}) copy-start(bf16[512,1024]{1,0:T(8,128)(2,1)S(1)} %get-tuple-element.98) | copy-start | bytes 3145732
  69.3 25.8 %copy-start.30 = (f32[1024]{0:T(1024)}, f32[1024]{0:T(1024)S(1)}, u32[]{:S(2)}) copy-start(f32[1024]{0:T(1024)S(1)} %add_rsqrt_fusion) | copy-start | bytes 12292
  81.6 7.7 %slice-start = ((s8[6553600]{0:T(1024)(128)(4,1)}), s8[4194304]{0:T(1024)(128)(4,1)S(1)}, s32[]{:S(2)}) async-start(s8[6553600]{0:T(1024)(128)(4,1)} %bitcast.92), calls=%async_computation.7 | async-start | bytes 8388608
  83.2 11.9 %copy-start.26 = (f32[1024]{0:T(1024)}, f32[1024]{0:T(1024)S(1)}, u32[]{:S(2)}) copy-start(f32[1024]{0:T(1024)S(1)} %get-tuple-element.87) | copy-start | bytes 12292
  138.5 25.5 %collective-permute-start.1 = (bf16[512,1024]{1,0:T(8,128)(2,1)S(1)}, bf16[512,1024]{1,0:T(8,128)(2,1)}, u32[]{:S(2)}, u32[]{:S(2)}) collective-permute-start(bf16[512,1024]{1,0:T(8,128)(2,1)S(1)} %get-tuple-element.100), channel_id=1, source_target_pairs={{0,16},{16,0},{1,17},{17,1},{2,18},{18,2},{3,19},{19,3},{4,20},{20... | collective-permute-start | bytes 3145736 | tf_op jit(solution)/shard_map/ppermute | solution.py:693
  150.4 16.0 %copy-start.7 = (bf16[16,128,1024]{2,1,0:T(8,128)(2,1)}, bf16[16,128,1024]{2,1,0:T(8,128)(2,1)S(1)}, u32[]{:S(2)}) copy-start(bf16[16,128,1024]{2,1,0:T(8,128)(2,1)S(1)} %slice.173) | copy-start | bytes 12582916
  169.1 24.7 %collective-permute-start.2 = (bf16[512,1024]{1,0:T(8,128)(2,1)S(1)}, bf16[512,1024]{1,0:T(8,128)(2,1)}, u32[]{:S(2)}, u32[]{:S(2)}) collective-permute-start(bf16[512,1024]{1,0:T(8,128)(2,1)S(1)} %multiply_convert_fusion.2), channel_id=1, source_target_pairs={{0,16},{16,0},{1,17},{17,1},{2,18},{18,2},{3,19},{19,3},{4,20},{20... | collective-permute-start | bytes 3145736 | tf_op jit(solution)/shard_map/ppermute | solution.py:693
  208.2 12.0 %copy-start.13 = (bf16[1,512,1024]{2,1,0:T(8,128)(2,1)S(1)}, bf16[1,512,1024]{2,1,0:T(8,128)(2,1)}, u32[]{:S(2)}) copy-start(bf16[1,512,1024]{2,1,0:T(8,128)(2,1)} %param.33) | copy-start | bytes 3145732
  208.2 12.0 %copy-start.14 = (bf16[16,88,1024]{2,1,0:T(8,128)(2,1)S(1)}, bf16[16,88,1024]{2,1,0:T(8,128)(2,1)}, u32[]{:S(2)}) copy-start(bf16[16,88,1024]{2,1,0:T(8,128)(2,1)} %slice.172) | copy-start | bytes 8650756
  208.2 12.0 %copy-start.22 = (bf16[512,1024]{1,0:T(8,128)(2,1)S(1)}, bf16[512,1024]{1,0:T(8,128)(2,1)}, u32[]{:S(2)}) copy-start(bf16[512,1024]{1,0:T(8,128)(2,1)} %get-tuple-element.97) | copy-start | bytes 3145732
  220.2 11.5 %copy-start.21 = (bf16[1024,2,2,4,64]{0,4,3,2,1:T(8,128)(2,1)S(1)}, bf16[1024,2,2,4,64]{0,4,3,2,1:T(8,128)(2,1)}, u32[]{:S(2)}) copy-start(bf16[1024,2,2,4,64]{0,4,3,2,1:T(8,128)(2,1)} %copy.60) | copy-start | bytes 6291460
  242.6 36.1 %collective-permute-start.4 = (bf16[512,2816]{1,0:T(8,128)(2,1)}, bf16[512,2816]{1,0:T(8,128)(2,1)}, u32[]{:S(2)}, u32[]{:S(2)}) collective-permute-start(bf16[512,2816]{1,0:T(8,128)(2,1)} %constant_dynamic-slice_fusion.7), channel_id=1, source_target_pairs={{0,1},{1,0},{2,3},{3,2},{4,5},{5,4},{6,7},{7,6},{8,9},{9,8},{10,11... | collective-permute-start | bytes 8650760 | tf_op jit(solution)/shard_map/ppermute | solution.py:760
  252.8 8.3 %copy-start.17 = (f32[1024,1024]{1,0:T(8,128)}, f32[1024,1024]{1,0:T(8,128)S(1)}, u32[]{:S(2)}) copy-start(f32[1024,1024]{1,0:T(8,128)S(1)} %fusion.9) | copy-start | bytes 12582916
  252.9 25.4 %collective-permute-start.3 = (bf16[512,1024]{1,0:T(8,128)(2,1)S(1)}, bf16[512,1024]{1,0:T(8,128)(2,1)S(1)}, u32[]{:S(2)}, u32[]{:S(2)}) collective-permute-start(bf16[512,1024]{1,0:T(8,128)(2,1)S(1)} %slice.225), channel_id=1, source_target_pairs={{0,16},{16,0},{1,17},{17,1},{2,18},{18,2},{3,19},{19,3},{4,20},{20... | collective-permute-start | bytes 3145736 | tf_op jit(solution)/shard_map/ppermute | solution.py:693
  266.6 11.7 %copy-start.18 = (f32[1024,1024]{1,0:T(8,128)S(1)}, f32[1024,1024]{1,0:T(8,128)}, u32[]{:S(2)}) copy-start(f32[1024,1024]{1,0:T(8,128)} %copy-done.17) | copy-start | bytes 12582916
  271.9 6.7 %copy-start.15 = (f32[1024,1024]{1,0:T(8,128)}, f32[1024,1024]{1,0:T(8,128)S(1)}, u32[]{:S(2)}) copy-start(f32[1024,1024]{1,0:T(8,128)S(1)} %fusion.46) | copy-start | bytes 12582916
  282.4 7.4 %copy-start.5 = (f32[512,1024]{1,0:T(8,128)}, f32[512,1024]{1,0:T(8,128)S(1)}, u32[]{:S(2)}) copy-start(f32[512,1024]{1,0:T(8,128)S(1)} %fusion.12) | copy-start | bytes 6291460
  282.5 33.0 %collective-permute-start.6 = (bf16[256,2816]{1,0:T(8,128)(2,1)S(1)}, bf16[256,2816]{1,0:T(8,128)(2,1)S(1)}, u32[]{:S(2)}, u32[]{:S(2)}) collective-permute-start(bf16[256,2816]{1,0:T(8,128)(2,1)S(1)} %constant_dynamic-slice_fusion.4), channel_id=1, source_target_pairs={{0,2},{1,3},{2,0},{3,1},{4,6},{5,7},{6,4},{7,5},{8,10},{9,11},{10,... | collective-permute-start | bytes 4325384 | tf_op jit(solution)/shard_map/ppermute | solution.py:760
  288.4 28.6 %collective-permute-start.5 = (bf16[512,1024]{1,0:T(8,128)(2,1)S(1)}, bf16[512,1024]{1,0:T(8,128)(2,1)S(1)}, u32[]{:S(2)}, u32[]{:S(2)}) collective-permute-start(bf16[512,1024]{1,0:T(8,128)(2,1)S(1)} %get-tuple-element.95), channel_id=1, source_target_pairs={{0,16},{16,0},{1,17},{17,1},{2,18},{18,2},{3,19},{19,3},{4,20},{20... | collective-permute-start | bytes 3145736 | tf_op jit(solution)/shard_map/ppermute | solution.py:693
  318.0 179.7 %reduce-scatter.3.cloned.1.call-start = ((), (), s32[]{:S(2)}) async-start(), calls=%async_computation.5 | async-start | bytes 6963200 | tf_op jit(solution)/shard_map/reduce_scatter | solution.py:773
  319.4 58.0 %collective-permute-start.9 = (bf16[64,2816]{1,0:T(8,128)(2,1)S(1)}, bf16[64,2816]{1,0:T(8,128)(2,1)S(1)}, u32[]{:S(2)}, u32[]{:S(2)}) collective-permute-start(bf16[64,2816]{1,0:T(8,128)(2,1)S(1)} %get-tuple-element.102), channel_id=1, source_target_pairs={{0,4},{1,5},{2,6},{3,7},{4,8},{5,9},{6,10},{7,11},{8,12},{9,13},{1... | collective-permute-start | bytes 1081352 | tf_op jit(solution)/shard_map/ppermute | solution.py:765
  321.0 56.5 %collective-permute-start.8 = (bf16[64,2816]{1,0:T(8,128)(2,1)S(1)}, bf16[64,2816]{1,0:T(8,128)(2,1)S(1)}, u32[]{:S(2)}, u32[]{:S(2)}) collective-permute-start(bf16[64,2816]{1,0:T(8,128)(2,1)S(1)} %get-tuple-element.103), channel_id=1, source_target_pairs={{0,8},{1,9},{2,10},{3,11},{4,12},{5,13},{6,14},{7,15},{8,0},{9,1},... | collective-permute-start | bytes 1081352 | tf_op jit(solution)/shard_map/ppermute | solution.py:765
  321.9 55.5 %collective-permute-start.7 = (bf16[64,2816]{1,0:T(8,128)(2,1)S(1)}, bf16[64,2816]{1,0:T(8,128)(2,1)}, u32[]{:S(2)}, u32[]{:S(2)}) collective-permute-start(bf16[64,2816]{1,0:T(8,128)(2,1)S(1)} %get-tuple-element.101), channel_id=1, source_target_pairs={{0,12},{1,13},{2,14},{3,15},{4,0},{5,1},{6,2},{7,3},{8,4},{9,5},{1... | collective-permute-start | bytes 1081352 | tf_op jit(solution)/shard_map/ppermute | solution.py:765
  324.3 54.5 %collective-permute-start.10 = (bf16[512,1024]{1,0:T(8,128)(2,1)}, bf16[512,1024]{1,0:T(8,128)(2,1)}, u32[]{:S(2)}, u32[]{:S(2)}) collective-permute-start(bf16[512,1024]{1,0:T(8,128)(2,1)} %slice.224), channel_id=1, source_target_pairs={{0,16},{16,0},{1,17},{17,1},{2,18},{18,2},{3,19},{19,3},{4,20},{20... | collective-permute-start | bytes 3145736 | tf_op jit(solution)/shard_map/ppermute | solution.py:693
  325.8 53.0 %copy-start.16 = (f32[1024,1024]{1,0:T(8,128)S(1)}, f32[1024,1024]{1,0:T(8,128)}, u32[]{:S(2)}) copy-start(f32[1024,1024]{1,0:T(8,128)} %copy-done.15) | copy-start | bytes 12582916
  411.7 1.2 collective-permute-start.12
  412.9 4.1 collective-permute-start.13
  417.0 4.1 collective-permute-start.14
  417.1 43.7 %collective-permute-start.11 = (bf16[512,1024]{1,0:T(8,128)(2,1)}, bf16[512,1024]{1,0:T(8,128)(2,1)}, u32[]{:S(2)}, u32[]{:S(2)}) collective-permute-start(bf16[512,1024]{1,0:T(8,128)(2,1)} %dynamic-slice_convert_fusion), channel_id=1, source_target_pairs={{0,16},{16,0},{1,17},{17,1},{2,18},{18,2},{3,19},{19,3},{4,20},{20... | collective-permute-start | bytes 3145736 | tf_op jit(solution)/shard_map/ppermute | solution.py:693
  421.1 5.0 collective-permute-start.15
  422.7 32.0 %collective-permute-start.19 = (bf16[64,16,88]{2,1,0:T(8,128)(2,1)S(1)}, bf16[64,16,88]{2,1,0:T(8,128)(2,1)S(1)}, u32[]{:S(2)}, u32[]{:S(2)}) collective-permute-start(bf16[64,16,88]{2,1,0:T(8,128)(2,1)S(1)} %reshape.239), channel_id=1, source_target_pairs={{0,16},{16,0},{1,17},{17,1},{2,18},{18,2},{3,19},{19,3},{4,20},{20... | collective-permute-start | bytes 540680 | tf_op jit(solution)/shard_map/ppermute | solution.py:693
  423.9 32.7 %collective-permute-start.20 = (bf16[64,16,88]{2,1,0:T(8,128)(2,1)S(1)}, bf16[64,16,88]{2,1,0:T(8,128)(2,1)S(1)}, u32[]{:S(2)}, u32[]{:S(2)}) collective-permute-start(bf16[64,16,88]{2,1,0:T(8,128)(2,1)S(1)} %reshape.240), channel_id=1, source_target_pairs={{0,16},{16,0},{1,17},{17,1},{2,18},{18,2},{3,19},{19,3},{4,20},{20... | collective-permute-start | bytes 540680 | tf_op jit(solution)/shard_map/ppermute | solution.py:693
  426.2 26.7 %collective-permute-start.16 = (f32[2304]{0:T(1024)S(1)}, f32[2304]{0:T(1024)S(1)}, u32[]{:S(2)}, u32[]{:S(2)}) collective-permute-start(f32[2304]{0:T(1024)S(1)} %slice.180), channel_id=1, source_target_pairs={{0,16},{16,0},{1,17},{17,1},{2,18},{18,2},{3,19},{19,3},{4,20},{20... | collective-permute-start | bytes 27656 | tf_op jit(solution)/shard_map/ppermute | solution.py:693
  463.4 36.5 %collective-permute-start.18 = (bf16[1,216,1024]{2,1,0:T(8,128)(2,1)}, bf16[1,216,1024]{2,1,0:T(8,128)(2,1)}, u32[]{:S(2)}, u32[]{:S(2)}) collective-permute-start(bf16[1,216,1024]{2,1,0:T(8,128)(2,1)} %bitcast.88), channel_id=1, source_target_pairs={{0,16},{16,0},{1,17},{17,1},{2,18},{18,2},{3,19},{19,3},{4,20},{20... | collective-permute-start | bytes 1327112 | tf_op jit(solution)/shard_map/ppermute | solution.py:693
  497.7 11.0 %collective-permute-start.17 = (bf16[64,3200]{1,0:T(8,128)(2,1)}, bf16[64,3200]{1,0:T(8,128)(2,1)S(1)}, u32[]{:S(2)}, u32[]{:S(2)}) collective-permute-start(bf16[64,3200]{1,0:T(8,128)(2,1)} %reduce-scatter.3.cloned.1.call-done.own_ref), channel_id=1, source_target_pairs={{0,16},{16,0},{1,17},{17,1},{2,18},{18,2},{3,19},{19,3},{4,20},{20... | collective-permute-start | bytes 1228808 | tf_op jit(solution)/shard_map/ppermute | solution.py:693
  499.9 10.7 %copy-start.1 = (bf16[176,1024]{1,0:T(8,128)(2,1)S(1)}, bf16[176,1024]{1,0:T(8,128)(2,1)}, u32[]{:S(2)}) copy-start(bf16[176,1024]{1,0:T(8,128)(2,1)} %param.32) | copy-start | bytes 1081348
  499.9 9.4 %copy-start.2 = (bf16[64,3200]{1,0:T(8,128)(2,1)S(1)}, bf16[64,3200]{1,0:T(8,128)(2,1)}, u32[]{:S(2)}) copy-start(bf16[64,3200]{1,0:T(8,128)(2,1)} %reduce-scatter.3.cloned.1.call-done.own_ref) | copy-start | bytes 1228804
  (15 other events, 43.2 us)
Sparse Core Ops, SparseCore 0:
  13.6 66.0 all-gather.3
  82.5 65.1 all-gather.5
  150.6 57.4 all-gather.7
  318.1 88.6 reduce-scatter.4
  411.1 86.4 reduce-scatter.2
